TPU v7x, 128 devices: a whole 4x4x4 slice. The times are simulated.
128 devices in a mesh: member: 4 (over y_hi, core), band: 32 (over y_lo, x, z).
Axes of the slice: x: 4, y: 4 (y_hi: 2, y_lo: 2; y = y_hi * 2 + y_lo), z: 4, core: 2. Of those that a mesh axis runs over, the one named last changes fastest.
Arguments:
- fields: float32 [32, 2, 2048, 2048], P('member', None, 'band'), may hold values from -48 to 48
- observed: float32 [2, 512, 512], P(None, 'band'), may hold values from -2.4 to 2.4
Outputs:
- field_gradient: float32 [32, 2, 2048, 2048], P('member', None, 'band')
All inputs are finite; a program needn't handle non-finite values.
Results may differ from a plain program's by a relative error of at most 0.00013.
Values sent between devices are 32-bit elements; how exact they have to be, the bound alone decides.
No kernel may reach another device: no remote copies, remote signals or barrier semaphores. Data moves between devices by JAX's collectives and lax.ppermute only.
A program may use at most 64 MiB of HBM per device.

v0:
```python
import jax
import jax.numpy as jnp
from jax import lax
from jax.sharding import PartitionSpec as P

RADIUS = 16


smooth_sigma = 6.0
huber_width = 0.05


def padded_2(value, sides, width):
    for axis, dim in sides:
        devices, length = (lax.axis_size(axis), value.shape[dim])
        up = [(i, (i + 1) % devices) for i in range(devices - 1)]
        down = [(j, i) for i, j in up]
        last = lax.slice_in_dim(value, length - width, length, axis=dim)
        leading = lax.slice_in_dim(value, 0, width, axis=dim)
        before = lax.ppermute(last, axis, up)
        after = lax.ppermute(leading, axis, down)
        value = jnp.concatenate([before, value, after], axis=dim)
    return value


def kernel(offset):
    spot = offset.astype(jnp.float32)
    tap_ids = jnp.arange(-RADIUS, RADIUS + 1).astype(jnp.float32)
    normaliser = jnp.sum(jnp.exp(-tap_ids * tap_ids / (2.0 * smooth_sigma * smooth_sigma)))
    inside = jnp.abs(spot) <= RADIUS
    return (
        jnp.where(inside, jnp.exp(-spot * spot / (2.0 * smooth_sigma * smooth_sigma)), 0.0)
        / normaliser
    )


def thin_last(values):
    length = values.shape[-1]
    block_width = min(512, length)
    padded = jnp.pad(values, [(0, 0)] * (values.ndim - 1) + [(RADIUS, RADIUS)])
    row_ids = jnp.arange(block_width + 2 * RADIUS)[:, None]
    col_ids = jnp.arange(block_width // 4)[None, :]
    table = kernel(row_ids - RADIUS - 4 * col_ids)
    pieces = []
    for piece_num in range(length // block_width):
        window = padded[
            ..., piece_num * block_width : piece_num * block_width + block_width + 2 * RADIUS
        ]
        pieces.append(jnp.einsum("...p,pq->...q", window, table, precision=lax.Precision.HIGHEST))
    return jnp.concatenate(pieces, axis=-1)


def spread_last(values):
    coarse_len = values.shape[-1]
    block_width = min(512, 4 * coarse_len)
    margin = RADIUS // 4
    padded = jnp.pad(values, [(0, 0)] * (values.ndim - 1) + [(margin, margin)])
    row_ids = jnp.arange(block_width // 4 + 2 * margin)[:, None]
    col_ids = jnp.arange(block_width)[None, :]
    table = kernel(col_ids - 4 * (row_ids - margin))
    pieces = []
    for piece_num in range(4 * coarse_len // block_width):
        start = piece_num * block_width // 4
        window = padded[..., start : start + block_width // 4 + 2 * margin]
        pieces.append(jnp.einsum("...q,qp->...p", window, table, precision=lax.Precision.HIGHEST))
    return jnp.concatenate(pieces, axis=-1)


def soft_sign(diff):
    return diff * lax.rsqrt(diff * diff + huber_width * huber_width)


def member_grad(member_rows, everyone, observed, ensemble):
    own_term = soft_sign(member_rows - observed[None]) / ensemble
    pair_term = jnp.sum(soft_sign(member_rows[:, None] - everyone[None]), axis=1)
    return own_term - pair_term / (ensemble * (ensemble - 1))


def shards(fields, observed):
    band_rows = fields.shape[2]
    coarse_rows = band_rows // 4
    margin = RADIUS // 4
    ensemble = fields.shape[0] * lax.axis_size("member")
    lat_ids = jnp.arange(coarse_rows)[:, None]
    extended = padded_2(fields, (("band", 2),), RADIUS)
    lon_pass = thin_last(extended)
    ext_ids = jnp.arange(band_rows + 2 * RADIUS)[None, :]
    lat_table = kernel(ext_ids - RADIUS - 4 * lat_ids)
    coarse = jnp.einsum("ce,mvej->mvcj", lat_table, lon_pass, precision=lax.Precision.HIGHEST)
    everyone = lax.all_gather(coarse, "member", axis=0, tiled=True)
    cell_grad = member_grad(coarse, everyone, observed, ensemble)
    grad_ext = padded_2(cell_grad, (("band", 2),), margin)
    fine_ids = jnp.arange(band_rows)[:, None]
    near_ids = jnp.arange(coarse_rows + 2 * margin)[None, :]
    back_table = kernel(fine_ids - 4 * (near_ids - margin))
    lat_back = jnp.einsum("rc,mvcj->mvrj", back_table, grad_ext, precision=lax.Precision.HIGHEST)
    return 64.0 * ensemble * spread_last(lat_back)


def solution(mesh):
    return jax.shard_map(
        shards,
        mesh=mesh,
        in_specs=(P("member", None, "band", None), P(None, "band", None)),
        out_specs=P("member", None, "band", None),
        check_vma=False,
    )
```

profile of v0, /device:TPU:8, one launch (start us, length us, event | category | flops | bytes accessed | tf_op | source)
XLA Modules:
  0.0 166.3 jit_solution(8670881723411689468)
XLA Ops:
  6.5 0.0 all-gather.2.cloned.1.call-start
  6.5 4.1 %fusion.156 = (f32[8,2,16,2048]{3,2,1,0:T(8,128)}, f32[8,2,16,2048]{3,2,1,0:T(8,128)S(1)}) fusion(f32[8,2,64,2048]{3,2,1,0:T(8,128)} %param.2), kind=kLoop, calls=%fused_computation.171 | loop fusion | bytes 8388608 | tf_op jit(solution)/shard_map/slice | solution.py:19
  10.6 3.9 %collective-permute-start = (f32[8,2,16,2048]{3,2,1,0:T(8,128)S(1)}, f32[8,2,16,2048]{3,2,1,0:T(8,128)S(1)}, u32[]{:S(2)}, u32[]{:S(2)}) collective-permute-start(f32[8,2,16,2048]{3,2,1,0:T(8,128)S(1)} %get-tuple-element.6), channel_id=1, source_target_pairs={{0,1},{1,2},{2,3},{3,4},{4,5},{5,6},{6,7},{7,8},{8,9},{9,10},{10,1... | collective-permute-start | bytes 6291464 | tf_op jit(solution)/shard_map/ppermute | solution.py:20
  14.6 6.2 %collective-permute-start.1 = (f32[8,2,16,2048]{3,2,1,0:T(8,128)}, f32[8,2,16,2048]{3,2,1,0:T(8,128)}, u32[]{:S(2)}, u32[]{:S(2)}) collective-permute-start(f32[8,2,16,2048]{3,2,1,0:T(8,128)} %get-tuple-element.5), channel_id=1, source_target_pairs={{1,0},{2,1},{3,2},{4,3},{5,4},{6,5},{7,6},{8,7},{9,8},{10,9},{11,1... | collective-permute-start | bytes 6291464 | tf_op jit(solution)/shard_map/ppermute | solution.py:21
  20.8 0.7 fusion.123
  21.5 42.9 %collective-permute-done = f32[8,2,16,2048]{3,2,1,0:T(8,128)S(1)} collective-permute-done((f32[8,2,16,2048]{3,2,1,0:T(8,128)S(1)}, f32[8,2,16,2048]{3,2,1,0:T(8,128)S(1)}, u32[]{:S(2)}, u32[]{:S(2)}) %collective-permute-start) | collective-permute-done | bytes 2097184 | tf_op jit(solution)/shard_map/ppermute | solution.py:20
  64.4 0.1 constant_dynamic-update-slice_fusion.2
  64.5 0.6 constant_dynamic-update-slice_fusion.1
  65.1 0.7 collective-permute-done.1
  65.9 1.7 %constant_dynamic-update-slice_fusion = f32[8,2,96,2048]{3,2,1,0:T(8,128)S(1)} fusion(f32[8,2,96,2048]{3,2,1,0:T(8,128)S(1)} %constant_dynamic-update-slice_fusion.1, f32[8,2,16,2048]{3,2,1,0:T(8,128)} %collective-permute-done.1), kind=kLoop, calls=%fused_computation.112 | loop fusion | bytes 4194304 | tf_op jit(solution)/shard_map/concatenate | solution.py:22
  67.6 4.5 %fusion.4 = f32[8,2,96,128]{3,2,1,0:T(8,128)S(1)} fusion(f32[8,2,96,2048]{3,2,1,0:T(8,128)S(1)} %constant_dynamic-update-slice_fusion, f32[]{:T(128)} %fusion.123, s32[128]{0:T(128)S(1)} %iota_multiply_fusion.1, s32[544]{0:T(1024)S(1)} %iota_add_fusion), kind=kOutput, calls=%fused_computation.9 | convolution fusion | flops 1284083712 | bytes 13372036 | tf_op jit(solution)/shard_map/...p,pq->...q/dot_general | solution.py:49
  72.1 4.5 %fusion.5 = f32[8,2,96,128]{3,2,1,0:T(8,128)S(1)} fusion(f32[8,2,96,2048]{3,2,1,0:T(8,128)S(1)} %constant_dynamic-update-slice_fusion, f32[]{:T(128)} %fusion.123, s32[128]{0:T(128)S(1)} %iota_multiply_fusion.1, s32[544]{0:T(1024)S(1)} %iota_add_fusion), kind=kOutput, calls=%fused_computation.10 | convolution fusion | flops 1284083712 | bytes 4723204 | tf_op jit(solution)/shard_map/...p,pq->...q/dot_general | solution.py:49
  76.7 4.7 %fusion.7 = f32[8,2,96,128]{3,2,1,0:T(8,128)S(1)} fusion(f32[8,2,96,2048]{3,2,1,0:T(8,128)S(1)} %constant_dynamic-update-slice_fusion, f32[]{:T(128)} %fusion.123, s32[128]{0:T(128)S(1)} %iota_multiply_fusion.1, s32[544]{0:T(1024)S(1)} %iota_add_fusion), kind=kOutput, calls=%fused_computation.12 | convolution fusion | flops 1284083712 | bytes 4723204 | tf_op jit(solution)/shard_map/...p,pq->...q/dot_general | solution.py:49
  81.4 4.5 %fusion.3 = f32[8,2,96,128]{3,2,1,0:T(8,128)S(1)} fusion(f32[8,2,96,2048]{3,2,1,0:T(8,128)S(1)} %constant_dynamic-update-slice_fusion, f32[]{:T(128)} %fusion.123, s32[128]{0:T(128)S(1)} %iota_multiply_fusion.1, s32[544]{0:T(1024)S(1)} %iota_add_fusion), kind=kOutput, calls=%fused_computation.8 | convolution fusion | flops 1284083712 | bytes 13372036 | tf_op jit(solution)/shard_map/...p,pq->...q/dot_general | solution.py:49
  85.9 3.2 %fusion.17 = f32[8,2,16,512]{3,2,1,0:T(8,128)} fusion(f32[8,2,96,128]{3,2,1,0:T(8,128)S(1)} %fusion.4, f32[8,2,96,128]{3,2,1,0:T(8,128)S(1)} %fusion.5, f32[8,2,96,128]{3,2,1,0:T(8,128)S(1)} %fusion.7, f32[8,2,96,128]{3,2,1,0:T(8,128)S(1)} %fusion.3, f32[]{:T(128)} %fusion.123, s32[16]{0:T(128)S(1)} %iota_multiply_fusion, s32[96]{0:T(128)S(1)} %iota_add_fusion.1), kind=kOutput, calls=%fused_computation.25 | convolution fusion | flops 153368064 | bytes 3670468 | tf_op jit(solution)/shard_map/ce,mvej->mvcj/dot_general | solution.py:89
  89.1 0.0 all-gather.2.cloned.1.call-update
  89.1 0.0 copy-start.1
  89.1 0.0 copy-start.2
  89.2 28.5 %all-gather.2.cloned.1.call-done = f32[32,2,16,512]{3,2,1,0:T(8,128)} async-done(((f32[8,2,16,512]{3,2,1,0:T(8,128)}), f32[32,2,16,512]{3,2,1,0:T(8,128)}) %all-gather.2.cloned.1.call-update) | async-done | bytes 2097168 | tf_op jit(solution)/shard_map/all_gather | solution.py:90
  117.6 5.0 %fusion.2 = f32[8,2,16,512]{3,2,1,0:T(8,128)S(1)} fusion(f32[32,2,16,512]{3,2,1,0:T(8,128)} %all-gather.2.cloned.1.call-done, f32[8,2,16,512]{3,2,1,0:T(8,128)} %fusion.17), kind=kLoop, calls=%fused_computation.4 | loop fusion | flops 20840448 | bytes 3145728 | tf_op jit(solution)/shard_map/reduce_sum | solution.py:75
  122.6 0.2 multiply_subtract_fusion
  122.8 0.1 fusion.157
  122.9 7.9 %collective-permute-start.3 = (f32[8,2,4,512]{3,2,1,0:T(4,128)S(1)}, f32[8,2,4,512]{3,2,1,0:T(4,128)S(1)}, u32[]{:S(2)}, u32[]{:S(2)}) collective-permute-start(f32[8,2,4,512]{3,2,1,0:T(4,128)S(1)} %get-tuple-element.8), channel_id=1, source_target_pairs={{1,0},{2,1},{3,2},{4,3},{5,4},{6,5},{7,6},{8,7},{9,8},{10,9},{11,1... | collective-permute-start | bytes 393224 | tf_op jit(solution)/shard_map/ppermute | solution.py:21
  130.7 2.1 %collective-permute-start.2 = (f32[8,2,4,512]{3,2,1,0:T(4,128)S(1)}, f32[8,2,4,512]{3,2,1,0:T(4,128)S(1)}, u32[]{:S(2)}, u32[]{:S(2)}) collective-permute-start(f32[8,2,4,512]{3,2,1,0:T(4,128)S(1)} %get-tuple-element.7), channel_id=1, source_target_pairs={{0,1},{1,2},{2,3},{3,4},{4,5},{5,6},{6,7},{7,8},{8,9},{9,10},{10,1... | collective-permute-start | bytes 393224 | tf_op jit(solution)/shard_map/ppermute | solution.py:20
  132.9 1.0 collective-permute-done.3
  133.9 8.3 %collective-permute-done.2 = f32[8,2,4,512]{3,2,1,0:T(4,128)S(1)} collective-permute-done((f32[8,2,4,512]{3,2,1,0:T(4,128)S(1)}, f32[8,2,4,512]{3,2,1,0:T(4,128)S(1)}, u32[]{:S(2)}, u32[]{:S(2)}) %collective-permute-start.2) | collective-permute-done | bytes 131104 | tf_op jit(solution)/shard_map/ppermute | solution.py:20
  142.2 2.7 %convolution_bitcast_fusion = f32[8,2,64,512]{3,2,1,0:T(8,128)S(1)} fusion(f32[8,2,4,512]{3,2,1,0:T(4,128)S(1)} %collective-permute-done.3, f32[8,2,16,512]{3,2,1,0:T(8,128)S(1)} %multiply_subtract_fusion, f32[8,2,4,512]{3,2,1,0:T(4,128)S(1)} %collective-permute-done.2, f32[]{:T(128)} %fusion.123, s32[24]{0:T(128)S(1)} %add_multiply_fusion.1), kind=kOutput, calls=%fused_computation.24 | convolution fusion | flops 151401984 | bytes 2883684 | tf_op jit(solution)/shard_map/rc,mvcj->mvrj/dot_general | solution.py:96
  144.9 2.6 %fusion.21 = f32[8,2,64,512]{3,2,1,0:T(8,128)S(1)} fusion(f32[8,2,64,512]{3,2,1,0:T(8,128)S(1)} %convolution_bitcast_fusion, f32[]{:T(128)} %fusion.123, s32[136]{0:T(256)S(1)} %add_multiply_fusion), kind=kOutput, calls=%fused_computation.27 | convolution fusion | flops 856264704 | bytes 4194852 | tf_op jit(solution)/shard_map/...q,qp->...p/dot_general | solution.py:65
  147.6 2.6 %fusion.22 = f32[8,2,64,512]{3,2,1,0:T(8,128)S(1)} fusion(f32[8,2,64,512]{3,2,1,0:T(8,128)S(1)} %convolution_bitcast_fusion, f32[]{:T(128)} %fusion.123, s32[136]{0:T(256)S(1)} %add_multiply_fusion), kind=kOutput, calls=%fused_computation.28 | convolution fusion | flops 856264704 | bytes 3146756 | tf_op jit(solution)/shard_map/...q,qp->...p/dot_general | solution.py:65
  150.2 2.6 %fusion.24 = f32[8,2,64,512]{3,2,1,0:T(8,128)S(1)} fusion(f32[8,2,64,512]{3,2,1,0:T(8,128)S(1)} %convolution_bitcast_fusion, f32[]{:T(128)} %fusion.123, s32[136]{0:T(256)S(1)} %add_multiply_fusion), kind=kOutput, calls=%fused_computation.30 | convolution fusion | flops 856264704 | bytes 3146756 | tf_op jit(solution)/shard_map/...q,qp->...p/dot_general | solution.py:65
  152.9 2.6 %fusion.20 = f32[8,2,64,512]{3,2,1,0:T(8,128)S(1)} fusion(f32[8,2,64,512]{3,2,1,0:T(8,128)S(1)} %convolution_bitcast_fusion, f32[]{:T(128)} %fusion.123, s32[136]{0:T(256)S(1)} %add_multiply_fusion), kind=kOutput, calls=%fused_computation.26 | convolution fusion | flops 856264704 | bytes 4194852 | tf_op jit(solution)/shard_map/...q,qp->...p/dot_general | solution.py:65
  155.5 3.9 %maximum_multiply_fusion = f32[8,2,64,2048]{3,2,1,0:T(8,128)} fusion(f32[8,2,64,512]{3,2,1,0:T(8,128)S(1)} %fusion.21, f32[8,2,64,512]{3,2,1,0:T(8,128)S(1)} %fusion.22, f32[8,2,64,512]{3,2,1,0:T(8,128)S(1)} %fusion.24, f32[8,2,64,512]{3,2,1,0:T(8,128)S(1)} %fusion.20), kind=kLoop, calls=%fused_computation.7 | loop fusion | flops 8388608 | bytes 16777216 | tf_op jit(solution)/shard_map/mul | solution.py:97
  (10 shorter events, 0.0 us)
Async XLA Ops:
  6.5 111.1 %all-gather.2.cloned.1.call-start = ((), (), s32[]{:S(2)}) async-start(), calls=%async_computation | async-start | bytes 2621440 | tf_op jit(solution)/shard_map/all_gather | solution.py:90
  6.5 58.0 %copy-start = (f32[8,2,64,2048]{3,2,1,0:T(8,128)S(1)}, f32[8,2,64,2048]{3,2,1,0:T(8,128)}, u32[]{:S(2)}) copy-start(f32[8,2,64,2048]{3,2,1,0:T(8,128)} %param.2) | copy-start | bytes 25165828
  10.6 53.8 %collective-permute-start = (f32[8,2,16,2048]{3,2,1,0:T(8,128)S(1)}, f32[8,2,16,2048]{3,2,1,0:T(8,128)S(1)}, u32[]{:S(2)}, u32[]{:S(2)}) collective-permute-start(f32[8,2,16,2048]{3,2,1,0:T(8,128)S(1)} %get-tuple-element.6), channel_id=1, source_target_pairs={{0,1},{1,2},{2,3},{3,4},{4,5},{5,6},{6,7},{7,8},{8,9},{9,10},{10,1... | collective-permute-start | bytes 6291464 | tf_op jit(solution)/shard_map/ppermute | solution.py:20
  14.6 51.3 %collective-permute-start.1 = (f32[8,2,16,2048]{3,2,1,0:T(8,128)}, f32[8,2,16,2048]{3,2,1,0:T(8,128)}, u32[]{:S(2)}, u32[]{:S(2)}) collective-permute-start(f32[8,2,16,2048]{3,2,1,0:T(8,128)} %get-tuple-element.5), channel_id=1, source_target_pairs={{1,0},{2,1},{3,2},{4,3},{5,4},{6,5},{7,6},{8,7},{9,8},{10,9},{11,1... | collective-permute-start | bytes 6291464 | tf_op jit(solution)/shard_map/ppermute | solution.py:21
  89.1 33.5 %copy-start.1 = (f32[8,2,16,512]{3,2,1,0:T(8,128)S(1)}, f32[8,2,16,512]{3,2,1,0:T(8,128)}, u32[]{:S(2)}) copy-start(f32[8,2,16,512]{3,2,1,0:T(8,128)} %fusion.17) | copy-start | bytes 1572868
  89.1 33.5 %copy-start.2 = (f32[2,16,512]{2,1,0:T(8,128)S(1)}, f32[2,16,512]{2,1,0:T(8,128)}, u32[]{:S(2)}) copy-start(f32[2,16,512]{2,1,0:T(8,128)} %param.3) | copy-start | bytes 196612
  122.9 11.0 %collective-permute-start.3 = (f32[8,2,4,512]{3,2,1,0:T(4,128)S(1)}, f32[8,2,4,512]{3,2,1,0:T(4,128)S(1)}, u32[]{:S(2)}, u32[]{:S(2)}) collective-permute-start(f32[8,2,4,512]{3,2,1,0:T(4,128)S(1)} %get-tuple-element.8), channel_id=1, source_target_pairs={{1,0},{2,1},{3,2},{4,3},{5,4},{6,5},{7,6},{8,7},{9,8},{10,9},{11,1... | collective-permute-start | bytes 393224 | tf_op jit(solution)/shard_map/ppermute | solution.py:21
  130.7 11.5 %collective-permute-start.2 = (f32[8,2,4,512]{3,2,1,0:T(4,128)S(1)}, f32[8,2,4,512]{3,2,1,0:T(4,128)S(1)}, u32[]{:S(2)}, u32[]{:S(2)}) collective-permute-start(f32[8,2,4,512]{3,2,1,0:T(4,128)S(1)} %get-tuple-element.7), channel_id=1, source_target_pairs={{0,1},{1,2},{2,3},{3,4},{4,5},{5,6},{6,7},{7,8},{8,9},{9,10},{10,1... | collective-permute-start | bytes 393224 | tf_op jit(solution)/shard_map/ppermute | solution.py:20
Sparse Core Ops, SparseCore 0:
  89.3 28.3 all-gather.1
where the time goes:
time: 167 us; the launch traced here: 166 us
  waiting for transfers between devices  81.4 us (49%)
  matrix products  34.8 us (21%)
  starting transfers between devices  20.2 us (12%)
  between operations  13.6 us (8%)
  other arithmetic  9.72 us (6%)
  local copies, waits for them, and re-layouts  6.6 us (4%)
    ppermute x2, waiting for transfers between devices, padded_2(): before = lax.ppermute(last, axis, up)  51.2 us
    all_gather x1, waiting for transfers between devices, shards(): everyone = lax.all_gather(coarse, 'member', axis=0, tiled=True)  28.5 us
    dot_general x4, matrix products, thin_last(): jnp.einsum('...p,pq->...q', window, table, precision=lax.Precision.HIGHEST)  18.3 us
    ppermute x2, starting transfers between devices, padded_2(): after = lax.ppermute(leading, axis, down)  14.1 us
    dot_general x4, matrix products, spread_last(): jnp.einsum('...q,qp->...p', window, table, precision=lax.Precision.HIGHEST)  10.6 us
    ppermute x2, starting transfers between devices, padded_2(): before = lax.ppermute(last, axis, up)  6.09 us
    reduce_sum x1, other arithmetic, member_grad(): jnp.sum(soft_sign(member_rows[:, None] - everyone[None]), axis=1)  4.98 us
    slice x1, local copies, waits for them, and re-layouts, padded_2(): leading = lax.slice_in_dim(value, 0, width, axis=dim)  4.08 us
  transfers between devices with their start and end apart: 5, of which 5 were waited for; matrix products, arithmetic and copies ran while one was open for 1% of the time, Pallas kernels for 0%

commit v1 on v0

v1 whole, which is shorter than its diff:
```python
import functools

import jax
import jax.numpy as jnp
import ml_dtypes
import numpy as np
from jax import lax
from jax.experimental import pallas as pl
from jax.experimental.pallas import tpu as pltpu
from jax.sharding import PartitionSpec as P

RADIUS = 16
SIGMA = 6.0
HUBER = 0.05
STRIDE = 4
MARGIN = RADIUS // STRIDE
LANES = 128
BLOCK = 256
VMEM = 48 * 1024 * 1024


def kern(offset):
    taps = np.arange(-RADIUS, RADIUS + 1).astype(np.float64)
    norm = np.sum(np.exp(-taps * taps / (2.0 * SIGMA * SIGMA)))
    spot = np.asarray(offset).astype(np.float64)
    inside = np.abs(spot) <= RADIUS
    return np.where(inside, np.exp(-spot * spot / (2.0 * SIGMA * SIGMA)), 0.0) / norm


def parts(table):
    high = table.astype(np.float32).astype(ml_dtypes.bfloat16)
    low = (table - high.astype(np.float64)).astype(ml_dtypes.bfloat16)
    return high, low


def lon_offsets():
    lane = np.arange(LANES)
    even = np.where(lane < LANES - MARGIN, lane, lane - LANES)
    odd = np.where(lane < MARGIN, lane + LANES, lane) - LANES // 2
    fine = np.arange(BLOCK)
    return [fine[:, None] - STRIDE * place[None, :] for place in (even, odd)]


def thin_lon_table():
    pairs = [parts(kern(offset)) for offset in lon_offsets()]
    return np.stack([np.concatenate(pair, axis=1) for pair in pairs])


def spread_lon_table():
    pairs = [parts(kern(offset).T) for offset in lon_offsets()]
    return np.stack([np.concatenate([part, part], axis=0) for pair in pairs for part in pair])


def lat_offsets(rows):
    near = np.arange(rows // STRIDE + 2 * MARGIN) - MARGIN
    return np.arange(rows)[:, None] - STRIDE * near[None, :]


def thin_lat_table(rows):
    high, low = parts(kern(lat_offsets(rows)).T)
    return np.concatenate(
        [np.concatenate([high, high], axis=1), np.concatenate([low, low], axis=1)], axis=0
    )


def spread_lat_table(rows, scale):
    high, low = parts(scale * kern(lat_offsets(rows)))
    return np.concatenate([high, high, low], axis=1)


def dot(a, b):
    return jnp.dot(a, b, preferred_element_type=jnp.float32)


def split(value):
    high = value.astype(jnp.bfloat16)
    low = (value - high.astype(jnp.float32)).astype(jnp.bfloat16)
    return high, low


def thin_kernel(bands, where_ref, x_ref, lon_ref, lat_ref, top_ref, mid_ref, low_ref):
    variables, rows, length = x_ref.shape[1:]
    value = x_ref[0].reshape(variables * rows, length)
    sums = []
    for k in range(length // BLOCK):
        high, low = split(value[:, k * BLOCK : (k + 1) * BLOCK])
        table = lon_ref[k % 2]
        both = dot(high, table) + dot(low, table)
        sums.append(both[:, :LANES] + both[:, LANES:])
    lane = lax.broadcasted_iota(jnp.int32, sums[0].shape, 1)
    zero = jnp.zeros_like(sums[0])
    columns = []
    for j in range(len(sums) // 2):
        after = sums[2 * j + 2] if 2 * j + 2 < len(sums) else zero
        before = sums[2 * j - 1] if j > 0 else zero
        columns.append(
            jnp.where(lane >= LANES - MARGIN, after, sums[2 * j])
            + jnp.where(lane < MARGIN, before, sums[2 * j + 1])
        )
    thin = jnp.concatenate(columns, axis=1)
    band = where_ref[0]
    for v in range(variables):
        high, low = split(thin[v * rows : (v + 1) * rows])
        both = dot(lat_ref[...], jnp.concatenate([high, low], axis=0))
        half = both.shape[0] // 2
        coarse = both[:half] + both[half:]
        row = lax.broadcasted_iota(jnp.int32, (8, coarse.shape[1]), 0)
        top_ref[0, v] = jnp.where((row < MARGIN) & (band == 0), 0.0, coarse[:8])
        mid_ref[0, v] = coarse[8:16]
        low_ref[0, v] = jnp.where((row >= MARGIN) & (band == bands - 1), 0.0, coarse[16:])


def thin(fields, where, bands):
    members, variables, rows, length = fields.shape
    lon = thin_lon_table()
    lat = thin_lat_table(rows)
    columns = length // STRIDE
    tile = jax.ShapeDtypeStruct((members, variables, 8, columns), jnp.float32)
    spec = pl.BlockSpec((1, variables, 8, columns), lambda m: (m, 0, 0, 0))
    return pl.pallas_call(
        functools.partial(thin_kernel, bands),
        grid=(members,),
        in_specs=[
            pl.BlockSpec(memory_space=pltpu.SMEM),
            pl.BlockSpec((1, variables, rows, length), lambda m: (m, 0, 0, 0)),
            pl.BlockSpec(lon.shape, lambda m: (0, 0, 0)),
            pl.BlockSpec(lat.shape, lambda m: (0, 0)),
        ],
        out_specs=[spec] * 3,
        out_shape=[tile] * 3,
        compiler_params=pltpu.CompilerParams(vmem_limit_bytes=VMEM),
        cost_estimate=pl.CostEstimate(flops=4_000_000_000, bytes_accessed=10_000_000, transcendentals=0),
    )(where, fields, jnp.asarray(lon), jnp.asarray(lat))


def soft_sign(diff):
    return diff * lax.rsqrt(diff * diff + HUBER * HUBER)


def pair_kernel(ensemble, own_ref, *refs):
    others, observed_ref, out_ref = refs[:-2], refs[-2], refs[-1]
    members = own_ref.shape[0]
    for j in range(own_ref.shape[-1] // LANES):
        columns = pl.ds(j * LANES, LANES)
        own = [own_ref[m, 0, :, columns] for m in range(members)]
        total = [None] * members
        for m in range(members):
            for n in range(m + 1, members):
                term = soft_sign(own[m] - own[n])
                total[m] = term if total[m] is None else total[m] + term
                total[n] = -term if total[n] is None else total[n] - term
        for other in others:
            for n in range(other.shape[0]):
                value = other[n, 0, :, columns]
                for m in range(members):
                    total[m] = total[m] + soft_sign(own[m] - value)
        seen = observed_ref[0, :, columns]
        for m in range(members):
            out_ref[m, 0, :, columns] = soft_sign(own[m] - seen) * (1.0 / ensemble) - total[m] * (
                1.0 / (ensemble * (ensemble - 1))
            )


def pair_gradient(own, others, observed, ensemble):
    members, variables, rows, columns = own.shape
    spec = pl.BlockSpec((members, 1, 8, columns), lambda v, r: (0, v, r, 0))
    return pl.pallas_call(
        functools.partial(pair_kernel, ensemble),
        grid=(variables, rows // 8),
        in_specs=[spec] * (1 + len(others))
        + [pl.BlockSpec((1, 8, columns), lambda v, r: (v, r, 0))],
        out_specs=spec,
        out_shape=jax.ShapeDtypeStruct(own.shape, jnp.float32),
        compiler_params=pltpu.CompilerParams(vmem_limit_bytes=VMEM),
        cost_estimate=pl.CostEstimate(flops=25_000_000, bytes_accessed=3_000_000, transcendentals=4_000_000),
    )(own, *others, observed)


def spread_kernel(bands, where_ref, top_ref, mid_ref, low_ref, lat_ref, lon_ref, out_ref):
    variables, rows, length = out_ref.shape[1:]
    band = where_ref[0]
    row = lax.broadcasted_iota(jnp.int32, top_ref.shape[2:], 0)
    tall = []
    for v in range(variables):
        top = jnp.where((row < MARGIN) & (band == 0), 0.0, top_ref[0, v])
        low = jnp.where((row >= MARGIN) & (band == bands - 1), 0.0, low_ref[0, v])
        grad = jnp.concatenate([top, mid_ref[0, v], low], axis=0)
        high = grad.astype(jnp.bfloat16).astype(jnp.float32)
        stack = jnp.concatenate([high, grad - high, high], axis=0).astype(jnp.bfloat16)
        tall.append(dot(lat_ref[...], stack))
    tall = jnp.concatenate(tall, axis=0)
    tiles = [tall[:, j * LANES : (j + 1) * LANES] for j in range(tall.shape[1] // LANES)]
    lane = lax.broadcasted_iota(jnp.int32, tiles[0].shape, 1)
    zero = jnp.zeros_like(tiles[0])
    for k in range(length // BLOCK):
        j = k // 2
        if k % 2 == 0:
            near = jnp.where(lane >= LANES - MARGIN, tiles[j - 1] if j > 0 else zero, tiles[j])
        else:
            near = jnp.where(lane < MARGIN, tiles[j + 1] if j + 1 < len(tiles) else zero, tiles[j])
        stack = jnp.concatenate(split(near), axis=1)
        wide = dot(stack, lon_ref[2 * (k % 2)]) + dot(stack, lon_ref[2 * (k % 2) + 1])
        out_ref[0, :, :, k * BLOCK : (k + 1) * BLOCK] = wide.reshape(variables, rows, BLOCK)


def spread(top, mid, low, where, bands, rows, length, scale):
    members, variables, _, columns = mid.shape
    lat = spread_lat_table(rows, scale)
    lon = spread_lon_table()
    spec = pl.BlockSpec((1, variables, 8, columns), lambda m: (m, 0, 0, 0))
    return pl.pallas_call(
        functools.partial(spread_kernel, bands),
        grid=(members,),
        in_specs=[
            pl.BlockSpec(memory_space=pltpu.SMEM),
            spec,
            spec,
            spec,
            pl.BlockSpec(lat.shape, lambda m: (0, 0)),
            pl.BlockSpec(lon.shape, lambda m: (0, 0, 0)),
        ],
        out_specs=pl.BlockSpec((1, variables, rows, length), lambda m: (m, 0, 0, 0)),
        out_shape=jax.ShapeDtypeStruct((members, variables, rows, length), jnp.float32),
        compiler_params=pltpu.CompilerParams(vmem_limit_bytes=VMEM),
        cost_estimate=pl.CostEstimate(flops=4_000_000_000, bytes_accessed=10_000_000, transcendentals=0),
    )(where, top, mid, low, jnp.asarray(lat), jnp.asarray(lon))


def swap(value, bit):
    devices = lax.axis_size("member")
    return lax.ppermute(value, "member", [(i, i ^ bit) for i in range(devices)])


def shards(fields, observed):
    members, _, rows, length = fields.shape
    bands = lax.axis_size("band")
    ensemble = members * lax.axis_size("member")
    where = lax.axis_index("band").astype(jnp.int32).reshape(1)
    up = [(i, (i + 1) % bands) for i in range(bands)]
    down = [(j, i) for i, j in up]
    seen = lax.ppermute(observed[:, -MARGIN:], "band", up)
    seen = jnp.concatenate([seen, observed[:, :-MARGIN]], axis=1)
    top, mid, low = thin(fields, where, bands)
    top = top + lax.ppermute(low, "band", up)
    own = jnp.concatenate([top, mid], axis=2)
    beside = swap(own, 1)
    across = swap(own, 2)
    corner = swap(across, 1)
    grad = pair_gradient(own, [beside, across, corner], seen, ensemble)
    top, mid = grad[:, :, :8], grad[:, :, 8:]
    low = lax.ppermute(top, "band", down)
    return spread(top, mid, low, where, bands, rows, length, 64.0 * ensemble)


def solution(mesh):
    return jax.shard_map(
        shards,
        mesh=mesh,
        in_specs=(P("member", None, "band", None), P(None, "band", None)),
        out_specs=P("member", None, "band", None),
        check_vma=False,
    )
```

time: 167 us -> 64.5 us (0.39)
  the two profiles are of different devices: /device:TPU:8 before, /device:TPU:0 now
where the time goes in v1:
time: 64.5 us; the launch traced here: 64.2 us
  waiting for transfers between devices  38.8 us (60%)
  Pallas kernels  18.3 us (28%)
  starting transfers between devices  5.2 us (8%)
  local copies, waits for them, and re-layouts  1.72 us (3%)
    ppermute x3, waiting for transfers between devices, swap(): return lax.ppermute(value, 'member', [(i, i ^ bit) for i in range(devices)])  11.7 us
    ppermute x1, waiting for transfers between devices, shards(): top = top + lax.ppermute(low, 'band', up)  11.6 us
    pallas_call x1, Pallas kernels, thin(): pl.pallas_call(functools.partial(thin_kernel, bands), grid=(members,), in...  8.21 us
    ppermute x1, waiting for transfers between devices, shards(): seen = lax.ppermute(observed[:, -MARGIN:], 'band', up)  7.94 us
    ppermute x1, waiting for transfers between devices, shards(): low = lax.ppermute(top, 'band', down)  7.55 us
    pallas_call x1, Pallas kernels, spread(): pl.pallas_call(functools.partial(spread_kernel, bands), grid=(members,),...  6.74 us
    pallas_call x1, Pallas kernels, pair_gradient(): pl.pallas_call(functools.partial(pair_kernel, ensemble), grid=(variables,...  3.34 us
    ppermute x3, starting transfers between devices, swap(): return lax.ppermute(value, 'member', [(i, i ^ bit) for i in range(devices)])  2.99 us
  transfers between devices with their start and end apart: 6, of which 4 were waited for; matrix products, arithmetic and copies ran while one was open for 0% of the time, Pallas kernels for 0%

profile of v1, /device:TPU:0, one launch (start us, length us, event | category | flops | bytes accessed | tf_op | source)
XLA Modules:
  0.0 64.2 jit_solution(2057054102859761554)
XLA Ops:
  0.0 0.0 copy-start.1
  0.0 0.9 %copy-done.1 = bf16[2,256,256]{2,1,0:T(8,128)(2,1)S(1)} copy-done((bf16[2,256,256]{2,1,0:T(8,128)(2,1)S(1)}, bf16[2,256,256]{2,1,0:T(8,128)(2,1)}, u32[]{:S(2)}) %copy-start.1) | copy-done | bytes 262168
  1.0 0.0 copy-start.3
  1.0 0.7 %copy-done.3 = bf16[48,128]{1,0:T(8,128)(2,1)S(1)} copy-done((bf16[48,128]{1,0:T(8,128)(2,1)S(1)}, bf16[48,128]{1,0:T(8,128)(2,1)}, u32[]{:S(2)}) %copy-start.3) | copy-done | bytes 12312
  1.7 0.0 copy-start.4
  1.7 8.2 %shard_map.64 = (f32[8,2,8,512]{3,2,1,0:T(8,128)S(1)}, f32[8,2,8,512]{3,2,1,0:T(8,128)S(1)}, f32[8,2,8,512]{3,2,1,0:T(8,128)S(1)}) custom-call(s32[1]{0:T(128)} %bitcast.where_ref, f32[8,2,64,2048]{3,2,1,0:T(8,128)} %x_ref.1, bf16[2,256,256]{2,1,0:T(8,128)(2,1)S(1)} %copy-done.1, bf16[48,128]{1,0:T(8,128)(2,1)S(1)} %copy-done.3), custom_call_target="tpu_custom_call" | custom-call | flops 4000000000 | bytes 10000000 | tf_op jit(solution)/shard_map/pallas_call | solution.py:120
  9.9 0.0 copy-start
  9.9 0.0 copy-start.2
  9.9 2.1 %collective-permute-start = (f32[8,2,8,512]{3,2,1,0:T(8,128)S(1)}, f32[8,2,8,512]{3,2,1,0:T(8,128)S(1)}, u32[]{:S(2)}, u32[]{:S(2)}) collective-permute-start(f32[8,2,8,512]{3,2,1,0:T(8,128)S(1)} %get-tuple-element.9), channel_id=1, source_target_pairs={{0,1},{1,2},{2,3},{3,4},{4,5},{5,6},{6,7},{7,8},{8,9},{9,10},{10,1... | collective-permute-start | bytes 786440 | tf_op jit(solution)/shard_map/ppermute | solution.py:244
  12.0 11.6 %collective-permute-done = f32[8,2,8,512]{3,2,1,0:T(8,128)S(1)} collective-permute-done((f32[8,2,8,512]{3,2,1,0:T(8,128)S(1)}, f32[8,2,8,512]{3,2,1,0:T(8,128)S(1)}, u32[]{:S(2)}, u32[]{:S(2)}) %collective-permute-start) | collective-permute-done | bytes 262176 | tf_op jit(solution)/shard_map/ppermute | solution.py:244
  23.7 3.0 %collective-permute-start.2 = (f32[8,2,16,512]{3,2,1,0:T(8,128)S(1)}, f32[8,2,16,512]{3,2,1,0:T(8,128)S(1)}, u32[]{:S(2)}, u32[]{:S(2)}) collective-permute-start(f32[8,2,16,512]{3,2,1,0:T(8,128)S(1)} %pad_maximum_fusion.own_ref), channel_id=1, source_target_pairs={{0,64},{32,96},{64,0},{96,32},{1,65},{33,97},{65,1},{97,33},{2,66}... | collective-permute-start | bytes 1572872 | tf_op jit(solution)/shard_map/ppermute | solution.py:231
  26.7 0.0 collective-permute-start.1
  26.7 11.7 %collective-permute-done.2.refs_1_ = f32[8,2,16,512]{3,2,1,0:T(8,128)S(1)} collective-permute-done((f32[8,2,16,512]{3,2,1,0:T(8,128)S(1)}, f32[8,2,16,512]{3,2,1,0:T(8,128)S(1)}, u32[]{:S(2)}, u32[]{:S(2)}) %collective-permute-start.2) | collective-permute-done | bytes 524320 | tf_op jit(solution)/shard_map/ppermute | solution.py:231
  38.4 0.0 collective-permute-start.3
  38.4 0.0 copy-done.4
  38.4 0.1 collective-permute-start.4
  38.5 7.9 %collective-permute-done.4 = f32[2,4,512]{2,1,0:T(4,128)S(1)} collective-permute-done((f32[2,4,512]{2,1,0:T(4,128)S(1)}, f32[2,4,512]{2,1,0:T(4,128)S(1)}, u32[]{:S(2)}, u32[]{:S(2)}) %collective-permute-start.4) | collective-permute-done | bytes 16416 | tf_op jit(solution)/shard_map/ppermute | solution.py:241
  46.4 0.0 collective-permute-done.1.refs_0_
  46.4 0.0 collective-permute-done.3.refs_2_
  46.5 3.3 %shard_map.65 = f32[8,2,16,512]{3,2,1,0:T(8,128)S(1)} custom-call(f32[8,2,16,512]{3,2,1,0:T(8,128)S(1)} %pad_maximum_fusion.own_ref, f32[8,2,16,512]{3,2,1,0:T(8,128)S(1)} %collective-permute-done.1.refs_0_, f32[8,2,16,512]{3,2,1,0:T(8,128)S(1)} %collective-permute-done.2.refs_1_, f32[8,2,16,512]{3,2,1,0:T(8,128)S(1)} %collective-permute-done.3.refs_2_, ...), custom_call_target="tpu_custom_call" | custom-call | flops 25000000 | bytes 3000000 | tf_op jit(solution)/shard_map/pallas_call | solution.py:167
  49.8 0.1 collective-permute-start.5
  49.9 7.6 %collective-permute-done.5.low_ref = f32[8,2,8,512]{3,2,1,0:T(8,128)S(1)} collective-permute-done((f32[8,2,8,512]{3,2,1,0:T(8,128)S(1)}, f32[8,2,8,512]{3,2,1,0:T(8,128)S(1)}, u32[]{:S(2)}, u32[]{:S(2)}) %collective-permute-start.5) | collective-permute-done | bytes 262176 | tf_op jit(solution)/shard_map/ppermute | solution.py:251
  57.5 0.0 copy-done
  57.5 0.0 copy-done.2
  57.5 6.7 %shard_map.66 = f32[8,2,64,2048]{3,2,1,0:T(8,128)} custom-call(s32[1]{0:T(128)} %bitcast.where_ref, f32[8,2,8,512]{3,2,1,0:T(8,128)S(1)} %get-tuple-element.12.top_ref, f32[8,2,8,512]{3,2,1,0:T(8,128)S(1)} %get-tuple-element.11.mid_ref, f32[8,2,8,512]{3,2,1,0:T(8,128)S(1)} %collective-permute-done.5.low_ref, bf16[64,72]{1,0:T(8,128)(2,1)S(1)} %copy-done.2, ...), custom_call_target="tpu_custom_call" | custom-call | flops 4000000000 | bytes 10000000 | tf_op jit(solution)/shard_map/pallas_call | solution.py:211
  (5 shorter events, 0.1 us)
Async XLA Ops:
  0.0 0.9 %copy-start.1 = (bf16[2,256,256]{2,1,0:T(8,128)(2,1)S(1)}, bf16[2,256,256]{2,1,0:T(8,128)(2,1)}, u32[]{:S(2)}) copy-start(bf16[2,256,256]{2,1,0:T(8,128)(2,1)} %constant.12.clone.lon_ref) | copy-start | bytes 786436
  1.0 0.7 %copy-start.3 = (bf16[48,128]{1,0:T(8,128)(2,1)S(1)}, bf16[48,128]{1,0:T(8,128)(2,1)}, u32[]{:S(2)}) copy-start(bf16[48,128]{1,0:T(8,128)(2,1)} %constant.13.clone.lat_ref) | copy-start | bytes 36868
  1.7 36.7 %copy-start.4 = (f32[2,16,512]{2,1,0:T(8,128)S(1)}, f32[2,16,512]{2,1,0:T(8,128)}, u32[]{:S(2)}) copy-start(f32[2,16,512]{2,1,0:T(8,128)} %param.7) | copy-start | bytes 196612
  9.9 47.6 %copy-start = (bf16[4,256,256]{2,1,0:T(8,128)(2,1)S(1)}, bf16[4,256,256]{2,1,0:T(8,128)(2,1)}, u32[]{:S(2)}) copy-start(bf16[4,256,256]{2,1,0:T(8,128)(2,1)} %constant.15.clone.lon_ref) | copy-start | bytes 1572868
  9.9 47.6 %copy-start.2 = (bf16[64,72]{1,0:T(8,128)(2,1)S(1)}, bf16[64,72]{1,0:T(8,128)(2,1)}, u32[]{:S(2)}) copy-start(bf16[64,72]{1,0:T(8,128)(2,1)} %constant.14.clone.lat_ref) | copy-start | bytes 27652
  9.9 13.7 %collective-permute-start = (f32[8,2,8,512]{3,2,1,0:T(8,128)S(1)}, f32[8,2,8,512]{3,2,1,0:T(8,128)S(1)}, u32[]{:S(2)}, u32[]{:S(2)}) collective-permute-start(f32[8,2,8,512]{3,2,1,0:T(8,128)S(1)} %get-tuple-element.9), channel_id=1, source_target_pairs={{0,1},{1,2},{2,3},{3,4},{4,5},{5,6},{6,7},{7,8},{8,9},{9,10},{10,1... | collective-permute-start | bytes 786440 | tf_op jit(solution)/shard_map/ppermute | solution.py:244
  23.7 14.7 %collective-permute-start.2 = (f32[8,2,16,512]{3,2,1,0:T(8,128)S(1)}, f32[8,2,16,512]{3,2,1,0:T(8,128)S(1)}, u32[]{:S(2)}, u32[]{:S(2)}) collective-permute-start(f32[8,2,16,512]{3,2,1,0:T(8,128)S(1)} %pad_maximum_fusion.own_ref), channel_id=1, source_target_pairs={{0,64},{32,96},{64,0},{96,32},{1,65},{33,97},{65,1},{97,33},{2,66}... | collective-permute-start | bytes 1572872 | tf_op jit(solution)/shard_map/ppermute | solution.py:231
  26.7 19.8 %collective-permute-start.1 = (f32[8,2,16,512]{3,2,1,0:T(8,128)S(1)}, f32[8,2,16,512]{3,2,1,0:T(8,128)S(1)}, u32[]{:S(2)}, u32[]{:S(2)}) collective-permute-start(f32[8,2,16,512]{3,2,1,0:T(8,128)S(1)} %pad_maximum_fusion.own_ref), channel_id=1, source_target_pairs={{0,32},{32,0},{64,96},{96,64},{1,33},{33,1},{65,97},{97,65},{2,34}... | collective-permute-start | bytes 1572872 | tf_op jit(solution)/shard_map/ppermute | solution.py:231
  38.4 8.1 %collective-permute-start.3 = (f32[8,2,16,512]{3,2,1,0:T(8,128)S(1)}, f32[8,2,16,512]{3,2,1,0:T(8,128)S(1)}, u32[]{:S(2)}, u32[]{:S(2)}) collective-permute-start(f32[8,2,16,512]{3,2,1,0:T(8,128)S(1)} %collective-permute-done.2.refs_1_), channel_id=1, source_target_pairs={{0,32},{32,0},{64,96},{96,64},{1,33},{33,1},{65,97},{97,65},{2,34}... | collective-permute-start | bytes 1572872 | tf_op jit(solution)/shard_map/ppermute | solution.py:231
  38.4 8.0 %collective-permute-start.4 = (f32[2,4,512]{2,1,0:T(4,128)S(1)}, f32[2,4,512]{2,1,0:T(4,128)S(1)}, u32[]{:S(2)}, u32[]{:S(2)}) collective-permute-start(f32[2,4,512]{2,1,0:T(4,128)S(1)} %slice.12), channel_id=1, source_target_pairs={{0,1},{1,2},{2,3},{3,4},{4,5},{5,6},{6,7},{7,8},{8,9},{9,10},{10,1... | collective-permute-start | bytes 49160 | tf_op jit(solution)/shard_map/ppermute | solution.py:241
  49.8 7.6 %collective-permute-start.5 = (f32[8,2,8,512]{3,2,1,0:T(8,128)S(1)}, f32[8,2,8,512]{3,2,1,0:T(8,128)S(1)}, u32[]{:S(2)}, u32[]{:S(2)}) collective-permute-start(f32[8,2,8,512]{3,2,1,0:T(8,128)S(1)} %get-tuple-element.12.top_ref), channel_id=1, source_target_pairs={{1,0},{2,1},{3,2},{4,3},{5,4},{6,5},{7,6},{8,7},{9,8},{10,9},{11,1... | collective-permute-start | bytes 786440 | tf_op jit(solution)/shard_map/ppermute | solution.py:251

commit v2 on v1

v2 whole, which is shorter than its diff:
```python
import functools

import jax
import jax.numpy as jnp
import ml_dtypes
import numpy as np
from jax import lax
from jax.experimental import pallas as pl
from jax.experimental.pallas import tpu as pltpu
from jax.sharding import PartitionSpec as P

RADIUS = 16
SIGMA = 6.0
HUBER = 0.05
STRIDE = 4
MARGIN = RADIUS // STRIDE
LANES = 128
BLOCK = 256
TILE = 8
HALF = 32
NEAR = HALF // STRIDE + 2 * MARGIN
GROUP = 2
AHEAD = 3
VMEM = 40 * 1024 * 1024
WHOLE = 50 * 1024 * 1024


def kern(offset):
    taps = np.arange(-RADIUS, RADIUS + 1).astype(np.float64)
    norm = np.sum(np.exp(-taps * taps / (2.0 * SIGMA * SIGMA)))
    spot = np.asarray(offset).astype(np.float64)
    inside = np.abs(spot) <= RADIUS
    return np.where(inside, np.exp(-spot * spot / (2.0 * SIGMA * SIGMA)), 0.0) / norm


def parts(table):
    high = table.astype(np.float32).astype(ml_dtypes.bfloat16)
    low = (table - high.astype(np.float64)).astype(ml_dtypes.bfloat16)
    return high, low


def lon_offsets():
    lane = np.arange(LANES)
    even = np.where(lane < LANES - MARGIN, lane, lane - LANES)
    odd = np.where(lane < MARGIN, lane + LANES, lane) - LANES // 2
    fine = np.arange(BLOCK)
    return [fine[:, None] - STRIDE * place[None, :] for place in (even, odd)]


def spread_lon_table():
    pairs = [parts(kern(offset).T) for offset in lon_offsets()]
    return np.stack([np.concatenate([part, part], axis=0) for pair in pairs for part in pair])


def half_table():
    near = np.arange(NEAR) - MARGIN
    return kern(np.arange(HALF)[:, None] - STRIDE * near[None, :])


def per_image(table, images):
    eye = np.eye(images, dtype=np.float32)
    return np.kron(eye, table.astype(np.float32)).astype(ml_dtypes.bfloat16)


def spread_lat_table(images, scale):
    high, low = (per_image(part, images) for part in parts(scale * half_table()))
    return np.concatenate([high, high, low], axis=1)


def dot(a, b):
    return jnp.dot(a, b, preferred_element_type=jnp.float32)


def split(value):
    high = value.astype(jnp.bfloat16)
    low = (value - high.astype(jnp.float32)).astype(jnp.bfloat16)
    return high, low


def outside(shape, axis, band, bands, half):
    row = lax.broadcasted_iota(jnp.int32, shape, axis)
    above = (row < MARGIN) & (band == 0) & (half == 0)
    below = (row >= MARGIN) & (band == bands - 1) & (half == 1)
    return above | below


def taps(offset):
    norm = np.sum(np.exp(-np.arange(-RADIUS, RADIUS + 1).astype(np.float64) ** 2 / (2.0 * SIGMA * SIGMA)))
    spot = offset.astype(jnp.float32)
    value = jnp.exp(spot * spot * (-1.0 / (2.0 * SIGMA * SIGMA))) * (1.0 / norm)
    return jnp.where(jnp.abs(offset) <= RADIUS, value, 0.0)


def fill_thin_tables(lon_ref, lat_ref, variables, rows):
    shape = (BLOCK, LANES)
    fine = lax.broadcasted_iota(jnp.int32, shape, 0)
    lane = lax.broadcasted_iota(jnp.int32, shape, 1)
    even = jnp.where(lane < LANES - MARGIN, lane, lane - LANES)
    odd = jnp.where(lane < MARGIN, lane + LANES, lane) - LANES // 2
    for i, place in enumerate((even, odd)):
        high, low = split(taps(fine - STRIDE * place))
        lon_ref[i, :, :LANES] = high
        lon_ref[i, :, LANES:] = low
    near = rows // STRIDE + 2 * MARGIN
    depth = variables * rows
    shape = (variables * near, depth)
    out = lax.broadcasted_iota(jnp.int32, shape, 0)
    row = lax.broadcasted_iota(jnp.int32, shape, 1)
    image = sum((out >= v * near).astype(jnp.int32) for v in range(1, variables))
    offset = (row - image * rows) - STRIDE * (out - image * near - MARGIN)
    inside = (row >= image * rows) & (row < (image + 1) * rows)
    high, low = split(jnp.where(inside, taps(offset), 0.0))
    for part, value in enumerate((high, low)):
        place = pl.ds(part * variables * near, variables * near)
        lat_ref[place, :depth] = value
        lat_ref[place, depth:] = value


def thin_rows(value, lon_ref, lat_ref):
    variables, rows, length = value.shape
    value = value.reshape(variables * rows, length)
    count = length // BLOCK
    depth = value.shape[0]
    half = count // 2
    sums = [None] * count
    for odd in range(2):
        pairs = [split(value[:, k * BLOCK : (k + 1) * BLOCK]) for k in range(odd, count, 2)]
        stack = jnp.concatenate([p[0] for p in pairs] + [p[1] for p in pairs], axis=0)
        both = dot(stack, lon_ref[odd])
        both = both[:, :LANES] + both[:, LANES:]
        for i in range(half):
            sums[2 * i + odd] = (
                both[i * depth : (i + 1) * depth]
                + both[(half + i) * depth : (half + i + 1) * depth]
            )
    lane = lax.broadcasted_iota(jnp.int32, sums[0].shape, 1)
    zero = jnp.zeros_like(sums[0])
    columns = []
    for j in range(half):
        after = sums[2 * j + 2] if 2 * j + 2 < count else zero
        before = sums[2 * j - 1] if j > 0 else zero
        columns.append(
            jnp.where(lane >= LANES - MARGIN, after, sums[2 * j])
            + jnp.where(lane < MARGIN, before, sums[2 * j + 1])
        )
    high, low = split(jnp.concatenate(columns, axis=1))
    both = dot(lat_ref[...], jnp.concatenate([high, low], axis=0))
    middle = both.shape[0] // 2
    coarse = both[:middle] + both[middle:]
    return coarse.reshape(variables, 3, TILE, length // STRIDE)


def thin_kernel(bands, where_ref, x_ref, seen_hbm, near_ref, far_ref, mid_ref, held, lon_ref, lat_ref, seen_ref, arrived, seen_here):
    band = where_ref[0]
    even = band % 2 == 0
    members, variables, rows, _ = held.shape

    def copy(m):
        return pltpu.make_async_copy(x_ref.at[m], held.at[m], arrived.at[m])

    for m in range(AHEAD):
        copy(m).start()
    seen_copy = pltpu.make_async_copy(seen_hbm, seen_ref, seen_here)
    seen_copy.start()
    fill_thin_tables(lon_ref, lat_ref, variables, rows)
    for m in range(members):
        copy(m).wait()
        if m + AHEAD < members:
            copy(m + AHEAD).start()
        coarse = thin_rows(held[m], lon_ref, lat_ref)
        upper, lower = coarse[:, 0], coarse[:, 2]
        upper = jnp.where(outside(upper.shape, 1, band, bands, 0), 0.0, upper)
        lower = jnp.where(outside(lower.shape, 1, band, bands, 1), 0.0, lower)
        near_ref[m] = jnp.where(even, lower, upper)
        far_ref[m] = jnp.where(even, upper, lower)
        mid_ref[m] = coarse[:, 1]
    seen_copy.wait()
    seen = seen_ref[...]
    zero = jnp.zeros((seen.shape[0], MARGIN, seen.shape[2]), jnp.float32)
    upper = jnp.concatenate([zero, seen[:, :MARGIN]], axis=1)
    lower = jnp.concatenate([seen[:, -MARGIN:], zero], axis=1)
    near_ref[members] = jnp.where(even, lower, upper)
    far_ref[members] = jnp.where(even, upper, lower)


def thin(fields, observed, where, bands):
    members, variables, rows, length = fields.shape
    columns = length // STRIDE
    near = rows // STRIDE + 2 * MARGIN
    full = pl.BlockSpec(memory_space=pltpu.VMEM)
    any_space = pl.BlockSpec(memory_space=pl.ANY)
    edge = jax.ShapeDtypeStruct((members + 1, variables, TILE, columns), jnp.float32)
    return pl.pallas_call(
        functools.partial(thin_kernel, bands),
        in_specs=[pl.BlockSpec(memory_space=pltpu.SMEM), any_space, any_space],
        out_specs=[full] * 3,
        out_shape=[edge, edge, jax.ShapeDtypeStruct((members, variables, TILE, columns), jnp.float32)],
        scratch_shapes=[
            pltpu.VMEM(fields.shape, jnp.float32),
            pltpu.VMEM((2, BLOCK, 2 * LANES), jnp.bfloat16),
            pltpu.VMEM((2 * variables * near, 2 * variables * rows), jnp.bfloat16),
            pltpu.VMEM(observed.shape, jnp.float32),
            pltpu.SemaphoreType.DMA((members,)),
            pltpu.SemaphoreType.DMA,
        ],
        compiler_params=pltpu.CompilerParams(vmem_limit_bytes=WHOLE),
        cost_estimate=pl.CostEstimate(flops=1, bytes_accessed=1, transcendentals=0),
    )(where, fields, observed)


def soft_sign(diff):
    return diff * lax.rsqrt(diff * diff + HUBER * HUBER)


def pair_kernel(ensemble, own_ref, beside_ref, across_ref, corner_ref, seen_ref, out_ref):
    members, variables, _, columns = own_ref.shape
    tiles = columns // LANES

    def step(i, carry):
        v = i // tiles
        place = pl.ds(pl.multiple_of((i % tiles) * LANES, LANES), LANES)
        own = [own_ref[m, v, :, place] for m in range(members)]
        total = [None] * members
        for m in range(members):
            for n in range(m + 1, members):
                term = soft_sign(own[m] - own[n])
                total[m] = term if total[m] is None else total[m] + term
                total[n] = -term if total[n] is None else total[n] - term
        for other in (beside_ref, across_ref, corner_ref):
            for n in range(members):
                value = other[n, v, :, place]
                for m in range(members):
                    total[m] = total[m] + soft_sign(own[m] - value)
        seen = seen_ref[v, :, place]
        for m in range(members):
            out_ref[m, v, :, place] = soft_sign(own[m] - seen) * (1.0 / ensemble) - total[m] * (
                1.0 / (ensemble * (ensemble - 1))
            )
        return carry

    lax.fori_loop(0, variables * tiles, step, 0)


def pair_gradient(own, beside, across, corner, seen, ensemble):
    full = pl.BlockSpec(memory_space=pltpu.VMEM)
    return pl.pallas_call(
        functools.partial(pair_kernel, ensemble),
        in_specs=[full] * 5,
        out_specs=full,
        out_shape=jax.ShapeDtypeStruct(own.shape, jnp.float32),
        compiler_params=pltpu.CompilerParams(vmem_limit_bytes=VMEM),
        cost_estimate=pl.CostEstimate(flops=1, bytes_accessed=1, transcendentals=0),
    )(own, beside, across, corner, seen)


def spread_rows(edge, mid, band, bands, half, lat_ref, lon_ref, store):
    group, variables, _, columns = edge.shape
    edge = jnp.where(outside(edge.shape, 2, band, bands, half), 0.0, edge)
    upper = jnp.where(half == 0, edge, mid)
    lower = jnp.where(half == 0, mid, edge)
    grad = jnp.stack([upper, lower], axis=2).reshape(group * variables * NEAR, columns)
    high, low = split(grad)
    tall = dot(lat_ref[...], jnp.concatenate([high, low, high], axis=0))
    depth = tall.shape[0]
    tiles = [tall[:, j * LANES : (j + 1) * LANES] for j in range(columns // LANES)]
    lane = lax.broadcasted_iota(jnp.int32, tiles[0].shape, 1)
    zero = jnp.zeros_like(tiles[0])
    count = len(tiles)
    for odd in range(2):
        stacks = []
        for j in range(count):
            if odd:
                after = tiles[j + 1] if j + 1 < count else zero
                near = jnp.where(lane < MARGIN, after, tiles[j])
            else:
                before = tiles[j - 1] if j > 0 else zero
                near = jnp.where(lane >= LANES - MARGIN, before, tiles[j])
            stacks.append(jnp.concatenate(split(near), axis=1))
        stack = jnp.concatenate(stacks, axis=0)
        wide = dot(stack, lon_ref[2 * odd]) + dot(stack, lon_ref[2 * odd + 1])
        for j in range(count):
            store(2 * j + odd, wide[j * depth : (j + 1) * depth].reshape(group, variables, HALF, BLOCK))


def spread_kernel(bands, where_ref, *refs):
    edge_ref, mid_ref, lat_ref, lon_ref, out_ref, held, sent = refs[-7:]
    band, half = where_ref[0], where_ref[1]
    members = held.shape[0]
    start = pl.multiple_of(half * HALF, HALF)

    def copy(c):
        group = pl.ds(c * GROUP, GROUP)
        return pltpu.make_async_copy(
            held.at[group], out_ref.at[group, :, pl.ds(start, HALF), :], sent.at[c]
        )

    chunks = members // GROUP
    for c in range(chunks):
        group = pl.ds(c * GROUP, GROUP)

        def store(k, value, group=group):
            held[group, :, :, k * BLOCK : (k + 1) * BLOCK] = value

        spread_rows(edge_ref[group], mid_ref[group], band, bands, half, lat_ref, lon_ref, store)
        copy(c).start()
    for c in range(chunks):
        copy(c).wait()


def spread(edge, mid, where, bands, shape, scale, out=None):
    members, variables, _, length = shape
    lat = spread_lat_table(GROUP * variables, scale)
    lon = spread_lon_table()
    full = pl.BlockSpec(memory_space=pltpu.VMEM)
    any_space = pl.BlockSpec(memory_space=pl.ANY)
    extra = [] if out is None else [out]
    return pl.pallas_call(
        functools.partial(spread_kernel, bands),
        in_specs=[pl.BlockSpec(memory_space=pltpu.SMEM)] + [any_space] * len(extra) + [full] * 4,
        out_specs=any_space,
        out_shape=jax.ShapeDtypeStruct(shape, jnp.float32),
        scratch_shapes=[
            pltpu.VMEM((members, variables, HALF, length), jnp.float32),
            pltpu.SemaphoreType.DMA((members // GROUP,)),
        ],
        input_output_aliases={1: 0} if extra else {},
        compiler_params=pltpu.CompilerParams(vmem_limit_bytes=VMEM),
        cost_estimate=pl.CostEstimate(flops=1, bytes_accessed=1, transcendentals=0),
    )(where, *extra, edge, mid, jnp.asarray(lat), jnp.asarray(lon))


def swap(value, bit):
    devices = lax.axis_size("member")
    return lax.ppermute(value, "member", [(i, i ^ bit) for i in range(devices)])


def pairs_of(bands, first):
    pairs = [(i, i + 1) for i in range(first, bands - 1, 2)]
    return pairs + [(j, i) for i, j in pairs]


def shards(fields, observed):
    members, _, rows, _ = fields.shape
    bands = lax.axis_size("band")
    ensemble = members * lax.axis_size("member")
    band = lax.axis_index("band").astype(jnp.int32)
    far = jnp.stack([band, band % 2])
    near = jnp.stack([band, 1 - band % 2])
    tie = lax.optimization_barrier
    near_part, far_part, mid = thin(fields, observed, band.reshape(1), bands)
    far_come = lax.ppermute(far_part, "band", pairs_of(bands, 1))
    near_come = lax.ppermute(near_part, "band", pairs_of(bands, 0))
    across_mid = swap(mid, 2)
    beside_mid = swap(mid, 1)
    near_tile = near_part[:members] + near_come[:members]
    near_seen = near_part[members] + near_come[members]
    across_near = swap(near_tile, 2)
    beside_near = swap(near_tile, 1)
    across_mid, near_tile = tie((across_mid, near_tile))
    corner_mid = swap(across_mid, 1)
    seen = observed[:, MARGIN:-MARGIN]
    mid_grad = pair_gradient(mid, beside_mid, across_mid, corner_mid, seen, ensemble)
    far_come, mid_grad = tie((far_come, mid_grad))
    far_tile = far_part[:members] + far_come[:members]
    far_seen = far_part[members] + far_come[members]
    across_far = swap(far_tile, 2)
    beside_far = swap(far_tile, 1)
    across_near, beside_far = tie((across_near, beside_far))
    corner_near = swap(across_near, 1)
    near_grad = pair_gradient(near_tile, beside_near, across_near, corner_near, near_seen, ensemble)
    scale = 64.0 * ensemble
    out = spread(near_grad, mid_grad, near, bands, fields.shape, scale)
    across_far, out = tie((across_far, out))
    corner_far = swap(across_far, 1)
    far_grad = pair_gradient(far_tile, beside_far, across_far, corner_far, far_seen, ensemble)
    return spread(far_grad, mid_grad, far, bands, fields.shape, scale, out)


def solution(mesh):
    return jax.shard_map(
        shards,
        mesh=mesh,
        in_specs=(P("member", None, "band", None), P(None, "band", None)),
        out_specs=P("member", None, "band", None),
        check_vma=False,
    )
```

time: 64.5 us -> 46.7 us (0.72)
  the two profiles are of different devices: /device:TPU:0 before, /device:TPU:31 now
where the time goes in v2:
time: 46.7 us; the launch traced here: 46.6 us
  Pallas kernels  17.9 us (38%)
  starting transfers between devices  15.1 us (32%)
  waiting for transfers between devices  12.3 us (26%)
  local copies, waits for them, and re-layouts  0.92 us (2%)
    ppermute x9, waiting for transfers between devices, swap(): return lax.ppermute(value, 'member', [(i, i ^ bit) for i in range(devices)])  10.5 us
    ppermute x9, starting transfers between devices, swap(): return lax.ppermute(value, 'member', [(i, i ^ bit) for i in range(devices)])  9 us
    pallas_call x2, Pallas kernels, spread(): pl.pallas_call(functools.partial(spread_kernel, bands), in_specs=[pl.Bloc...  6.85 us
    pallas_call x1, Pallas kernels, thin(): pl.pallas_call(functools.partial(thin_kernel, bands), in_specs=[pl.BlockS...  6.13 us
    pallas_call x3, Pallas kernels, pair_gradient(): pl.pallas_call(functools.partial(pair_kernel, ensemble), in_specs=[full]...  4.96 us
    ppermute x1, starting transfers between devices, shards(): far_come = lax.ppermute(far_part, 'band', pairs_of(bands, 1))  4.4 us
    ppermute x1, waiting for transfers between devices, shards(): far_come = lax.ppermute(far_part, 'band', pairs_of(bands, 1))  1.77 us
    ppermute x1, starting transfers between devices, shards(): near_come = lax.ppermute(near_part, 'band', pairs_of(bands, 0))  1.71 us
  transfers between devices with their start and end apart: 11, of which 6 were waited for; matrix products, arithmetic and copies ran while one was open for 1% of the time, Pallas kernels for 14%

profile of v2, /device:TPU:31, one launch (start us, length us, event | category | flops | bytes accessed | tf_op | source)
XLA Modules:
  0.0 46.6 jit_solution(13652949886687356968)
XLA Ops:
  0.0 0.9 %copy-done.2 = f32[2,16,512]{2,1,0:T(8,128)S(1)} copy-done((f32[2,16,512]{2,1,0:T(8,128)S(1)}, f32[2,16,512]{2,1,0:T(8,128)}, u32[]{:S(2)}) %copy-start.2) | copy-done | bytes 65560
  0.9 6.1 %shard_map.64 = (f32[9,2,8,512]{3,2,1,0:T(8,128)S(1)}, f32[9,2,8,512]{3,2,1,0:T(8,128)S(1)}, f32[8,2,8,512]{3,2,1,0:T(8,128)S(1)}) custom-call(s32[1]{0:T(128)} %bitcast.where_ref, f32[8,2,64,2048]{3,2,1,0:T(8,128)} %x_ref.1, f32[2,16,512]{2,1,0:T(8,128)S(1)} %copy-done.2), custom_call_target="tpu_custom_call" | custom-call | flops 1 | bytes 1 | tf_op jit(solution)/shard_map/pallas_call | solution.py:193
  7.0 1.7 %collective-permute-start.3 = (f32[9,2,8,512]{3,2,1,0:T(8,128)S(1)}, f32[9,2,8,512]{3,2,1,0:T(8,128)S(1)}, u32[]{:S(2)}, u32[]{:S(2)}) collective-permute-start(f32[9,2,8,512]{3,2,1,0:T(8,128)S(1)} %get-tuple-element.18), channel_id=1, source_target_pairs={{0,1},{2,3},{4,5},{6,7},{8,9},{10,11},{12,13},{14,15},{16,17},{18,... | collective-permute-start | bytes 884744 | tf_op jit(solution)/shard_map/ppermute | solution.py:352
  8.8 1.0 %collective-permute-start.2 = (f32[8,2,8,512]{3,2,1,0:T(8,128)S(1)}, f32[8,2,8,512]{3,2,1,0:T(8,128)S(1)}, u32[]{:S(2)}, u32[]{:S(2)}) collective-permute-start(f32[8,2,8,512]{3,2,1,0:T(8,128)S(1)} %get-tuple-element.17.own_ref), channel_id=1, source_target_pairs={{0,64},{32,96},{64,0},{96,32},{1,65},{33,97},{65,1},{97,33},{2,66}... | collective-permute-start | bytes 786440 | tf_op jit(solution)/shard_map/ppermute | solution.py:334
  9.7 1.2 %collective-permute-start.1 = (f32[8,2,8,512]{3,2,1,0:T(8,128)S(1)}, f32[8,2,8,512]{3,2,1,0:T(8,128)S(1)}, u32[]{:S(2)}, u32[]{:S(2)}) collective-permute-start(f32[8,2,8,512]{3,2,1,0:T(8,128)S(1)} %get-tuple-element.17.own_ref), channel_id=1, source_target_pairs={{0,32},{32,0},{64,96},{96,64},{1,33},{33,1},{65,97},{97,65},{2,34}... | collective-permute-start | bytes 786440 | tf_op jit(solution)/shard_map/ppermute | solution.py:334
  10.9 4.4 %collective-permute-start = (f32[9,2,8,512]{3,2,1,0:T(8,128)S(1)}, f32[9,2,8,512]{3,2,1,0:T(8,128)S(1)}, u32[]{:S(2)}, u32[]{:S(2)}) collective-permute-start(f32[9,2,8,512]{3,2,1,0:T(8,128)S(1)} %get-tuple-element.16), channel_id=1, source_target_pairs={{1,2},{3,4},{5,6},{7,8},{9,10},{11,12},{13,14},{15,16},{17,18},{19... | collective-permute-start | bytes 884744 | tf_op jit(solution)/shard_map/ppermute | solution.py:351
  15.4 0.0 collective-permute-done.3
  15.4 1.7 %collective-permute-done.2.across_ref = f32[8,2,8,512]{3,2,1,0:T(8,128)S(1)} collective-permute-done((f32[8,2,8,512]{3,2,1,0:T(8,128)S(1)}, f32[8,2,8,512]{3,2,1,0:T(8,128)S(1)}, u32[]{:S(2)}, u32[]{:S(2)}) %collective-permute-start.2) | collective-permute-done | bytes 262176 | tf_op jit(solution)/shard_map/ppermute | solution.py:334
  17.1 1.9 %collective-permute-start.4 = (f32[8,2,8,512]{3,2,1,0:T(8,128)S(1)}, f32[8,2,8,512]{3,2,1,0:T(8,128)S(1)}, u32[]{:S(2)}, u32[]{:S(2)}) collective-permute-start(f32[8,2,8,512]{3,2,1,0:T(8,128)S(1)} %collective-permute-done.2.across_ref), channel_id=1, source_target_pairs={{0,32},{32,0},{64,96},{96,64},{1,33},{33,1},{65,97},{97,65},{2,34}... | collective-permute-start | bytes 786440 | tf_op jit(solution)/shard_map/ppermute | solution.py:334
  19.0 0.0 copy-done.3
  19.0 1.0 %collective-permute-start.7 = (f32[8,2,8,512]{3,2,1,0:T(8,128)S(1)}, f32[8,2,8,512]{3,2,1,0:T(8,128)S(1)}, u32[]{:S(2)}, u32[]{:S(2)}) collective-permute-start(f32[8,2,8,512]{3,2,1,0:T(8,128)S(1)} %slice_add_fusion.own_ref), channel_id=1, source_target_pairs={{0,64},{32,96},{64,0},{96,32},{1,65},{33,97},{65,1},{97,33},{2,66}... | collective-permute-start | bytes 786440 | tf_op jit(solution)/shard_map/ppermute | solution.py:334
  20.0 0.0 collective-permute-done.1.beside_ref
  20.0 0.1 collective-permute-done.4.corner_ref
  20.1 1.7 %shard_map.65.refs_1_.refs_2_ = f32[8,2,8,512]{3,2,1,0:T(8,128)S(1)} custom-call(f32[8,2,8,512]{3,2,1,0:T(8,128)S(1)} %get-tuple-element.17.own_ref, f32[8,2,8,512]{3,2,1,0:T(8,128)S(1)} %collective-permute-done.1.beside_ref, f32[8,2,8,512]{3,2,1,0:T(8,128)S(1)} %collective-permute-done.2.across_ref, f32[8,2,8,512]{3,2,1,0:T(8,128)S(1)} %collective-permute-done.4.corner_ref, ...), custom_call_target="tpu_custom_call" | custom-call | flops 1 | bytes 1 | tf_op jit(solution)/shard_map/pallas_call | solution.py:246
  21.8 1.8 %collective-permute-done = f32[9,2,8,512]{3,2,1,0:T(8,128)S(1)} collective-permute-done((f32[9,2,8,512]{3,2,1,0:T(8,128)S(1)}, f32[9,2,8,512]{3,2,1,0:T(8,128)S(1)}, u32[]{:S(2)}, u32[]{:S(2)}) %collective-permute-start) | collective-permute-done | bytes 294944 | tf_op jit(solution)/shard_map/ppermute | solution.py:351
  23.6 0.9 %collective-permute-start.8 = (f32[8,2,8,512]{3,2,1,0:T(8,128)S(1)}, f32[8,2,8,512]{3,2,1,0:T(8,128)S(1)}, u32[]{:S(2)}, u32[]{:S(2)}) collective-permute-start(f32[8,2,8,512]{3,2,1,0:T(8,128)S(1)} %slice_add_fusion.1.own_ref), channel_id=1, source_target_pairs={{0,32},{32,0},{64,96},{96,64},{1,33},{33,1},{65,97},{97,65},{2,34}... | collective-permute-start | bytes 786440 | tf_op jit(solution)/shard_map/ppermute | solution.py:334
  24.5 0.1 collective-permute-start.6
  24.6 2.0 %collective-permute-start.5 = (f32[8,2,8,512]{3,2,1,0:T(8,128)S(1)}, f32[8,2,8,512]{3,2,1,0:T(8,128)S(1)}, u32[]{:S(2)}, u32[]{:S(2)}) collective-permute-start(f32[8,2,8,512]{3,2,1,0:T(8,128)S(1)} %slice_add_fusion.1.own_ref), channel_id=1, source_target_pairs={{0,64},{32,96},{64,0},{96,32},{1,65},{33,97},{65,1},{97,33},{2,66}... | collective-permute-start | bytes 786440 | tf_op jit(solution)/shard_map/ppermute | solution.py:334
  26.6 6.5 %collective-permute-done.7.across_ref = f32[8,2,8,512]{3,2,1,0:T(8,128)S(1)} collective-permute-done((f32[8,2,8,512]{3,2,1,0:T(8,128)S(1)}, f32[8,2,8,512]{3,2,1,0:T(8,128)S(1)}, u32[]{:S(2)}, u32[]{:S(2)}) %collective-permute-start.7) | collective-permute-done | bytes 262176 | tf_op jit(solution)/shard_map/ppermute | solution.py:334
  33.1 0.0 collective-permute-done.8.beside_ref
  33.1 0.5 %collective-permute-start.9 = (f32[8,2,8,512]{3,2,1,0:T(8,128)S(1)}, f32[8,2,8,512]{3,2,1,0:T(8,128)S(1)}, u32[]{:S(2)}, u32[]{:S(2)}) collective-permute-start(f32[8,2,8,512]{3,2,1,0:T(8,128)S(1)} %collective-permute-done.7.across_ref), channel_id=1, source_target_pairs={{0,32},{32,0},{64,96},{96,64},{1,33},{33,1},{65,97},{97,65},{2,34}... | collective-permute-start | bytes 786440 | tf_op jit(solution)/shard_map/ppermute | solution.py:334
  33.6 0.1 pad_add_fusion.1.where_ref
  33.7 0.0 collective-permute-done.6.beside_ref
  33.7 1.1 %collective-permute-done.9.corner_ref = f32[8,2,8,512]{3,2,1,0:T(8,128)S(1)} collective-permute-done((f32[8,2,8,512]{3,2,1,0:T(8,128)S(1)}, f32[8,2,8,512]{3,2,1,0:T(8,128)S(1)}, u32[]{:S(2)}, u32[]{:S(2)}) %collective-permute-start.9) | collective-permute-done | bytes 262176 | tf_op jit(solution)/shard_map/ppermute | solution.py:334
  34.8 1.7 %shard_map.66.refs_0_ = f32[8,2,8,512]{3,2,1,0:T(8,128)S(1)} custom-call(f32[8,2,8,512]{3,2,1,0:T(8,128)S(1)} %slice_add_fusion.own_ref, f32[8,2,8,512]{3,2,1,0:T(8,128)S(1)} %collective-permute-done.6.beside_ref, f32[8,2,8,512]{3,2,1,0:T(8,128)S(1)} %collective-permute-done.7.across_ref, f32[8,2,8,512]{3,2,1,0:T(8,128)S(1)} %collective-permute-done.9.corner_ref, ...), custom_call_target="tpu_custom_call" | custom-call | flops 1 | bytes 1 | tf_op jit(solution)/shard_map/pallas_call | solution.py:246
  36.5 3.4 %shard_map.67.refs_0_ = f32[8,2,64,2048]{3,2,1,0:T(8,128)} custom-call(s32[2]{0:T(128)S(1)} %pad_add_fusion.1.where_ref, f32[8,2,8,512]{3,2,1,0:T(8,128)S(1)} %shard_map.66.refs_0_, f32[8,2,8,512]{3,2,1,0:T(8,128)S(1)} %shard_map.65.refs_1_.refs_2_, bf16[128,192]{1,0:T(8,128)(2,1)S(1)} %copy-done.1, bf16[4,256,256]{2,1,0:T(8,128)(2,1)S(1)} %copy-done), custom_call_target="tpu_custom_call" | custom-call | flops 1 | bytes 1 | tf_op jit(solution)/shard_map/pallas_call | solution.py:317
  39.9 0.0 collective-permute-done.5.across_ref
  39.9 0.4 collective-permute-start.10
  40.3 0.1 pad_add_fusion.where_ref
  40.4 1.1 %collective-permute-done.10.corner_ref = f32[8,2,8,512]{3,2,1,0:T(8,128)S(1)} collective-permute-done((f32[8,2,8,512]{3,2,1,0:T(8,128)S(1)}, f32[8,2,8,512]{3,2,1,0:T(8,128)S(1)}, u32[]{:S(2)}, u32[]{:S(2)}) %collective-permute-start.10) | collective-permute-done | bytes 262176 | tf_op jit(solution)/shard_map/ppermute | solution.py:334
  41.5 1.7 %shard_map.68.refs_1_ = f32[8,2,8,512]{3,2,1,0:T(8,128)S(1)} custom-call(f32[8,2,8,512]{3,2,1,0:T(8,128)S(1)} %slice_add_fusion.1.own_ref, f32[8,2,8,512]{3,2,1,0:T(8,128)S(1)} %collective-permute-done.8.beside_ref, f32[8,2,8,512]{3,2,1,0:T(8,128)S(1)} %collective-permute-done.5.across_ref, f32[8,2,8,512]{3,2,1,0:T(8,128)S(1)} %collective-permute-done.10.corner_ref, ...), custom_call_target="tpu_custom_call" | custom-call | flops 1 | bytes 1 | tf_op jit(solution)/shard_map/pallas_call | solution.py:246
  43.2 3.4 %shard_map.69 = f32[8,2,64,2048]{3,2,1,0:T(8,128)} custom-call(s32[2]{0:T(128)S(1)} %pad_add_fusion.where_ref, f32[8,2,64,2048]{3,2,1,0:T(8,128)} %shard_map.67.refs_0_, f32[8,2,8,512]{3,2,1,0:T(8,128)S(1)} %shard_map.68.refs_1_, f32[8,2,8,512]{3,2,1,0:T(8,128)S(1)} %shard_map.65.refs_1_.refs_2_, ...), custom_call_target="tpu_custom_call", output_to_operand_aliasing={{}: (1, {})} | custom-call | flops 1 | bytes 1 | tf_op jit(solution)/shard_map/pallas_call | solution.py:317
  (11 shorter events, 0.1 us)
Async XLA Ops:
  0.0 36.4 %copy-start = (bf16[4,256,256]{2,1,0:T(8,128)(2,1)S(1)}, bf16[4,256,256]{2,1,0:T(8,128)(2,1)}, u32[]{:S(2)}) copy-start(bf16[4,256,256]{2,1,0:T(8,128)(2,1)} %constant.25.clone.refs_3_.refs_4_) | copy-start | bytes 1572868
  0.0 36.4 %copy-start.1 = (bf16[128,192]{1,0:T(8,128)(2,1)S(1)}, bf16[128,192]{1,0:T(8,128)(2,1)}, u32[]{:S(2)}) copy-start(bf16[128,192]{1,0:T(8,128)(2,1)} %constant.24.clone.refs_2_.refs_3_) | copy-start | bytes 147460
  0.0 0.9 %copy-start.2 = (f32[2,16,512]{2,1,0:T(8,128)S(1)}, f32[2,16,512]{2,1,0:T(8,128)}, u32[]{:S(2)}) copy-start(f32[2,16,512]{2,1,0:T(8,128)} %seen_hbm.1) | copy-start | bytes 196612
  0.9 18.1 %copy-start.3 = (f32[2,16,512]{2,1,0:T(8,128)S(1)}, f32[2,16,512]{2,1,0:T(8,128)}, u32[]{:S(2)}) copy-start(f32[2,16,512]{2,1,0:T(8,128)} %seen_hbm.1) | copy-start | bytes 196612
  7.0 8.3 %collective-permute-start.3 = (f32[9,2,8,512]{3,2,1,0:T(8,128)S(1)}, f32[9,2,8,512]{3,2,1,0:T(8,128)S(1)}, u32[]{:S(2)}, u32[]{:S(2)}) collective-permute-start(f32[9,2,8,512]{3,2,1,0:T(8,128)S(1)} %get-tuple-element.18), channel_id=1, source_target_pairs={{0,1},{2,3},{4,5},{6,7},{8,9},{10,11},{12,13},{14,15},{16,17},{18,... | collective-permute-start | bytes 884744 | tf_op jit(solution)/shard_map/ppermute | solution.py:352
  8.8 8.4 %collective-permute-start.2 = (f32[8,2,8,512]{3,2,1,0:T(8,128)S(1)}, f32[8,2,8,512]{3,2,1,0:T(8,128)S(1)}, u32[]{:S(2)}, u32[]{:S(2)}) collective-permute-start(f32[8,2,8,512]{3,2,1,0:T(8,128)S(1)} %get-tuple-element.17.own_ref), channel_id=1, source_target_pairs={{0,64},{32,96},{64,0},{96,32},{1,65},{33,97},{65,1},{97,33},{2,66}... | collective-permute-start | bytes 786440 | tf_op jit(solution)/shard_map/ppermute | solution.py:334
  9.7 10.3 %collective-permute-start.1 = (f32[8,2,8,512]{3,2,1,0:T(8,128)S(1)}, f32[8,2,8,512]{3,2,1,0:T(8,128)S(1)}, u32[]{:S(2)}, u32[]{:S(2)}) collective-permute-start(f32[8,2,8,512]{3,2,1,0:T(8,128)S(1)} %get-tuple-element.17.own_ref), channel_id=1, source_target_pairs={{0,32},{32,0},{64,96},{96,64},{1,33},{33,1},{65,97},{97,65},{2,34}... | collective-permute-start | bytes 786440 | tf_op jit(solution)/shard_map/ppermute | solution.py:334
  10.9 12.6 %collective-permute-start = (f32[9,2,8,512]{3,2,1,0:T(8,128)S(1)}, f32[9,2,8,512]{3,2,1,0:T(8,128)S(1)}, u32[]{:S(2)}, u32[]{:S(2)}) collective-permute-start(f32[9,2,8,512]{3,2,1,0:T(8,128)S(1)} %get-tuple-element.16), channel_id=1, source_target_pairs={{1,2},{3,4},{5,6},{7,8},{9,10},{11,12},{13,14},{15,16},{17,18},{19... | collective-permute-start | bytes 884744 | tf_op jit(solution)/shard_map/ppermute | solution.py:351
  17.1 3.0 %collective-permute-start.4 = (f32[8,2,8,512]{3,2,1,0:T(8,128)S(1)}, f32[8,2,8,512]{3,2,1,0:T(8,128)S(1)}, u32[]{:S(2)}, u32[]{:S(2)}) collective-permute-start(f32[8,2,8,512]{3,2,1,0:T(8,128)S(1)} %collective-permute-done.2.across_ref), channel_id=1, source_target_pairs={{0,32},{32,0},{64,96},{96,64},{1,33},{33,1},{65,97},{97,65},{2,34}... | collective-permute-start | bytes 786440 | tf_op jit(solution)/shard_map/ppermute | solution.py:334
  19.0 14.1 %collective-permute-start.7 = (f32[8,2,8,512]{3,2,1,0:T(8,128)S(1)}, f32[8,2,8,512]{3,2,1,0:T(8,128)S(1)}, u32[]{:S(2)}, u32[]{:S(2)}) collective-permute-start(f32[8,2,8,512]{3,2,1,0:T(8,128)S(1)} %slice_add_fusion.own_ref), channel_id=1, source_target_pairs={{0,64},{32,96},{64,0},{96,32},{1,65},{33,97},{65,1},{97,33},{2,66}... | collective-permute-start | bytes 786440 | tf_op jit(solution)/shard_map/ppermute | solution.py:334
  23.6 9.5 %collective-permute-start.8 = (f32[8,2,8,512]{3,2,1,0:T(8,128)S(1)}, f32[8,2,8,512]{3,2,1,0:T(8,128)S(1)}, u32[]{:S(2)}, u32[]{:S(2)}) collective-permute-start(f32[8,2,8,512]{3,2,1,0:T(8,128)S(1)} %slice_add_fusion.1.own_ref), channel_id=1, source_target_pairs={{0,32},{32,0},{64,96},{96,64},{1,33},{33,1},{65,97},{97,65},{2,34}... | collective-permute-start | bytes 786440 | tf_op jit(solution)/shard_map/ppermute | solution.py:334
  24.5 9.2 %collective-permute-start.6 = (f32[8,2,8,512]{3,2,1,0:T(8,128)S(1)}, f32[8,2,8,512]{3,2,1,0:T(8,128)S(1)}, u32[]{:S(2)}, u32[]{:S(2)}) collective-permute-start(f32[8,2,8,512]{3,2,1,0:T(8,128)S(1)} %slice_add_fusion.own_ref), channel_id=1, source_target_pairs={{0,32},{32,0},{64,96},{96,64},{1,33},{33,1},{65,97},{97,65},{2,34}... | collective-permute-start | bytes 786440 | tf_op jit(solution)/shard_map/ppermute | solution.py:334
  24.6 15.3 %collective-permute-start.5 = (f32[8,2,8,512]{3,2,1,0:T(8,128)S(1)}, f32[8,2,8,512]{3,2,1,0:T(8,128)S(1)}, u32[]{:S(2)}, u32[]{:S(2)}) collective-permute-start(f32[8,2,8,512]{3,2,1,0:T(8,128)S(1)} %slice_add_fusion.1.own_ref), channel_id=1, source_target_pairs={{0,64},{32,96},{64,0},{96,32},{1,65},{33,97},{65,1},{97,33},{2,66}... | collective-permute-start | bytes 786440 | tf_op jit(solution)/shard_map/ppermute | solution.py:334
  33.1 1.6 %collective-permute-start.9 = (f32[8,2,8,512]{3,2,1,0:T(8,128)S(1)}, f32[8,2,8,512]{3,2,1,0:T(8,128)S(1)}, u32[]{:S(2)}, u32[]{:S(2)}) collective-permute-start(f32[8,2,8,512]{3,2,1,0:T(8,128)S(1)} %collective-permute-done.7.across_ref), channel_id=1, source_target_pairs={{0,32},{32,0},{64,96},{96,64},{1,33},{33,1},{65,97},{97,65},{2,34}... | collective-permute-start | bytes 786440 | tf_op jit(solution)/shard_map/ppermute | solution.py:334
  39.9 1.6 %collective-permute-start.10 = (f32[8,2,8,512]{3,2,1,0:T(8,128)S(1)}, f32[8,2,8,512]{3,2,1,0:T(8,128)S(1)}, u32[]{:S(2)}, u32[]{:S(2)}) collective-permute-start(f32[8,2,8,512]{3,2,1,0:T(8,128)S(1)} %collective-permute-done.5.across_ref), channel_id=1, source_target_pairs={{0,32},{32,0},{64,96},{96,64},{1,33},{33,1},{65,97},{97,65},{2,34}... | collective-permute-start | bytes 786440 | tf_op jit(solution)/shard_map/ppermute | solution.py:334

commit v3 on v2

--- a/solution.py
+++ b/solution.py
@@ -212,7 +212,7 @@
     return diff * lax.rsqrt(diff * diff + HUBER * HUBER)
 
 
-def pair_kernel(ensemble, own_ref, beside_ref, across_ref, corner_ref, seen_ref, out_ref):
+def pair_kernel(ensemble, own_ref, beside_ref, across_ref, seen_ref, out_ref):
     members, variables, _, columns = own_ref.shape
     tiles = columns // LANES
 
@@ -226,7 +226,7 @@
                 term = soft_sign(own[m] - own[n])
                 total[m] = term if total[m] is None else total[m] + term
                 total[n] = -term if total[n] is None else total[n] - term
-        for other in (beside_ref, across_ref, corner_ref):
+        for other in (beside_ref, across_ref):
             for n in range(members):
                 value = other[n, v, :, place]
                 for m in range(members):
@@ -241,16 +241,24 @@
     lax.fori_loop(0, variables * tiles, step, 0)
 
 
-def pair_gradient(own, beside, across, corner, seen, ensemble):
+def pair_gradient(own, beside, across, seen, ensemble):
     full = pl.BlockSpec(memory_space=pltpu.VMEM)
     return pl.pallas_call(
         functools.partial(pair_kernel, ensemble),
-        in_specs=[full] * 5,
+        in_specs=[full] * 4,
         out_specs=full,
         out_shape=jax.ShapeDtypeStruct(own.shape, jnp.float32),
         compiler_params=pltpu.CompilerParams(vmem_limit_bytes=VMEM),
         cost_estimate=pl.CostEstimate(flops=1, bytes_accessed=1, transcendentals=0),
-    )(own, beside, across, corner, seen)
+    )(own, beside, across, seen)
+
+
+def finish(ensemble, group, own_ref, part_ref, corner_ref):
+    own = own_ref[group]
+    total = jnp.zeros_like(own)
+    for n in range(corner_ref.shape[0]):
+        total = total + soft_sign(own - corner_ref[n][None])
+    return part_ref[group] - total * (1.0 / (ensemble * (ensemble - 1)))
 
 
 def spread_rows(edge, mid, band, bands, half, lat_ref, lon_ref, store):
@@ -282,8 +290,13 @@
             store(2 * j + odd, wide[j * depth : (j + 1) * depth].reshape(group, variables, HALF, BLOCK))
 
 
-def spread_kernel(bands, where_ref, *refs):
-    edge_ref, mid_ref, lat_ref, lon_ref, out_ref, held, sent = refs[-7:]
+def spread_kernel(bands, ensemble, first, where_ref, *refs):
+    if first:
+        edge_trio, mid_trio = refs[:3], refs[3:6]
+        lat_ref, lon_ref, out_ref, mid_ref, held, sent = refs[6:]
+    else:
+        edge_trio, mid_ref = refs[1:4], refs[4]
+        lat_ref, lon_ref, out_ref, held, sent = refs[5:]
     band, half = where_ref[0], where_ref[1]
     members = held.shape[0]
     start = pl.multiple_of(half * HALF, HALF)
@@ -301,32 +314,43 @@
         def store(k, value, group=group):
             held[group, :, :, k * BLOCK : (k + 1) * BLOCK] = value
 
-        spread_rows(edge_ref[group], mid_ref[group], band, bands, half, lat_ref, lon_ref, store)
+        edge = finish(ensemble, group, *edge_trio)
+        if first:
+            mid = finish(ensemble, group, *mid_trio)
+            mid_ref[group] = mid
+        else:
+            mid = mid_ref[group]
+        spread_rows(edge, mid, band, bands, half, lat_ref, lon_ref, store)
         copy(c).start()
     for c in range(chunks):
         copy(c).wait()
 
 
-def spread(edge, mid, where, bands, shape, scale, out=None):
+def spread(edge, mid, where, bands, shape, ensemble, out=None):
     members, variables, _, length = shape
-    lat = spread_lat_table(GROUP * variables, scale)
+    lat = spread_lat_table(GROUP * variables, 64.0 * ensemble)
     lon = spread_lon_table()
+    tile = jax.ShapeDtypeStruct(edge[0].shape, jnp.float32)
+    whole = jax.ShapeDtypeStruct(shape, jnp.float32)
     full = pl.BlockSpec(memory_space=pltpu.VMEM)
     any_space = pl.BlockSpec(memory_space=pl.ANY)
-    extra = [] if out is None else [out]
+    first = out is None
+    operands = [*edge, *mid] if first else [out, *edge, mid]
     return pl.pallas_call(
-        functools.partial(spread_kernel, bands),
-        in_specs=[pl.BlockSpec(memory_space=pltpu.SMEM)] + [any_space] * len(extra) + [full] * 4,
-        out_specs=any_space,
-        out_shape=jax.ShapeDtypeStruct(shape, jnp.float32),
+        functools.partial(spread_kernel, bands, ensemble, first),
+        in_specs=[pl.BlockSpec(memory_space=pltpu.SMEM)]
+        + ([full] * 6 if first else [any_space] + [full] * 4)
+        + [full] * 2,
+        out_specs=[any_space, full] if first else any_space,
+        out_shape=[whole, tile] if first else whole,
         scratch_shapes=[
             pltpu.VMEM((members, variables, HALF, length), jnp.float32),
             pltpu.SemaphoreType.DMA((members // GROUP,)),
         ],
-        input_output_aliases={1: 0} if extra else {},
+        input_output_aliases={} if first else {1: 0},
         compiler_params=pltpu.CompilerParams(vmem_limit_bytes=VMEM),
         cost_estimate=pl.CostEstimate(flops=1, bytes_accessed=1, transcendentals=0),
-    )(where, *extra, edge, mid, jnp.asarray(lat), jnp.asarray(lon))
+    )(where, *operands, jnp.asarray(lat), jnp.asarray(lon))
 
 
 def swap(value, bit):
@@ -358,22 +382,23 @@
     beside_near = swap(near_tile, 1)
     across_mid, near_tile = tie((across_mid, near_tile))
     corner_mid = swap(across_mid, 1)
-    seen = observed[:, MARGIN:-MARGIN]
-    mid_grad = pair_gradient(mid, beside_mid, across_mid, corner_mid, seen, ensemble)
-    far_come, mid_grad = tie((far_come, mid_grad))
+    beside_mid, corner_mid = tie((beside_mid, corner_mid))
+    mid_part = pair_gradient(mid, beside_mid, across_mid, observed[:, MARGIN:-MARGIN], ensemble)
+    far_come, mid_part = tie((far_come, mid_part))
     far_tile = far_part[:members] + far_come[:members]
     far_seen = far_part[members] + far_come[members]
     across_far = swap(far_tile, 2)
     beside_far = swap(far_tile, 1)
     across_near, beside_far = tie((across_near, beside_far))
     corner_near = swap(across_near, 1)
-    near_grad = pair_gradient(near_tile, beside_near, across_near, corner_near, near_seen, ensemble)
-    scale = 64.0 * ensemble
-    out = spread(near_grad, mid_grad, near, bands, fields.shape, scale)
+    near_grad = pair_gradient(near_tile, beside_near, across_near, near_seen, ensemble)
+    out, mid_grad = spread(
+        (near_tile, near_grad, corner_near), (mid, mid_part, corner_mid), near, bands, fields.shape, ensemble
+    )
     across_far, out = tie((across_far, out))
     corner_far = swap(across_far, 1)
-    far_grad = pair_gradient(far_tile, beside_far, across_far, corner_far, far_seen, ensemble)
-    return spread(far_grad, mid_grad, far, bands, fields.shape, scale, out)
+    far_grad = pair_gradient(far_tile, beside_far, across_far, far_seen, ensemble)
+    return spread((far_tile, far_grad, corner_far), mid_grad, far, bands, fields.shape, ensemble, out)
 
 
 def solution(mesh):

time: 46.7 us -> 44.7 us (0.957)
  waiting for transfers between devices: 12.3 us -> 10.8 us
  Pallas kernels: 17.9 us -> 17 us
  other arithmetic: 0.23 us -> 0.99 us
    ppermute x9, waiting for transfers between devices: 10.5 us -> 8.58 us  [swap(): return lax.ppermute(value, 'member', [(i, i ^ bit) for i in range(devices)])]
    pallas_call x3, Pallas kernels: 4.96 us -> 3.72 us  [pair_gradient(): pl.pallas_call(functools.partial(pair_kernel, ensemble), in_specs=[full]...]
    add x1, other arithmetic: 0.01 us -> 0.76 us  [shards(): near_seen = near_part[members] + near_come[members]]
  transfers between devices with their start and end apart: 11 -> 11, of which waited for: 6 -> 5; matrix products, arithmetic and copies ran while one was open for 1% -> 2% of each run, Pallas kernels for 14% -> 17%
where the time goes in v3:
time: 44.7 us; the launch traced here: 44.5 us
  Pallas kernels  17 us (38%)
  starting transfers between devices  14.7 us (33%)
  waiting for transfers between devices  10.8 us (24%)
  other arithmetic  0.99 us (2%)
  local copies, waits for them, and re-layouts  0.92 us (2%)
    ppermute x9, starting transfers between devices, swap(): return lax.ppermute(value, 'member', [(i, i ^ bit) for i in range(devices)])  8.61 us
    ppermute x9, waiting for transfers between devices, swap(): return lax.ppermute(value, 'member', [(i, i ^ bit) for i in range(devices)])  8.58 us
    pallas_call x2, Pallas kernels, spread(): pl.pallas_call(functools.partial(spread_kernel, bands, ensemble, first),...  7.18 us
    pallas_call x1, Pallas kernels, thin(): pl.pallas_call(functools.partial(thin_kernel, bands), in_specs=[pl.BlockS...  6.1 us
    ppermute x1, starting transfers between devices, shards(): far_come = lax.ppermute(far_part, 'band', pairs_of(bands, 1))  4.4 us
    pallas_call x3, Pallas kernels, pair_gradient(): pl.pallas_call(functools.partial(pair_kernel, ensemble), in_specs=[full]...  3.72 us
    ppermute x1, waiting for transfers between devices, shards(): far_come = lax.ppermute(far_part, 'band', pairs_of(bands, 1))  2.19 us
    ppermute x1, starting transfers between devices, shards(): near_come = lax.ppermute(near_part, 'band', pairs_of(bands, 0))  1.71 us
  transfers between devices with their start and end apart: 11, of which 5 were waited for; matrix products, arithmetic and copies ran while one was open for 2% of the time, Pallas kernels for 17%

profile of v3, /device:TPU:31, one launch (start us, length us, event | category | flops | bytes accessed | tf_op | source)
XLA Modules:
  0.0 44.5 jit_solution(16366648990504888230)
XLA Ops:
  0.0 0.9 %copy-done.2 = f32[2,16,512]{2,1,0:T(8,128)S(1)} copy-done((f32[2,16,512]{2,1,0:T(8,128)S(1)}, f32[2,16,512]{2,1,0:T(8,128)}, u32[]{:S(2)}) %copy-start.2) | copy-done | bytes 65560
  0.9 6.1 %shard_map.64 = (f32[9,2,8,512]{3,2,1,0:T(8,128)S(1)}, f32[9,2,8,512]{3,2,1,0:T(8,128)S(1)}, f32[8,2,8,512]{3,2,1,0:T(8,128)S(1)}) custom-call(s32[1]{0:T(128)} %bitcast.where_ref, f32[8,2,64,2048]{3,2,1,0:T(8,128)} %x_ref.1, f32[2,16,512]{2,1,0:T(8,128)S(1)} %copy-done.2), custom_call_target="tpu_custom_call" | custom-call | flops 1 | bytes 1 | tf_op jit(solution)/shard_map/pallas_call | solution.py:193
  7.0 1.7 %collective-permute-start.3 = (f32[9,2,8,512]{3,2,1,0:T(8,128)S(1)}, f32[9,2,8,512]{3,2,1,0:T(8,128)S(1)}, u32[]{:S(2)}, u32[]{:S(2)}) collective-permute-start(f32[9,2,8,512]{3,2,1,0:T(8,128)S(1)} %get-tuple-element.22), channel_id=1, source_target_pairs={{0,1},{2,3},{4,5},{6,7},{8,9},{10,11},{12,13},{14,15},{16,17},{18,... | collective-permute-start | bytes 884744 | tf_op jit(solution)/shard_map/ppermute | solution.py:376
  8.7 1.0 %collective-permute-start.2 = (f32[8,2,8,512]{3,2,1,0:T(8,128)S(1)}, f32[8,2,8,512]{3,2,1,0:T(8,128)S(1)}, u32[]{:S(2)}, u32[]{:S(2)}) collective-permute-start(f32[8,2,8,512]{3,2,1,0:T(8,128)S(1)} %get-tuple-element.21.own_ref.refs_3_), channel_id=1, source_target_pairs={{0,64},{32,96},{64,0},{96,32},{1,65},{33,97},{65,1},{97,33},{2,66}... | collective-permute-start | bytes 786440 | tf_op jit(solution)/shard_map/ppermute | solution.py:358
  9.7 1.2 %collective-permute-start.1 = (f32[8,2,8,512]{3,2,1,0:T(8,128)S(1)}, f32[8,2,8,512]{3,2,1,0:T(8,128)S(1)}, u32[]{:S(2)}, u32[]{:S(2)}) collective-permute-start(f32[8,2,8,512]{3,2,1,0:T(8,128)S(1)} %get-tuple-element.21.own_ref.refs_3_), channel_id=1, source_target_pairs={{0,32},{32,0},{64,96},{96,64},{1,33},{33,1},{65,97},{97,65},{2,34}... | collective-permute-start | bytes 786440 | tf_op jit(solution)/shard_map/ppermute | solution.py:358
  10.9 4.4 %collective-permute-start = (f32[9,2,8,512]{3,2,1,0:T(8,128)S(1)}, f32[9,2,8,512]{3,2,1,0:T(8,128)S(1)}, u32[]{:S(2)}, u32[]{:S(2)}) collective-permute-start(f32[9,2,8,512]{3,2,1,0:T(8,128)S(1)} %get-tuple-element.20), channel_id=1, source_target_pairs={{1,2},{3,4},{5,6},{7,8},{9,10},{11,12},{13,14},{15,16},{17,18},{19... | collective-permute-start | bytes 884744 | tf_op jit(solution)/shard_map/ppermute | solution.py:375
  15.3 0.0 collective-permute-done.3
  15.4 1.7 %collective-permute-done.2.across_ref = f32[8,2,8,512]{3,2,1,0:T(8,128)S(1)} collective-permute-done((f32[8,2,8,512]{3,2,1,0:T(8,128)S(1)}, f32[8,2,8,512]{3,2,1,0:T(8,128)S(1)}, u32[]{:S(2)}, u32[]{:S(2)}) %collective-permute-start.2) | collective-permute-done | bytes 262176 | tf_op jit(solution)/shard_map/ppermute | solution.py:358
  17.1 1.9 %collective-permute-start.4 = (f32[8,2,8,512]{3,2,1,0:T(8,128)S(1)}, f32[8,2,8,512]{3,2,1,0:T(8,128)S(1)}, u32[]{:S(2)}, u32[]{:S(2)}) collective-permute-start(f32[8,2,8,512]{3,2,1,0:T(8,128)S(1)} %collective-permute-done.2.across_ref), channel_id=1, source_target_pairs={{0,32},{32,0},{64,96},{96,64},{1,33},{33,1},{65,97},{97,65},{2,34}... | collective-permute-start | bytes 786440 | tf_op jit(solution)/shard_map/ppermute | solution.py:358
  19.0 1.0 %collective-permute-start.7 = (f32[8,2,8,512]{3,2,1,0:T(8,128)S(1)}, f32[8,2,8,512]{3,2,1,0:T(8,128)S(1)}, u32[]{:S(2)}, u32[]{:S(2)}) collective-permute-start(f32[8,2,8,512]{3,2,1,0:T(8,128)S(1)} %slice_add_fusion.own_ref.refs_0_), channel_id=1, source_target_pairs={{0,64},{32,96},{64,0},{96,32},{1,65},{33,97},{65,1},{97,33},{2,66}... | collective-permute-start | bytes 786440 | tf_op jit(solution)/shard_map/ppermute | solution.py:358
  19.9 0.0 collective-permute-done.1.beside_ref
  19.9 0.2 collective-permute-done.4.refs_5_
  20.1 1.2 %shard_map.65.refs_4_ = f32[8,2,8,512]{3,2,1,0:T(8,128)S(1)} custom-call(f32[8,2,8,512]{3,2,1,0:T(8,128)S(1)} %get-tuple-element.21.own_ref.refs_3_, f32[8,2,8,512]{3,2,1,0:T(8,128)S(1)} %collective-permute-done.1.beside_ref, f32[8,2,8,512]{3,2,1,0:T(8,128)S(1)} %collective-permute-done.2.across_ref, f32[2,8,512]{2,1,0:T(8,128)S(1)} %slice.30.seen_ref), custom_call_target="tpu_custom_call" | custom-call | flops 1 | bytes 1 | tf_op jit(solution)/shard_map/pallas_call | solution.py:246
  21.4 2.2 %collective-permute-done = f32[9,2,8,512]{3,2,1,0:T(8,128)S(1)} collective-permute-done((f32[9,2,8,512]{3,2,1,0:T(8,128)S(1)}, f32[9,2,8,512]{3,2,1,0:T(8,128)S(1)}, u32[]{:S(2)}, u32[]{:S(2)}) %collective-permute-start) | collective-permute-done | bytes 294944 | tf_op jit(solution)/shard_map/ppermute | solution.py:375
  23.6 0.9 %collective-permute-start.8 = (f32[8,2,8,512]{3,2,1,0:T(8,128)S(1)}, f32[8,2,8,512]{3,2,1,0:T(8,128)S(1)}, u32[]{:S(2)}, u32[]{:S(2)}) collective-permute-start(f32[8,2,8,512]{3,2,1,0:T(8,128)S(1)} %slice_add_fusion.1.own_ref.refs_1_), channel_id=1, source_target_pairs={{0,32},{32,0},{64,96},{96,64},{1,33},{33,1},{65,97},{97,65},{2,34}... | collective-permute-start | bytes 786440 | tf_op jit(solution)/shard_map/ppermute | solution.py:358
  24.5 0.1 collective-permute-start.6
  24.6 2.0 %collective-permute-start.5 = (f32[8,2,8,512]{3,2,1,0:T(8,128)S(1)}, f32[8,2,8,512]{3,2,1,0:T(8,128)S(1)}, u32[]{:S(2)}, u32[]{:S(2)}) collective-permute-start(f32[8,2,8,512]{3,2,1,0:T(8,128)S(1)} %slice_add_fusion.1.own_ref.refs_1_), channel_id=1, source_target_pairs={{0,64},{32,96},{64,0},{96,32},{1,65},{33,97},{65,1},{97,33},{2,66}... | collective-permute-start | bytes 786440 | tf_op jit(solution)/shard_map/ppermute | solution.py:358
  26.6 6.5 %collective-permute-done.7.across_ref = f32[8,2,8,512]{3,2,1,0:T(8,128)S(1)} collective-permute-done((f32[8,2,8,512]{3,2,1,0:T(8,128)S(1)}, f32[8,2,8,512]{3,2,1,0:T(8,128)S(1)}, u32[]{:S(2)}, u32[]{:S(2)}) %collective-permute-start.7) | collective-permute-done | bytes 262176 | tf_op jit(solution)/shard_map/ppermute | solution.py:358
  33.1 0.0 collective-permute-done.8.beside_ref
  33.1 0.5 %collective-permute-start.9 = (f32[8,2,8,512]{3,2,1,0:T(8,128)S(1)}, f32[8,2,8,512]{3,2,1,0:T(8,128)S(1)}, u32[]{:S(2)}, u32[]{:S(2)}) collective-permute-start(f32[8,2,8,512]{3,2,1,0:T(8,128)S(1)} %collective-permute-done.7.across_ref), channel_id=1, source_target_pairs={{0,32},{32,0},{64,96},{96,64},{1,33},{33,1},{65,97},{97,65},{2,34}... | collective-permute-start | bytes 786440 | tf_op jit(solution)/shard_map/ppermute | solution.py:358
  33.6 0.1 pad_add_fusion.1.where_ref
  33.7 0.8 %fusion.seen_ref = f32[2,8,512]{2,1,0:T(8,128)S(1)} fusion(f32[9,2,8,512]{3,2,1,0:T(8,128)} %copy-done.3, f32[9,2,8,512]{3,2,1,0:T(8,128)S(1)} %get-tuple-element.22), kind=kLoop, calls=%fused_computation.3 | loop fusion | flops 8192 | bytes 98304 | tf_op jit(solution)/shard_map/add | solution.py:380
  34.4 0.0 collective-permute-done.6.beside_ref
  34.4 1.2 %shard_map.66.refs_1_ = f32[8,2,8,512]{3,2,1,0:T(8,128)S(1)} custom-call(f32[8,2,8,512]{3,2,1,0:T(8,128)S(1)} %slice_add_fusion.own_ref.refs_0_, f32[8,2,8,512]{3,2,1,0:T(8,128)S(1)} %collective-permute-done.6.beside_ref, f32[8,2,8,512]{3,2,1,0:T(8,128)S(1)} %collective-permute-done.7.across_ref, f32[2,8,512]{2,1,0:T(8,128)S(1)} %fusion.seen_ref), custom_call_target="tpu_custom_call" | custom-call | flops 1 | bytes 1 | tf_op jit(solution)/shard_map/pallas_call | solution.py:246
  35.7 0.0 collective-permute-done.9.refs_2_
  35.7 3.7 %shard_map.67 = (f32[8,2,64,2048]{3,2,1,0:T(8,128)}, f32[8,2,8,512]{3,2,1,0:T(8,128)S(1)}) custom-call(s32[2]{0:T(128)S(1)} %pad_add_fusion.1.where_ref, f32[8,2,8,512]{3,2,1,0:T(8,128)S(1)} %slice_add_fusion.own_ref.refs_0_, f32[8,2,8,512]{3,2,1,0:T(8,128)S(1)} %shard_map.66.refs_1_, f32[8,2,8,512]{3,2,1,0:T(8,128)S(1)} %collective-permute-done.9.refs_2_, ...), custom_call_target="tpu_custom_call" | custom-call | flops 1 | bytes 1 | tf_op jit(solution)/shard_map/pallas_call | solution.py:339
  39.4 0.0 collective-permute-done.5.across_ref
  39.4 0.1 collective-permute-start.10
  39.5 0.1 pad_add_fusion.where_ref
  39.6 1.2 %shard_map.68.refs_2_ = f32[8,2,8,512]{3,2,1,0:T(8,128)S(1)} custom-call(f32[8,2,8,512]{3,2,1,0:T(8,128)S(1)} %slice_add_fusion.1.own_ref.refs_1_, f32[8,2,8,512]{3,2,1,0:T(8,128)S(1)} %collective-permute-done.8.beside_ref, f32[8,2,8,512]{3,2,1,0:T(8,128)S(1)} %collective-permute-done.5.across_ref, f32[2,8,512]{2,1,0:T(8,128)S(1)} %add_bitcast_fusion.seen_ref), custom_call_target="tpu_custom_call" | custom-call | flops 1 | bytes 1 | tf_op jit(solution)/shard_map/pallas_call | solution.py:246
  40.8 0.2 collective-permute-done.10.refs_3_
  41.0 3.5 %shard_map.69 = f32[8,2,64,2048]{3,2,1,0:T(8,128)} custom-call(s32[2]{0:T(128)S(1)} %pad_add_fusion.where_ref, f32[8,2,64,2048]{3,2,1,0:T(8,128)} %get-tuple-element.31.refs_0_, f32[8,2,8,512]{3,2,1,0:T(8,128)S(1)} %slice_add_fusion.1.own_ref.refs_1_, f32[8,2,8,512]{3,2,1,0:T(8,128)S(1)} %shard_map.68.refs_2_, ...), custom_call_target="tpu_custom_call", output_to_operand_aliasing={{}: (1, {})} | custom-call | flops 1 | bytes 1 | tf_op jit(solution)/shard_map/pallas_call | solution.py:339
  (11 shorter events, 0.1 us)
Async XLA Ops:
  0.0 35.7 %copy-start = (bf16[4,256,256]{2,1,0:T(8,128)(2,1)S(1)}, bf16[4,256,256]{2,1,0:T(8,128)(2,1)}, u32[]{:S(2)}) copy-start(bf16[4,256,256]{2,1,0:T(8,128)(2,1)} %constant.25.clone.refs_7_.refs_6_) | copy-start | bytes 1572868
  0.0 35.7 %copy-start.1 = (bf16[128,192]{1,0:T(8,128)(2,1)S(1)}, bf16[128,192]{1,0:T(8,128)(2,1)}, u32[]{:S(2)}) copy-start(bf16[128,192]{1,0:T(8,128)(2,1)} %constant.24.clone.refs_6_.refs_5_) | copy-start | bytes 147460
  0.0 0.9 %copy-start.2 = (f32[2,16,512]{2,1,0:T(8,128)S(1)}, f32[2,16,512]{2,1,0:T(8,128)}, u32[]{:S(2)}) copy-start(f32[2,16,512]{2,1,0:T(8,128)} %seen_hbm.1) | copy-start | bytes 196612
  7.0 8.3 %collective-permute-start.3 = (f32[9,2,8,512]{3,2,1,0:T(8,128)S(1)}, f32[9,2,8,512]{3,2,1,0:T(8,128)S(1)}, u32[]{:S(2)}, u32[]{:S(2)}) collective-permute-start(f32[9,2,8,512]{3,2,1,0:T(8,128)S(1)} %get-tuple-element.22), channel_id=1, source_target_pairs={{0,1},{2,3},{4,5},{6,7},{8,9},{10,11},{12,13},{14,15},{16,17},{18,... | collective-permute-start | bytes 884744 | tf_op jit(solution)/shard_map/ppermute | solution.py:376
  8.7 8.4 %collective-permute-start.2 = (f32[8,2,8,512]{3,2,1,0:T(8,128)S(1)}, f32[8,2,8,512]{3,2,1,0:T(8,128)S(1)}, u32[]{:S(2)}, u32[]{:S(2)}) collective-permute-start(f32[8,2,8,512]{3,2,1,0:T(8,128)S(1)} %get-tuple-element.21.own_ref.refs_3_), channel_id=1, source_target_pairs={{0,64},{32,96},{64,0},{96,32},{1,65},{33,97},{65,1},{97,33},{2,66}... | collective-permute-start | bytes 786440 | tf_op jit(solution)/shard_map/ppermute | solution.py:358
  9.7 10.3 %collective-permute-start.1 = (f32[8,2,8,512]{3,2,1,0:T(8,128)S(1)}, f32[8,2,8,512]{3,2,1,0:T(8,128)S(1)}, u32[]{:S(2)}, u32[]{:S(2)}) collective-permute-start(f32[8,2,8,512]{3,2,1,0:T(8,128)S(1)} %get-tuple-element.21.own_ref.refs_3_), channel_id=1, source_target_pairs={{0,32},{32,0},{64,96},{96,64},{1,33},{33,1},{65,97},{97,65},{2,34}... | collective-permute-start | bytes 786440 | tf_op jit(solution)/shard_map/ppermute | solution.py:358
  10.9 12.6 %collective-permute-start = (f32[9,2,8,512]{3,2,1,0:T(8,128)S(1)}, f32[9,2,8,512]{3,2,1,0:T(8,128)S(1)}, u32[]{:S(2)}, u32[]{:S(2)}) collective-permute-start(f32[9,2,8,512]{3,2,1,0:T(8,128)S(1)} %get-tuple-element.20), channel_id=1, source_target_pairs={{1,2},{3,4},{5,6},{7,8},{9,10},{11,12},{13,14},{15,16},{17,18},{19... | collective-permute-start | bytes 884744 | tf_op jit(solution)/shard_map/ppermute | solution.py:375
  15.3 8.2 %copy-start.3 = (f32[9,2,8,512]{3,2,1,0:T(8,128)}, f32[9,2,8,512]{3,2,1,0:T(8,128)S(1)}, u32[]{:S(2)}) copy-start(f32[9,2,8,512]{3,2,1,0:T(8,128)S(1)} %collective-permute-done.3) | copy-start | bytes 884740
  17.1 3.0 %collective-permute-start.4 = (f32[8,2,8,512]{3,2,1,0:T(8,128)S(1)}, f32[8,2,8,512]{3,2,1,0:T(8,128)S(1)}, u32[]{:S(2)}, u32[]{:S(2)}) collective-permute-start(f32[8,2,8,512]{3,2,1,0:T(8,128)S(1)} %collective-permute-done.2.across_ref), channel_id=1, source_target_pairs={{0,32},{32,0},{64,96},{96,64},{1,33},{33,1},{65,97},{97,65},{2,34}... | collective-permute-start | bytes 786440 | tf_op jit(solution)/shard_map/ppermute | solution.py:358
  19.0 14.1 %collective-permute-start.7 = (f32[8,2,8,512]{3,2,1,0:T(8,128)S(1)}, f32[8,2,8,512]{3,2,1,0:T(8,128)S(1)}, u32[]{:S(2)}, u32[]{:S(2)}) collective-permute-start(f32[8,2,8,512]{3,2,1,0:T(8,128)S(1)} %slice_add_fusion.own_ref.refs_0_), channel_id=1, source_target_pairs={{0,64},{32,96},{64,0},{96,32},{1,65},{33,97},{65,1},{97,33},{2,66}... | collective-permute-start | bytes 786440 | tf_op jit(solution)/shard_map/ppermute | solution.py:358
  23.6 9.5 %collective-permute-start.8 = (f32[8,2,8,512]{3,2,1,0:T(8,128)S(1)}, f32[8,2,8,512]{3,2,1,0:T(8,128)S(1)}, u32[]{:S(2)}, u32[]{:S(2)}) collective-permute-start(f32[8,2,8,512]{3,2,1,0:T(8,128)S(1)} %slice_add_fusion.1.own_ref.refs_1_), channel_id=1, source_target_pairs={{0,32},{32,0},{64,96},{96,64},{1,33},{33,1},{65,97},{97,65},{2,34}... | collective-permute-start | bytes 786440 | tf_op jit(solution)/shard_map/ppermute | solution.py:358
  24.5 10.0 %collective-permute-start.6 = (f32[8,2,8,512]{3,2,1,0:T(8,128)S(1)}, f32[8,2,8,512]{3,2,1,0:T(8,128)S(1)}, u32[]{:S(2)}, u32[]{:S(2)}) collective-permute-start(f32[8,2,8,512]{3,2,1,0:T(8,128)S(1)} %slice_add_fusion.own_ref.refs_0_), channel_id=1, source_target_pairs={{0,32},{32,0},{64,96},{96,64},{1,33},{33,1},{65,97},{97,65},{2,34}... | collective-permute-start | bytes 786440 | tf_op jit(solution)/shard_map/ppermute | solution.py:358
  24.6 14.8 %collective-permute-start.5 = (f32[8,2,8,512]{3,2,1,0:T(8,128)S(1)}, f32[8,2,8,512]{3,2,1,0:T(8,128)S(1)}, u32[]{:S(2)}, u32[]{:S(2)}) collective-permute-start(f32[8,2,8,512]{3,2,1,0:T(8,128)S(1)} %slice_add_fusion.1.own_ref.refs_1_), channel_id=1, source_target_pairs={{0,64},{32,96},{64,0},{96,32},{1,65},{33,97},{65,1},{97,33},{2,66}... | collective-permute-start | bytes 786440 | tf_op jit(solution)/shard_map/ppermute | solution.py:358
  33.1 2.6 %collective-permute-start.9 = (f32[8,2,8,512]{3,2,1,0:T(8,128)S(1)}, f32[8,2,8,512]{3,2,1,0:T(8,128)S(1)}, u32[]{:S(2)}, u32[]{:S(2)}) collective-permute-start(f32[8,2,8,512]{3,2,1,0:T(8,128)S(1)} %collective-permute-done.7.across_ref), channel_id=1, source_target_pairs={{0,32},{32,0},{64,96},{96,64},{1,33},{33,1},{65,97},{97,65},{2,34}... | collective-permute-start | bytes 786440 | tf_op jit(solution)/shard_map/ppermute | solution.py:358
  39.4 1.6 %collective-permute-start.10 = (f32[8,2,8,512]{3,2,1,0:T(8,128)S(1)}, f32[8,2,8,512]{3,2,1,0:T(8,128)S(1)}, u32[]{:S(2)}, u32[]{:S(2)}) collective-permute-start(f32[8,2,8,512]{3,2,1,0:T(8,128)S(1)} %collective-permute-done.5.across_ref), channel_id=1, source_target_pairs={{0,32},{32,0},{64,96},{96,64},{1,33},{33,1},{65,97},{97,65},{2,34}... | collective-permute-start | bytes 786440 | tf_op jit(solution)/shard_map/ppermute | solution.py:358

commit v4 on v3

--- a/solution.py
+++ b/solution.py
@@ -19,7 +19,7 @@
 TILE = 8
 HALF = 32
 NEAR = HALF // STRIDE + 2 * MARGIN
-GROUP = 2
+GROUP = 1
 AHEAD = 3
 VMEM = 40 * 1024 * 1024
 WHOLE = 50 * 1024 * 1024
@@ -116,7 +116,7 @@
         lat_ref[place, depth:] = value
 
 
-def thin_rows(value, lon_ref, lat_ref):
+def thin_lon(value, lon_ref):
     variables, rows, length = value.shape
     value = value.reshape(variables * rows, length)
     count = length // BLOCK
@@ -144,10 +144,14 @@
             + jnp.where(lane < MARGIN, before, sums[2 * j + 1])
         )
     high, low = split(jnp.concatenate(columns, axis=1))
-    both = dot(lat_ref[...], jnp.concatenate([high, low], axis=0))
+    return jnp.concatenate([high, low], axis=0)
+
+
+def thin_lat(stack, lat_ref, variables):
+    both = dot(lat_ref[...], stack)
     middle = both.shape[0] // 2
     coarse = both[:middle] + both[middle:]
-    return coarse.reshape(variables, 3, TILE, length // STRIDE)
+    return coarse.reshape(variables, 3, TILE, stack.shape[1])
 
 
 def thin_kernel(bands, where_ref, x_ref, seen_hbm, near_ref, far_ref, mid_ref, held, lon_ref, lat_ref, seen_ref, arrived, seen_here):
@@ -163,17 +167,25 @@
     seen_copy = pltpu.make_async_copy(seen_hbm, seen_ref, seen_here)
     seen_copy.start()
     fill_thin_tables(lon_ref, lat_ref, variables, rows)
-    for m in range(members):
-        copy(m).wait()
-        if m + AHEAD < members:
-            copy(m + AHEAD).start()
-        coarse = thin_rows(held[m], lon_ref, lat_ref)
+    def finish_rows(m, stack):
+        coarse = thin_lat(stack, lat_ref, variables)
         upper, lower = coarse[:, 0], coarse[:, 2]
         upper = jnp.where(outside(upper.shape, 1, band, bands, 0), 0.0, upper)
         lower = jnp.where(outside(lower.shape, 1, band, bands, 1), 0.0, lower)
         near_ref[m] = jnp.where(even, lower, upper)
         far_ref[m] = jnp.where(even, upper, lower)
         mid_ref[m] = coarse[:, 1]
+
+    before = None
+    for m in range(members):
+        copy(m).wait()
+        if m + AHEAD < members:
+            copy(m + AHEAD).start()
+        stack = thin_lon(held[m], lon_ref)
+        if m > 0:
+            finish_rows(m - 1, before)
+        before = stack
+    finish_rows(members - 1, before)
     seen_copy.wait()
     seen = seen_ref[...]
     zero = jnp.zeros((seen.shape[0], MARGIN, seen.shape[2]), jnp.float32)
@@ -261,15 +273,18 @@
     return part_ref[group] - total * (1.0 / (ensemble * (ensemble - 1)))
 
 
-def spread_rows(edge, mid, band, bands, half, lat_ref, lon_ref, store):
+def spread_lat(edge, mid, band, bands, half, lat_ref):
     group, variables, _, columns = edge.shape
     edge = jnp.where(outside(edge.shape, 2, band, bands, half), 0.0, edge)
     upper = jnp.where(half == 0, edge, mid)
     lower = jnp.where(half == 0, mid, edge)
     grad = jnp.stack([upper, lower], axis=2).reshape(group * variables * NEAR, columns)
     high, low = split(grad)
-    tall = dot(lat_ref[...], jnp.concatenate([high, low, high], axis=0))
-    depth = tall.shape[0]
+    return dot(lat_ref[...], jnp.concatenate([high, low, high], axis=0))
+
+
+def spread_lon(tall, lon_ref, store):
+    depth, columns = tall.shape
     tiles = [tall[:, j * LANES : (j + 1) * LANES] for j in range(columns // LANES)]
     lane = lax.broadcasted_iota(jnp.int32, tiles[0].shape, 1)
     zero = jnp.zeros_like(tiles[0])
@@ -287,7 +302,7 @@
         stack = jnp.concatenate(stacks, axis=0)
         wide = dot(stack, lon_ref[2 * odd]) + dot(stack, lon_ref[2 * odd + 1])
         for j in range(count):
-            store(2 * j + odd, wide[j * depth : (j + 1) * depth].reshape(group, variables, HALF, BLOCK))
+            store(2 * j + odd, wide[j * depth : (j + 1) * depth])
 
 
 def spread_kernel(bands, ensemble, first, where_ref, *refs):
@@ -307,20 +322,29 @@
             held.at[group], out_ref.at[group, :, pl.ds(start, HALF), :], sent.at[c]
         )
 
-    chunks = members // GROUP
-    for c in range(chunks):
+    def tall_rows(c):
         group = pl.ds(c * GROUP, GROUP)
-
-        def store(k, value, group=group):
-            held[group, :, :, k * BLOCK : (k + 1) * BLOCK] = value
-
         edge = finish(ensemble, group, *edge_trio)
         if first:
             mid = finish(ensemble, group, *mid_trio)
             mid_ref[group] = mid
         else:
             mid = mid_ref[group]
-        spread_rows(edge, mid, band, bands, half, lat_ref, lon_ref, store)
+        return spread_lat(edge, mid, band, bands, half, lat_ref)
+
+    chunks = members // GROUP
+    after = tall_rows(0)
+    for c in range(chunks):
+        group = pl.ds(c * GROUP, GROUP)
+        tall = after
+
+        def store(k, value, group=group):
+            shape = (GROUP, *held.shape[1:3], BLOCK)
+            held[group, :, :, k * BLOCK : (k + 1) * BLOCK] = value.reshape(shape)
+
+        if c + 1 < chunks:
+            after = tall_rows(c + 1)
+        spread_lon(tall, lon_ref, store)
         copy(c).start()
     for c in range(chunks):
         copy(c).wait()

time: 44.7 us -> 43 us (0.962)
  Pallas kernels: 17 us -> 15.6 us
  other arithmetic: 0.99 us -> 0.24 us
    pallas_call x1, Pallas kernels: 6.1 us -> 5.24 us  [thin(): pl.pallas_call(functools.partial(thin_kernel, bands), in_specs=[pl.BlockS...]
    add x1, other arithmetic: 0.76 us -> 0.01 us  [shards(): near_seen = near_part[members] + near_come[members]]
    pallas_call x2, Pallas kernels: 7.18 us -> 6.59 us  [spread(): pl.pallas_call(functools.partial(spread_kernel, bands, ensemble, first),...]
    unnamed x8 -> x6, local copies, waits for them, and re-layouts: 0.91 us -> 0.9 us
  transfers between devices with their start and end apart: 11 -> 11, of which waited for: 5 -> 5; matrix products, arithmetic and copies ran while one was open for 2% -> 1% of each run, Pallas kernels for 17% -> 17%
where the time goes in v4:
time: 43 us; the launch traced here: 42.8 us
  Pallas kernels  15.6 us (36%)
  starting transfers between devices  15.1 us (35%)
  waiting for transfers between devices  10.9 us (25%)
  local copies, waits for them, and re-layouts  0.91 us (2%)
    ppermute x9, starting transfers between devices, swap(): return lax.ppermute(value, 'member', [(i, i ^ bit) for i in range(devices)])  8.96 us
    ppermute x9, waiting for transfers between devices, swap(): return lax.ppermute(value, 'member', [(i, i ^ bit) for i in range(devices)])  8.73 us
    pallas_call x2, Pallas kernels, spread(): pl.pallas_call(functools.partial(spread_kernel, bands, ensemble, first),...  6.59 us
    pallas_call x1, Pallas kernels, thin(): pl.pallas_call(functools.partial(thin_kernel, bands), in_specs=[pl.BlockS...  5.24 us
    ppermute x1, starting transfers between devices, shards(): far_come = lax.ppermute(far_part, 'band', pairs_of(bands, 1))  4.4 us
    pallas_call x3, Pallas kernels, pair_gradient(): pl.pallas_call(functools.partial(pair_kernel, ensemble), in_specs=[full]...  3.72 us
    ppermute x1, waiting for transfers between devices, shards(): far_come = lax.ppermute(far_part, 'band', pairs_of(bands, 1))  2.2 us
    ppermute x1, starting transfers between devices, shards(): near_come = lax.ppermute(near_part, 'band', pairs_of(bands, 0))  1.71 us
  transfers between devices with their start and end apart: 11, of which 5 were waited for; matrix products, arithmetic and copies ran while one was open for 1% of the time, Pallas kernels for 17%

profile of v4, /device:TPU:31, one launch (start us, length us, event | category | flops | bytes accessed | tf_op | source)
XLA Modules:
  0.0 42.8 jit_solution(1717383357843767057)
XLA Ops:
  0.0 0.9 %copy-done.1 = f32[2,16,512]{2,1,0:T(8,128)S(1)} copy-done((f32[2,16,512]{2,1,0:T(8,128)S(1)}, f32[2,16,512]{2,1,0:T(8,128)}, u32[]{:S(2)}) %copy-start.1) | copy-done | bytes 65560
  0.9 5.2 %shard_map.64 = (f32[9,2,8,512]{3,2,1,0:T(8,128)S(1)}, f32[9,2,8,512]{3,2,1,0:T(8,128)S(1)}, f32[8,2,8,512]{3,2,1,0:T(8,128)S(1)}) custom-call(s32[1]{0:T(128)} %bitcast.where_ref, f32[8,2,64,2048]{3,2,1,0:T(8,128)} %x_ref.1, f32[2,16,512]{2,1,0:T(8,128)S(1)} %copy-done.1), custom_call_target="tpu_custom_call" | custom-call | flops 1 | bytes 1 | tf_op jit(solution)/shard_map/pallas_call | solution.py:205
  6.2 1.7 %collective-permute-start.3 = (f32[9,2,8,512]{3,2,1,0:T(8,128)S(1)}, f32[9,2,8,512]{3,2,1,0:T(8,128)S(1)}, u32[]{:S(2)}, u32[]{:S(2)}) collective-permute-start(f32[9,2,8,512]{3,2,1,0:T(8,128)S(1)} %get-tuple-element.22), channel_id=1, source_target_pairs={{0,1},{2,3},{4,5},{6,7},{8,9},{10,11},{12,13},{14,15},{16,17},{18,... | collective-permute-start | bytes 884744 | tf_op jit(solution)/shard_map/ppermute | solution.py:400
  7.9 1.0 %collective-permute-start.2 = (f32[8,2,8,512]{3,2,1,0:T(8,128)S(1)}, f32[8,2,8,512]{3,2,1,0:T(8,128)S(1)}, u32[]{:S(2)}, u32[]{:S(2)}) collective-permute-start(f32[8,2,8,512]{3,2,1,0:T(8,128)S(1)} %get-tuple-element.21.own_ref.refs_3_), channel_id=1, source_target_pairs={{0,64},{32,96},{64,0},{96,32},{1,65},{33,97},{65,1},{97,33},{2,66}... | collective-permute-start | bytes 786440 | tf_op jit(solution)/shard_map/ppermute | solution.py:382
  8.8 1.2 %collective-permute-start.1 = (f32[8,2,8,512]{3,2,1,0:T(8,128)S(1)}, f32[8,2,8,512]{3,2,1,0:T(8,128)S(1)}, u32[]{:S(2)}, u32[]{:S(2)}) collective-permute-start(f32[8,2,8,512]{3,2,1,0:T(8,128)S(1)} %get-tuple-element.21.own_ref.refs_3_), channel_id=1, source_target_pairs={{0,32},{32,0},{64,96},{96,64},{1,33},{33,1},{65,97},{97,65},{2,34}... | collective-permute-start | bytes 786440 | tf_op jit(solution)/shard_map/ppermute | solution.py:382
  10.1 4.4 %collective-permute-start = (f32[9,2,8,512]{3,2,1,0:T(8,128)S(1)}, f32[9,2,8,512]{3,2,1,0:T(8,128)S(1)}, u32[]{:S(2)}, u32[]{:S(2)}) collective-permute-start(f32[9,2,8,512]{3,2,1,0:T(8,128)S(1)} %get-tuple-element.20), channel_id=1, source_target_pairs={{1,2},{3,4},{5,6},{7,8},{9,10},{11,12},{13,14},{15,16},{17,18},{19... | collective-permute-start | bytes 884744 | tf_op jit(solution)/shard_map/ppermute | solution.py:399
  14.5 0.0 collective-permute-done.3
  14.5 1.7 %collective-permute-done.2.across_ref = f32[8,2,8,512]{3,2,1,0:T(8,128)S(1)} collective-permute-done((f32[8,2,8,512]{3,2,1,0:T(8,128)S(1)}, f32[8,2,8,512]{3,2,1,0:T(8,128)S(1)}, u32[]{:S(2)}, u32[]{:S(2)}) %collective-permute-start.2) | collective-permute-done | bytes 262176 | tf_op jit(solution)/shard_map/ppermute | solution.py:382
  16.2 1.9 %collective-permute-start.4 = (f32[8,2,8,512]{3,2,1,0:T(8,128)S(1)}, f32[8,2,8,512]{3,2,1,0:T(8,128)S(1)}, u32[]{:S(2)}, u32[]{:S(2)}) collective-permute-start(f32[8,2,8,512]{3,2,1,0:T(8,128)S(1)} %collective-permute-done.2.across_ref), channel_id=1, source_target_pairs={{0,32},{32,0},{64,96},{96,64},{1,33},{33,1},{65,97},{97,65},{2,34}... | collective-permute-start | bytes 786440 | tf_op jit(solution)/shard_map/ppermute | solution.py:382
  18.1 1.0 %collective-permute-start.7 = (f32[8,2,8,512]{3,2,1,0:T(8,128)S(1)}, f32[8,2,8,512]{3,2,1,0:T(8,128)S(1)}, u32[]{:S(2)}, u32[]{:S(2)}) collective-permute-start(f32[8,2,8,512]{3,2,1,0:T(8,128)S(1)} %slice_add_fusion.own_ref.refs_0_), channel_id=1, source_target_pairs={{0,64},{32,96},{64,0},{96,32},{1,65},{33,97},{65,1},{97,33},{2,66}... | collective-permute-start | bytes 786440 | tf_op jit(solution)/shard_map/ppermute | solution.py:382
  19.1 0.0 collective-permute-done.1.beside_ref
  19.1 0.2 collective-permute-done.4.refs_5_
  19.3 1.2 %shard_map.65.refs_4_ = f32[8,2,8,512]{3,2,1,0:T(8,128)S(1)} custom-call(f32[8,2,8,512]{3,2,1,0:T(8,128)S(1)} %get-tuple-element.21.own_ref.refs_3_, f32[8,2,8,512]{3,2,1,0:T(8,128)S(1)} %collective-permute-done.1.beside_ref, f32[8,2,8,512]{3,2,1,0:T(8,128)S(1)} %collective-permute-done.2.across_ref, f32[2,8,512]{2,1,0:T(8,128)S(1)} %slice.30.seen_ref), custom_call_target="tpu_custom_call" | custom-call | flops 1 | bytes 1 | tf_op jit(solution)/shard_map/pallas_call | solution.py:258
  20.5 2.2 %collective-permute-done = f32[9,2,8,512]{3,2,1,0:T(8,128)S(1)} collective-permute-done((f32[9,2,8,512]{3,2,1,0:T(8,128)S(1)}, f32[9,2,8,512]{3,2,1,0:T(8,128)S(1)}, u32[]{:S(2)}, u32[]{:S(2)}) %collective-permute-start) | collective-permute-done | bytes 294944 | tf_op jit(solution)/shard_map/ppermute | solution.py:399
  22.7 0.9 %collective-permute-start.8 = (f32[8,2,8,512]{3,2,1,0:T(8,128)S(1)}, f32[8,2,8,512]{3,2,1,0:T(8,128)S(1)}, u32[]{:S(2)}, u32[]{:S(2)}) collective-permute-start(f32[8,2,8,512]{3,2,1,0:T(8,128)S(1)} %slice_add_fusion.1.own_ref.refs_1_), channel_id=1, source_target_pairs={{0,32},{32,0},{64,96},{96,64},{1,33},{33,1},{65,97},{97,65},{2,34}... | collective-permute-start | bytes 786440 | tf_op jit(solution)/shard_map/ppermute | solution.py:382
  23.6 0.1 collective-permute-start.6
  23.7 2.0 %collective-permute-start.5 = (f32[8,2,8,512]{3,2,1,0:T(8,128)S(1)}, f32[8,2,8,512]{3,2,1,0:T(8,128)S(1)}, u32[]{:S(2)}, u32[]{:S(2)}) collective-permute-start(f32[8,2,8,512]{3,2,1,0:T(8,128)S(1)} %slice_add_fusion.1.own_ref.refs_1_), channel_id=1, source_target_pairs={{0,64},{32,96},{64,0},{96,32},{1,65},{33,97},{65,1},{97,33},{2,66}... | collective-permute-start | bytes 786440 | tf_op jit(solution)/shard_map/ppermute | solution.py:382
  25.7 6.5 %collective-permute-done.7.across_ref = f32[8,2,8,512]{3,2,1,0:T(8,128)S(1)} collective-permute-done((f32[8,2,8,512]{3,2,1,0:T(8,128)S(1)}, f32[8,2,8,512]{3,2,1,0:T(8,128)S(1)}, u32[]{:S(2)}, u32[]{:S(2)}) %collective-permute-start.7) | collective-permute-done | bytes 262176 | tf_op jit(solution)/shard_map/ppermute | solution.py:382
  32.2 0.0 collective-permute-done.8.beside_ref
  32.2 0.5 %collective-permute-start.9 = (f32[8,2,8,512]{3,2,1,0:T(8,128)S(1)}, f32[8,2,8,512]{3,2,1,0:T(8,128)S(1)}, u32[]{:S(2)}, u32[]{:S(2)}) collective-permute-start(f32[8,2,8,512]{3,2,1,0:T(8,128)S(1)} %collective-permute-done.7.across_ref), channel_id=1, source_target_pairs={{0,32},{32,0},{64,96},{96,64},{1,33},{33,1},{65,97},{97,65},{2,34}... | collective-permute-start | bytes 786440 | tf_op jit(solution)/shard_map/ppermute | solution.py:382
  32.7 0.1 pad_add_fusion.1.where_ref
  32.8 0.0 collective-permute-done.6.beside_ref
  32.8 1.3 %shard_map.66.refs_1_ = f32[8,2,8,512]{3,2,1,0:T(8,128)S(1)} custom-call(f32[8,2,8,512]{3,2,1,0:T(8,128)S(1)} %slice_add_fusion.own_ref.refs_0_, f32[8,2,8,512]{3,2,1,0:T(8,128)S(1)} %collective-permute-done.6.beside_ref, f32[8,2,8,512]{3,2,1,0:T(8,128)S(1)} %collective-permute-done.7.across_ref, f32[2,8,512]{2,1,0:T(8,128)S(1)} %fusion.seen_ref), custom_call_target="tpu_custom_call" | custom-call | flops 1 | bytes 1 | tf_op jit(solution)/shard_map/pallas_call | solution.py:258
  34.1 0.0 collective-permute-done.9.refs_2_
  34.1 0.0 copy-done
  34.1 3.4 %shard_map.67 = (f32[8,2,64,2048]{3,2,1,0:T(8,128)}, f32[8,2,8,512]{3,2,1,0:T(8,128)S(1)}) custom-call(s32[2]{0:T(128)S(1)} %pad_add_fusion.1.where_ref, f32[8,2,8,512]{3,2,1,0:T(8,128)S(1)} %slice_add_fusion.own_ref.refs_0_, f32[8,2,8,512]{3,2,1,0:T(8,128)S(1)} %shard_map.66.refs_1_, f32[8,2,8,512]{3,2,1,0:T(8,128)S(1)} %collective-permute-done.9.refs_2_, ...), custom_call_target="tpu_custom_call" | custom-call | flops 1 | bytes 1 | tf_op jit(solution)/shard_map/pallas_call | solution.py:363
  37.5 0.4 collective-permute-done.5.across_ref
  37.8 0.4 %collective-permute-start.10 = (f32[8,2,8,512]{3,2,1,0:T(8,128)S(1)}, f32[8,2,8,512]{3,2,1,0:T(8,128)S(1)}, u32[]{:S(2)}, u32[]{:S(2)}) collective-permute-start(f32[8,2,8,512]{3,2,1,0:T(8,128)S(1)} %collective-permute-done.5.across_ref), channel_id=1, source_target_pairs={{0,32},{32,0},{64,96},{96,64},{1,33},{33,1},{65,97},{97,65},{2,34}... | collective-permute-start | bytes 786440 | tf_op jit(solution)/shard_map/ppermute | solution.py:382
  38.3 0.1 pad_add_fusion.where_ref
  38.4 1.2 %shard_map.68.refs_2_ = f32[8,2,8,512]{3,2,1,0:T(8,128)S(1)} custom-call(f32[8,2,8,512]{3,2,1,0:T(8,128)S(1)} %slice_add_fusion.1.own_ref.refs_1_, f32[8,2,8,512]{3,2,1,0:T(8,128)S(1)} %collective-permute-done.8.beside_ref, f32[8,2,8,512]{3,2,1,0:T(8,128)S(1)} %collective-permute-done.5.across_ref, f32[2,8,512]{2,1,0:T(8,128)S(1)} %add_bitcast_fusion.seen_ref), custom_call_target="tpu_custom_call" | custom-call | flops 1 | bytes 1 | tf_op jit(solution)/shard_map/pallas_call | solution.py:258
  39.6 0.0 collective-permute-done.10.refs_3_
  39.6 3.2 %shard_map.69 = f32[8,2,64,2048]{3,2,1,0:T(8,128)} custom-call(s32[2]{0:T(128)S(1)} %pad_add_fusion.where_ref, f32[8,2,64,2048]{3,2,1,0:T(8,128)} %get-tuple-element.31.refs_0_, f32[8,2,8,512]{3,2,1,0:T(8,128)S(1)} %slice_add_fusion.1.own_ref.refs_1_, f32[8,2,8,512]{3,2,1,0:T(8,128)S(1)} %shard_map.68.refs_2_, ...), custom_call_target="tpu_custom_call", output_to_operand_aliasing={{}: (1, {})} | custom-call | flops 1 | bytes 1 | tf_op jit(solution)/shard_map/pallas_call | solution.py:363
  (9 shorter events, 0.1 us)
Async XLA Ops:
  0.0 34.1 %copy-start = (bf16[4,256,256]{2,1,0:T(8,128)(2,1)S(1)}, bf16[4,256,256]{2,1,0:T(8,128)(2,1)}, u32[]{:S(2)}) copy-start(bf16[4,256,256]{2,1,0:T(8,128)(2,1)} %constant.25.clone.refs_7_.refs_6_) | copy-start | bytes 1572868
  0.0 0.9 %copy-start.1 = (f32[2,16,512]{2,1,0:T(8,128)S(1)}, f32[2,16,512]{2,1,0:T(8,128)}, u32[]{:S(2)}) copy-start(f32[2,16,512]{2,1,0:T(8,128)} %seen_hbm.1) | copy-start | bytes 196612
  0.9 33.2 %copy-start.2 = (bf16[64,96]{1,0:T(8,128)(2,1)S(1)}, bf16[64,96]{1,0:T(8,128)(2,1)}, u32[]{:S(2)}) copy-start(bf16[64,96]{1,0:T(8,128)(2,1)} %constant.24.clone.refs_6_.refs_5_) | copy-start | bytes 36868
  6.2 8.3 %collective-permute-start.3 = (f32[9,2,8,512]{3,2,1,0:T(8,128)S(1)}, f32[9,2,8,512]{3,2,1,0:T(8,128)S(1)}, u32[]{:S(2)}, u32[]{:S(2)}) collective-permute-start(f32[9,2,8,512]{3,2,1,0:T(8,128)S(1)} %get-tuple-element.22), channel_id=1, source_target_pairs={{0,1},{2,3},{4,5},{6,7},{8,9},{10,11},{12,13},{14,15},{16,17},{18,... | collective-permute-start | bytes 884744 | tf_op jit(solution)/shard_map/ppermute | solution.py:400
  7.9 8.3 %collective-permute-start.2 = (f32[8,2,8,512]{3,2,1,0:T(8,128)S(1)}, f32[8,2,8,512]{3,2,1,0:T(8,128)S(1)}, u32[]{:S(2)}, u32[]{:S(2)}) collective-permute-start(f32[8,2,8,512]{3,2,1,0:T(8,128)S(1)} %get-tuple-element.21.own_ref.refs_3_), channel_id=1, source_target_pairs={{0,64},{32,96},{64,0},{96,32},{1,65},{33,97},{65,1},{97,33},{2,66}... | collective-permute-start | bytes 786440 | tf_op jit(solution)/shard_map/ppermute | solution.py:382
  8.8 10.3 %collective-permute-start.1 = (f32[8,2,8,512]{3,2,1,0:T(8,128)S(1)}, f32[8,2,8,512]{3,2,1,0:T(8,128)S(1)}, u32[]{:S(2)}, u32[]{:S(2)}) collective-permute-start(f32[8,2,8,512]{3,2,1,0:T(8,128)S(1)} %get-tuple-element.21.own_ref.refs_3_), channel_id=1, source_target_pairs={{0,32},{32,0},{64,96},{96,64},{1,33},{33,1},{65,97},{97,65},{2,34}... | collective-permute-start | bytes 786440 | tf_op jit(solution)/shard_map/ppermute | solution.py:382
  10.1 12.6 %collective-permute-start = (f32[9,2,8,512]{3,2,1,0:T(8,128)S(1)}, f32[9,2,8,512]{3,2,1,0:T(8,128)S(1)}, u32[]{:S(2)}, u32[]{:S(2)}) collective-permute-start(f32[9,2,8,512]{3,2,1,0:T(8,128)S(1)} %get-tuple-element.20), channel_id=1, source_target_pairs={{1,2},{3,4},{5,6},{7,8},{9,10},{11,12},{13,14},{15,16},{17,18},{19... | collective-permute-start | bytes 884744 | tf_op jit(solution)/shard_map/ppermute | solution.py:399
  16.2 3.0 %collective-permute-start.4 = (f32[8,2,8,512]{3,2,1,0:T(8,128)S(1)}, f32[8,2,8,512]{3,2,1,0:T(8,128)S(1)}, u32[]{:S(2)}, u32[]{:S(2)}) collective-permute-start(f32[8,2,8,512]{3,2,1,0:T(8,128)S(1)} %collective-permute-done.2.across_ref), channel_id=1, source_target_pairs={{0,32},{32,0},{64,96},{96,64},{1,33},{33,1},{65,97},{97,65},{2,34}... | collective-permute-start | bytes 786440 | tf_op jit(solution)/shard_map/ppermute | solution.py:382
  18.1 14.1 %collective-permute-start.7 = (f32[8,2,8,512]{3,2,1,0:T(8,128)S(1)}, f32[8,2,8,512]{3,2,1,0:T(8,128)S(1)}, u32[]{:S(2)}, u32[]{:S(2)}) collective-permute-start(f32[8,2,8,512]{3,2,1,0:T(8,128)S(1)} %slice_add_fusion.own_ref.refs_0_), channel_id=1, source_target_pairs={{0,64},{32,96},{64,0},{96,32},{1,65},{33,97},{65,1},{97,33},{2,66}... | collective-permute-start | bytes 786440 | tf_op jit(solution)/shard_map/ppermute | solution.py:382
  22.7 9.5 %collective-permute-start.8 = (f32[8,2,8,512]{3,2,1,0:T(8,128)S(1)}, f32[8,2,8,512]{3,2,1,0:T(8,128)S(1)}, u32[]{:S(2)}, u32[]{:S(2)}) collective-permute-start(f32[8,2,8,512]{3,2,1,0:T(8,128)S(1)} %slice_add_fusion.1.own_ref.refs_1_), channel_id=1, source_target_pairs={{0,32},{32,0},{64,96},{96,64},{1,33},{33,1},{65,97},{97,65},{2,34}... | collective-permute-start | bytes 786440 | tf_op jit(solution)/shard_map/ppermute | solution.py:382
  23.6 9.2 %collective-permute-start.6 = (f32[8,2,8,512]{3,2,1,0:T(8,128)S(1)}, f32[8,2,8,512]{3,2,1,0:T(8,128)S(1)}, u32[]{:S(2)}, u32[]{:S(2)}) collective-permute-start(f32[8,2,8,512]{3,2,1,0:T(8,128)S(1)} %slice_add_fusion.own_ref.refs_0_), channel_id=1, source_target_pairs={{0,32},{32,0},{64,96},{96,64},{1,33},{33,1},{65,97},{97,65},{2,34}... | collective-permute-start | bytes 786440 | tf_op jit(solution)/shard_map/ppermute | solution.py:382
  23.7 14.1 %collective-permute-start.5 = (f32[8,2,8,512]{3,2,1,0:T(8,128)S(1)}, f32[8,2,8,512]{3,2,1,0:T(8,128)S(1)}, u32[]{:S(2)}, u32[]{:S(2)}) collective-permute-start(f32[8,2,8,512]{3,2,1,0:T(8,128)S(1)} %slice_add_fusion.1.own_ref.refs_1_), channel_id=1, source_target_pairs={{0,64},{32,96},{64,0},{96,32},{1,65},{33,97},{65,1},{97,33},{2,66}... | collective-permute-start | bytes 786440 | tf_op jit(solution)/shard_map/ppermute | solution.py:382
  32.2 1.8 %collective-permute-start.9 = (f32[8,2,8,512]{3,2,1,0:T(8,128)S(1)}, f32[8,2,8,512]{3,2,1,0:T(8,128)S(1)}, u32[]{:S(2)}, u32[]{:S(2)}) collective-permute-start(f32[8,2,8,512]{3,2,1,0:T(8,128)S(1)} %collective-permute-done.7.across_ref), channel_id=1, source_target_pairs={{0,32},{32,0},{64,96},{96,64},{1,33},{33,1},{65,97},{97,65},{2,34}... | collective-permute-start | bytes 786440 | tf_op jit(solution)/shard_map/ppermute | solution.py:382
  37.8 1.8 %collective-permute-start.10 = (f32[8,2,8,512]{3,2,1,0:T(8,128)S(1)}, f32[8,2,8,512]{3,2,1,0:T(8,128)S(1)}, u32[]{:S(2)}, u32[]{:S(2)}) collective-permute-start(f32[8,2,8,512]{3,2,1,0:T(8,128)S(1)} %collective-permute-done.5.across_ref), channel_id=1, source_target_pairs={{0,32},{32,0},{64,96},{96,64},{1,33},{33,1},{65,97},{97,65},{2,34}... | collective-permute-start | bytes 786440 | tf_op jit(solution)/shard_map/ppermute | solution.py:382

commit v5 on v4

--- a/solution.py
+++ b/solution.py
@@ -253,7 +253,7 @@
     lax.fori_loop(0, variables * tiles, step, 0)
 
 
-def pair_gradient(own, beside, across, seen, ensemble):
+def pair_gradient(own, beside, across, seen, ensemble, moved=1):
     full = pl.BlockSpec(memory_space=pltpu.VMEM)
     return pl.pallas_call(
         functools.partial(pair_kernel, ensemble),
@@ -261,7 +261,7 @@
         out_specs=full,
         out_shape=jax.ShapeDtypeStruct(own.shape, jnp.float32),
         compiler_params=pltpu.CompilerParams(vmem_limit_bytes=VMEM),
-        cost_estimate=pl.CostEstimate(flops=1, bytes_accessed=1, transcendentals=0),
+        cost_estimate=pl.CostEstimate(flops=1, bytes_accessed=moved, transcendentals=0),
     )(own, beside, across, seen)
 
 
@@ -350,7 +350,7 @@
         copy(c).wait()
 
 
-def spread(edge, mid, where, bands, shape, ensemble, out=None):
+def spread(edge, mid, where, bands, shape, ensemble, moved, out=None):
     members, variables, _, length = shape
     lat = spread_lat_table(GROUP * variables, 64.0 * ensemble)
     lon = spread_lon_table()
@@ -373,7 +373,7 @@
         ],
         input_output_aliases={} if first else {1: 0},
         compiler_params=pltpu.CompilerParams(vmem_limit_bytes=VMEM),
-        cost_estimate=pl.CostEstimate(flops=1, bytes_accessed=1, transcendentals=0),
+        cost_estimate=pl.CostEstimate(flops=1, bytes_accessed=moved, transcendentals=0),
     )(where, *operands, jnp.asarray(lat), jnp.asarray(lon))
 
 
@@ -395,34 +395,51 @@
     far = jnp.stack([band, band % 2])
     near = jnp.stack([band, 1 - band % 2])
     tie = lax.optimization_barrier
-    near_part, far_part, mid = thin(fields, observed, band.reshape(1), bands)
-    far_come = lax.ppermute(far_part, "band", pairs_of(bands, 1))
-    near_come = lax.ppermute(near_part, "band", pairs_of(bands, 0))
-    across_mid = swap(mid, 2)
-    beside_mid = swap(mid, 1)
+    with jax.named_scope("k_thin"):
+        near_part, far_part, mid = thin(fields, observed, band.reshape(1), bands)
+    with jax.named_scope("x_near"):
+        near_come = lax.ppermute(near_part, "band", pairs_of(bands, 0))
+    with jax.named_scope("x_ymid"):
+        across_mid = swap(mid, 2)
+    with jax.named_scope("x_cmid"):
+        beside_mid = swap(mid, 1)
+    with jax.named_scope("x_far"):
+        far_come = lax.ppermute(far_part, "band", pairs_of(bands, 1))
     near_tile = near_part[:members] + near_come[:members]
     near_seen = near_part[members] + near_come[members]
-    across_near = swap(near_tile, 2)
-    beside_near = swap(near_tile, 1)
+    with jax.named_scope("x_ynear"):
+        across_near = swap(near_tile, 2)
+    with jax.named_scope("x_cnear"):
+        beside_near = swap(near_tile, 1)
     across_mid, near_tile = tie((across_mid, near_tile))
-    corner_mid = swap(across_mid, 1)
+    with jax.named_scope("x_dmid"):
+        corner_mid = swap(across_mid, 1)
     beside_mid, corner_mid = tie((beside_mid, corner_mid))
-    mid_part = pair_gradient(mid, beside_mid, across_mid, observed[:, MARGIN:-MARGIN], ensemble)
-    far_come, mid_part = tie((far_come, mid_part))
+    far_come, beside_near = tie((far_come, beside_near))
     far_tile = far_part[:members] + far_come[:members]
     far_seen = far_part[members] + far_come[members]
-    across_far = swap(far_tile, 2)
-    beside_far = swap(far_tile, 1)
-    across_near, beside_far = tie((across_near, beside_far))
-    corner_near = swap(across_near, 1)
-    near_grad = pair_gradient(near_tile, beside_near, across_near, near_seen, ensemble)
-    out, mid_grad = spread(
-        (near_tile, near_grad, corner_near), (mid, mid_part, corner_mid), near, bands, fields.shape, ensemble
-    )
+    with jax.named_scope("x_yfar"):
+        across_far = swap(far_tile, 2)
+    with jax.named_scope("x_cfar"):
+        beside_far = swap(far_tile, 1)
+    with jax.named_scope("k_pmid"):
+        mid_part = pair_gradient(mid, beside_mid, across_mid, observed[:, MARGIN:-MARGIN], ensemble, 1)
+    with jax.named_scope("x_dnear"):
+        corner_near = swap(across_near, 1)
+    with jax.named_scope("k_pnear"):
+        near_grad = pair_gradient(near_tile, beside_near, across_near, near_seen, ensemble, 1)
+    trio = (near_tile, near_grad, corner_near)
+    with jax.named_scope("k_near"):
+        out, mid_grad = spread(trio, (mid, mid_part, corner_mid), near, bands, fields.shape, ensemble, 8000000)
     across_far, out = tie((across_far, out))
-    corner_far = swap(across_far, 1)
-    far_grad = pair_gradient(far_tile, beside_far, across_far, far_seen, ensemble)
-    return spread((far_tile, far_grad, corner_far), mid_grad, far, bands, fields.shape, ensemble, out)
+    with jax.named_scope("x_dfar"):
+        corner_far = swap(across_far, 1)
+    with jax.named_scope("k_pfar"):
+        far_grad = pair_gradient(far_tile, beside_far, across_far, far_seen, ensemble, 1)
+    trio = (far_tile, far_grad, corner_far)
+    with jax.named_scope("k_far"):
+        out = spread(trio, mid_grad, far, bands, fields.shape, ensemble, 1, out)
+    return out
 
 
 def solution(mesh):

time: 43 us -> 42.9 us (level)
  waiting for transfers between devices: 10.9 us -> 8.73 us
  starting transfers between devices: 15.1 us -> 17.2 us
    ppermute x9, waiting for transfers between devices: 8.73 us -> 5.51 us  [swap(): return lax.ppermute(value, 'member', [(i, i ^ bit) for i in range(devices)])]
    ppermute x9, starting transfers between devices: 8.96 us -> 11.1 us  [swap(): return lax.ppermute(value, 'member', [(i, i ^ bit) for i in range(devices)])]
    ppermute x1, waiting for transfers between devices: 0.01 us -> 1.23 us  [shards(): near_come = lax.ppermute(near_part, 'band', pairs_of(bands, 0))]
    unnamed x6 -> x8, local copies, waits for them, and re-layouts: 0.9 us -> 0.91 us
  transfers between devices with their start and end apart: 11 -> 11, of which waited for: 5 -> 3; matrix products, arithmetic and copies ran while one was open for 1% -> 1% of each run, Pallas kernels for 17% -> 17%
where the time goes in v5:
time: 42.9 us; the launch traced here: 42.8 us
  starting transfers between devices  17.2 us (40%)
  Pallas kernels  15.6 us (36%)
  waiting for transfers between devices  8.73 us (20%)
  local copies, waits for them, and re-layouts  0.92 us (2%)
    ppermute x9, starting transfers between devices, swap(): return lax.ppermute(value, 'member', [(i, i ^ bit) for i in range(devices)])  11.1 us
    pallas_call x2, Pallas kernels, spread(): pl.pallas_call(functools.partial(spread_kernel, bands, ensemble, first),...  6.56 us
    ppermute x9, waiting for transfers between devices, swap(): return lax.ppermute(value, 'member', [(i, i ^ bit) for i in range(devices)])  5.51 us
    pallas_call x1, Pallas kernels, thin(): pl.pallas_call(functools.partial(thin_kernel, bands), in_specs=[pl.BlockS...  5.26 us
    ppermute x1, starting transfers between devices, shards(): far_come = lax.ppermute(far_part, 'band', pairs_of(bands, 1))  4.4 us
    pallas_call x3, Pallas kernels, pair_gradient(): pl.pallas_call(functools.partial(pair_kernel, ensemble), in_specs=[full]...  3.75 us
    ppermute x1, waiting for transfers between devices, shards(): far_come = lax.ppermute(far_part, 'band', pairs_of(bands, 1))  1.99 us
    ppermute x1, starting transfers between devices, shards(): near_come = lax.ppermute(near_part, 'band', pairs_of(bands, 0))  1.72 us
  transfers between devices with their start and end apart: 11, of which 3 were waited for; matrix products, arithmetic and copies ran while one was open for 1% of the time, Pallas kernels for 17%

profile of v5, /device:TPU:31, one launch (start us, length us, event | category | flops | bytes accessed | tf_op | source)
XLA Modules:
  0.0 42.8 jit_solution(13689220454804624974)
XLA Ops:
  0.0 0.9 %copy-done.1 = f32[2,16,512]{2,1,0:T(8,128)S(1)} copy-done((f32[2,16,512]{2,1,0:T(8,128)S(1)}, f32[2,16,512]{2,1,0:T(8,128)}, u32[]{:S(2)}) %copy-start.1) | copy-done | bytes 65560
  0.9 5.3 %k_thin.1 = (f32[9,2,8,512]{3,2,1,0:T(8,128)S(1)}, f32[9,2,8,512]{3,2,1,0:T(8,128)S(1)}, f32[8,2,8,512]{3,2,1,0:T(8,128)S(1)}) custom-call(s32[1]{0:T(128)} %bitcast.where_ref, f32[8,2,64,2048]{3,2,1,0:T(8,128)} %x_ref.1, f32[2,16,512]{2,1,0:T(8,128)S(1)} %copy-done.1), custom_call_target="tpu_custom_call" | custom-call | flops 1 | bytes 1 | tf_op jit(solution)/shard_map/k_thin/pallas_call | solution.py:205
  6.2 1.7 %collective-permute-start.1 = (f32[9,2,8,512]{3,2,1,0:T(8,128)S(1)}, f32[9,2,8,512]{3,2,1,0:T(8,128)S(1)}, u32[]{:S(2)}, u32[]{:S(2)}) collective-permute-start(f32[9,2,8,512]{3,2,1,0:T(8,128)S(1)} %get-tuple-element.19), channel_id=1, source_target_pairs={{0,1},{2,3},{4,5},{6,7},{8,9},{10,11},{12,13},{14,15},{16,17},{18,... | collective-permute-start | bytes 884744 | tf_op jit(solution)/shard_map/x_near/ppermute | solution.py:401
  7.9 1.0 %collective-permute-start.4 = (f32[8,2,8,512]{3,2,1,0:T(8,128)S(1)}, f32[8,2,8,512]{3,2,1,0:T(8,128)S(1)}, u32[]{:S(2)}, u32[]{:S(2)}) collective-permute-start(f32[8,2,8,512]{3,2,1,0:T(8,128)S(1)} %get-tuple-element.21.own_ref.refs_3_), channel_id=1, source_target_pairs={{0,64},{32,96},{64,0},{96,32},{1,65},{33,97},{65,1},{97,33},{2,66}... | collective-permute-start | bytes 786440 | tf_op jit(solution)/shard_map/x_ymid/ppermute | solution.py:382
  8.9 4.4 %collective-permute-start = (f32[9,2,8,512]{3,2,1,0:T(8,128)S(1)}, f32[9,2,8,512]{3,2,1,0:T(8,128)S(1)}, u32[]{:S(2)}, u32[]{:S(2)}) collective-permute-start(f32[9,2,8,512]{3,2,1,0:T(8,128)S(1)} %get-tuple-element.18), channel_id=1, source_target_pairs={{1,2},{3,4},{5,6},{7,8},{9,10},{11,12},{13,14},{15,16},{17,18},{19... | collective-permute-start | bytes 884744 | tf_op jit(solution)/shard_map/x_far/ppermute | solution.py:407
  13.3 1.2 %collective-permute-done.1 = f32[9,2,8,512]{3,2,1,0:T(8,128)S(1)} collective-permute-done((f32[9,2,8,512]{3,2,1,0:T(8,128)S(1)}, f32[9,2,8,512]{3,2,1,0:T(8,128)S(1)}, u32[]{:S(2)}, u32[]{:S(2)}) %collective-permute-start.1) | collective-permute-done | bytes 294944 | tf_op jit(solution)/shard_map/x_near/ppermute | solution.py:401
  14.5 1.4 %collective-permute-start.2 = (f32[8,2,8,512]{3,2,1,0:T(8,128)S(1)}, f32[8,2,8,512]{3,2,1,0:T(8,128)S(1)}, u32[]{:S(2)}, u32[]{:S(2)}) collective-permute-start(f32[8,2,8,512]{3,2,1,0:T(8,128)S(1)} %slice_add_fusion.own_ref.refs_0_), channel_id=1, source_target_pairs={{0,32},{32,0},{64,96},{96,64},{1,33},{33,1},{65,97},{97,65},{2,34}... | collective-permute-start | bytes 786440 | tf_op jit(solution)/shard_map/x_cnear/ppermute | solution.py:382
  16.0 1.0 %collective-permute-start.5 = (f32[8,2,8,512]{3,2,1,0:T(8,128)S(1)}, f32[8,2,8,512]{3,2,1,0:T(8,128)S(1)}, u32[]{:S(2)}, u32[]{:S(2)}) collective-permute-start(f32[8,2,8,512]{3,2,1,0:T(8,128)S(1)} %slice_add_fusion.own_ref.refs_0_), channel_id=1, source_target_pairs={{0,64},{32,96},{64,0},{96,32},{1,65},{33,97},{65,1},{97,33},{2,66}... | collective-permute-start | bytes 786440 | tf_op jit(solution)/shard_map/x_ynear/ppermute | solution.py:382
  17.0 0.4 collective-permute-start.7
  17.3 0.0 collective-permute-done.4.across_ref
  17.3 0.8 %collective-permute-start.8 = (f32[8,2,8,512]{3,2,1,0:T(8,128)S(1)}, f32[8,2,8,512]{3,2,1,0:T(8,128)S(1)}, u32[]{:S(2)}, u32[]{:S(2)}) collective-permute-start(f32[8,2,8,512]{3,2,1,0:T(8,128)S(1)} %collective-permute-done.4.across_ref), channel_id=1, source_target_pairs={{0,32},{32,0},{64,96},{96,64},{1,33},{33,1},{65,97},{97,65},{2,34}... | collective-permute-start | bytes 786440 | tf_op jit(solution)/shard_map/x_dmid/ppermute | solution.py:382
  18.1 2.0 %collective-permute-done = f32[9,2,8,512]{3,2,1,0:T(8,128)S(1)} collective-permute-done((f32[9,2,8,512]{3,2,1,0:T(8,128)S(1)}, f32[9,2,8,512]{3,2,1,0:T(8,128)S(1)}, u32[]{:S(2)}, u32[]{:S(2)}) %collective-permute-start) | collective-permute-done | bytes 294944 | tf_op jit(solution)/shard_map/x_far/ppermute | solution.py:407
  20.1 0.0 collective-permute-done.2.beside_ref
  20.2 5.4 %collective-permute-start.3 = (f32[8,2,8,512]{3,2,1,0:T(8,128)S(1)}, f32[8,2,8,512]{3,2,1,0:T(8,128)S(1)}, u32[]{:S(2)}, u32[]{:S(2)}) collective-permute-start(f32[8,2,8,512]{3,2,1,0:T(8,128)S(1)} %slice_add_fusion.1.own_ref.refs_1_), channel_id=1, source_target_pairs={{0,64},{32,96},{64,0},{96,32},{1,65},{33,97},{65,1},{97,33},{2,66}... | collective-permute-start | bytes 786440 | tf_op jit(solution)/shard_map/x_yfar/ppermute | solution.py:382
  25.5 5.5 %collective-permute-done.5.across_ref = f32[8,2,8,512]{3,2,1,0:T(8,128)S(1)} collective-permute-done((f32[8,2,8,512]{3,2,1,0:T(8,128)S(1)}, f32[8,2,8,512]{3,2,1,0:T(8,128)S(1)}, u32[]{:S(2)}, u32[]{:S(2)}) %collective-permute-start.5) | collective-permute-done | bytes 262176 | tf_op jit(solution)/shard_map/x_ynear/ppermute | solution.py:382
  31.0 0.5 %collective-permute-start.6 = (f32[8,2,8,512]{3,2,1,0:T(8,128)S(1)}, f32[8,2,8,512]{3,2,1,0:T(8,128)S(1)}, u32[]{:S(2)}, u32[]{:S(2)}) collective-permute-start(f32[8,2,8,512]{3,2,1,0:T(8,128)S(1)} %collective-permute-done.5.across_ref), channel_id=1, source_target_pairs={{0,32},{32,0},{64,96},{96,64},{1,33},{33,1},{65,97},{97,65},{2,34}... | collective-permute-start | bytes 786440 | tf_op jit(solution)/shard_map/x_dnear/ppermute | solution.py:382
  31.5 0.1 pad_add_fusion.1.where_ref
  31.6 0.0 copy-done.2
  31.6 0.1 collective-permute-start.9
  31.7 0.0 collective-permute-done.7.beside_ref
  31.7 0.0 collective-permute-done.8.refs_5_
  31.7 1.3 %k_pmid.1.refs_4_ = f32[8,2,8,512]{3,2,1,0:T(8,128)S(1)} custom-call(f32[8,2,8,512]{3,2,1,0:T(8,128)S(1)} %get-tuple-element.21.own_ref.refs_3_, f32[8,2,8,512]{3,2,1,0:T(8,128)S(1)} %collective-permute-done.7.beside_ref, f32[8,2,8,512]{3,2,1,0:T(8,128)S(1)} %collective-permute-done.4.across_ref, f32[2,8,512]{2,1,0:T(8,128)S(1)} %slice.33.seen_ref), custom_call_target="tpu_custom_call" | custom-call | flops 1 | bytes 1 | tf_op jit(solution)/shard_map/k_pmid/pallas_call | solution.py:258
  33.0 1.3 %k_pnear.1.refs_1_ = f32[8,2,8,512]{3,2,1,0:T(8,128)S(1)} custom-call(f32[8,2,8,512]{3,2,1,0:T(8,128)S(1)} %slice_add_fusion.own_ref.refs_0_, f32[8,2,8,512]{3,2,1,0:T(8,128)S(1)} %collective-permute-done.2.beside_ref, f32[8,2,8,512]{3,2,1,0:T(8,128)S(1)} %collective-permute-done.5.across_ref, f32[2,8,512]{2,1,0:T(8,128)S(1)} %fusion.seen_ref), custom_call_target="tpu_custom_call" | custom-call | flops 1 | bytes 1 | tf_op jit(solution)/shard_map/k_pnear/pallas_call | solution.py:258
  34.2 0.0 collective-permute-done.6.refs_2_
  34.3 3.3 %k_near.1 = (f32[8,2,64,2048]{3,2,1,0:T(8,128)}, f32[8,2,8,512]{3,2,1,0:T(8,128)S(1)}) custom-call(s32[2]{0:T(128)S(1)} %pad_add_fusion.1.where_ref, f32[8,2,8,512]{3,2,1,0:T(8,128)S(1)} %slice_add_fusion.own_ref.refs_0_, f32[8,2,8,512]{3,2,1,0:T(8,128)S(1)} %k_pnear.1.refs_1_, f32[8,2,8,512]{3,2,1,0:T(8,128)S(1)} %collective-permute-done.6.refs_2_, ...), custom_call_target="tpu_custom_call" | custom-call | flops 1 | bytes 8000000 | tf_op jit(solution)/shard_map/k_near/pallas_call | solution.py:363
  37.6 0.0 collective-permute-done.3.across_ref
  37.6 0.6 %collective-permute-start.10 = (f32[8,2,8,512]{3,2,1,0:T(8,128)S(1)}, f32[8,2,8,512]{3,2,1,0:T(8,128)S(1)}, u32[]{:S(2)}, u32[]{:S(2)}) collective-permute-start(f32[8,2,8,512]{3,2,1,0:T(8,128)S(1)} %collective-permute-done.3.across_ref), channel_id=1, source_target_pairs={{0,32},{32,0},{64,96},{96,64},{1,33},{33,1},{65,97},{97,65},{2,34}... | collective-permute-start | bytes 786440 | tf_op jit(solution)/shard_map/x_dfar/ppermute | solution.py:382
  38.2 0.1 pad_add_fusion.where_ref
  38.3 0.0 collective-permute-done.9.beside_ref
  38.3 1.3 %k_pfar.1.refs_2_ = f32[8,2,8,512]{3,2,1,0:T(8,128)S(1)} custom-call(f32[8,2,8,512]{3,2,1,0:T(8,128)S(1)} %slice_add_fusion.1.own_ref.refs_1_, f32[8,2,8,512]{3,2,1,0:T(8,128)S(1)} %collective-permute-done.9.beside_ref, f32[8,2,8,512]{3,2,1,0:T(8,128)S(1)} %collective-permute-done.3.across_ref, f32[2,8,512]{2,1,0:T(8,128)S(1)} %add_bitcast_fusion.seen_ref), custom_call_target="tpu_custom_call" | custom-call | flops 1 | bytes 1 | tf_op jit(solution)/shard_map/k_pfar/pallas_call | solution.py:258
  39.5 0.0 collective-permute-done.10.refs_3_
  39.5 3.2 %k_far.1 = f32[8,2,64,2048]{3,2,1,0:T(8,128)} custom-call(s32[2]{0:T(128)S(1)} %pad_add_fusion.where_ref, f32[8,2,64,2048]{3,2,1,0:T(8,128)} %get-tuple-element.28.refs_0_, f32[8,2,8,512]{3,2,1,0:T(8,128)S(1)} %slice_add_fusion.1.own_ref.refs_1_, f32[8,2,8,512]{3,2,1,0:T(8,128)S(1)} %k_pfar.1.refs_2_, ...), custom_call_target="tpu_custom_call", output_to_operand_aliasing={{}: (1, {})} | custom-call | flops 1 | bytes 1 | tf_op jit(solution)/shard_map/k_far/pallas_call | solution.py:363
  (11 shorter events, 0.1 us)
Async XLA Ops:
  0.0 34.3 %copy-start = (bf16[4,256,256]{2,1,0:T(8,128)(2,1)S(1)}, bf16[4,256,256]{2,1,0:T(8,128)(2,1)}, u32[]{:S(2)}) copy-start(bf16[4,256,256]{2,1,0:T(8,128)(2,1)} %constant.25.clone.refs_7_.refs_6_) | copy-start | bytes 1572868
  0.0 0.9 %copy-start.1 = (f32[2,16,512]{2,1,0:T(8,128)S(1)}, f32[2,16,512]{2,1,0:T(8,128)}, u32[]{:S(2)}) copy-start(f32[2,16,512]{2,1,0:T(8,128)} %seen_hbm.1) | copy-start | bytes 196612
  0.9 30.7 %copy-start.2 = (f32[2,16,512]{2,1,0:T(8,128)S(1)}, f32[2,16,512]{2,1,0:T(8,128)}, u32[]{:S(2)}) copy-start(f32[2,16,512]{2,1,0:T(8,128)} %seen_hbm.1) | copy-start | bytes 196612
  0.9 33.4 %copy-start.3 = (bf16[64,96]{1,0:T(8,128)(2,1)S(1)}, bf16[64,96]{1,0:T(8,128)(2,1)}, u32[]{:S(2)}) copy-start(bf16[64,96]{1,0:T(8,128)(2,1)} %constant.24.clone.refs_6_.refs_5_) | copy-start | bytes 36868
  6.2 8.3 %collective-permute-start.1 = (f32[9,2,8,512]{3,2,1,0:T(8,128)S(1)}, f32[9,2,8,512]{3,2,1,0:T(8,128)S(1)}, u32[]{:S(2)}, u32[]{:S(2)}) collective-permute-start(f32[9,2,8,512]{3,2,1,0:T(8,128)S(1)} %get-tuple-element.19), channel_id=1, source_target_pairs={{0,1},{2,3},{4,5},{6,7},{8,9},{10,11},{12,13},{14,15},{16,17},{18,... | collective-permute-start | bytes 884744 | tf_op jit(solution)/shard_map/x_near/ppermute | solution.py:401
  7.9 9.4 %collective-permute-start.4 = (f32[8,2,8,512]{3,2,1,0:T(8,128)S(1)}, f32[8,2,8,512]{3,2,1,0:T(8,128)S(1)}, u32[]{:S(2)}, u32[]{:S(2)}) collective-permute-start(f32[8,2,8,512]{3,2,1,0:T(8,128)S(1)} %get-tuple-element.21.own_ref.refs_3_), channel_id=1, source_target_pairs={{0,64},{32,96},{64,0},{96,32},{1,65},{33,97},{65,1},{97,33},{2,66}... | collective-permute-start | bytes 786440 | tf_op jit(solution)/shard_map/x_ymid/ppermute | solution.py:382
  8.9 11.3 %collective-permute-start = (f32[9,2,8,512]{3,2,1,0:T(8,128)S(1)}, f32[9,2,8,512]{3,2,1,0:T(8,128)S(1)}, u32[]{:S(2)}, u32[]{:S(2)}) collective-permute-start(f32[9,2,8,512]{3,2,1,0:T(8,128)S(1)} %get-tuple-element.18), channel_id=1, source_target_pairs={{1,2},{3,4},{5,6},{7,8},{9,10},{11,12},{13,14},{15,16},{17,18},{19... | collective-permute-start | bytes 884744 | tf_op jit(solution)/shard_map/x_far/ppermute | solution.py:407
  14.5 5.6 %collective-permute-start.2 = (f32[8,2,8,512]{3,2,1,0:T(8,128)S(1)}, f32[8,2,8,512]{3,2,1,0:T(8,128)S(1)}, u32[]{:S(2)}, u32[]{:S(2)}) collective-permute-start(f32[8,2,8,512]{3,2,1,0:T(8,128)S(1)} %slice_add_fusion.own_ref.refs_0_), channel_id=1, source_target_pairs={{0,32},{32,0},{64,96},{96,64},{1,33},{33,1},{65,97},{97,65},{2,34}... | collective-permute-start | bytes 786440 | tf_op jit(solution)/shard_map/x_cnear/ppermute | solution.py:382
  16.0 15.0 %collective-permute-start.5 = (f32[8,2,8,512]{3,2,1,0:T(8,128)S(1)}, f32[8,2,8,512]{3,2,1,0:T(8,128)S(1)}, u32[]{:S(2)}, u32[]{:S(2)}) collective-permute-start(f32[8,2,8,512]{3,2,1,0:T(8,128)S(1)} %slice_add_fusion.own_ref.refs_0_), channel_id=1, source_target_pairs={{0,64},{32,96},{64,0},{96,32},{1,65},{33,97},{65,1},{97,33},{2,66}... | collective-permute-start | bytes 786440 | tf_op jit(solution)/shard_map/x_ynear/ppermute | solution.py:382
  17.0 14.8 %collective-permute-start.7 = (f32[8,2,8,512]{3,2,1,0:T(8,128)S(1)}, f32[8,2,8,512]{3,2,1,0:T(8,128)S(1)}, u32[]{:S(2)}, u32[]{:S(2)}) collective-permute-start(f32[8,2,8,512]{3,2,1,0:T(8,128)S(1)} %get-tuple-element.21.own_ref.refs_3_), channel_id=1, source_target_pairs={{0,32},{32,0},{64,96},{96,64},{1,33},{33,1},{65,97},{97,65},{2,34}... | collective-permute-start | bytes 786440 | tf_op jit(solution)/shard_map/x_cmid/ppermute | solution.py:382
  17.3 14.4 %collective-permute-start.8 = (f32[8,2,8,512]{3,2,1,0:T(8,128)S(1)}, f32[8,2,8,512]{3,2,1,0:T(8,128)S(1)}, u32[]{:S(2)}, u32[]{:S(2)}) collective-permute-start(f32[8,2,8,512]{3,2,1,0:T(8,128)S(1)} %collective-permute-done.4.across_ref), channel_id=1, source_target_pairs={{0,32},{32,0},{64,96},{96,64},{1,33},{33,1},{65,97},{97,65},{2,34}... | collective-permute-start | bytes 786440 | tf_op jit(solution)/shard_map/x_dmid/ppermute | solution.py:382
  20.2 17.5 %collective-permute-start.3 = (f32[8,2,8,512]{3,2,1,0:T(8,128)S(1)}, f32[8,2,8,512]{3,2,1,0:T(8,128)S(1)}, u32[]{:S(2)}, u32[]{:S(2)}) collective-permute-start(f32[8,2,8,512]{3,2,1,0:T(8,128)S(1)} %slice_add_fusion.1.own_ref.refs_1_), channel_id=1, source_target_pairs={{0,64},{32,96},{64,0},{96,32},{1,65},{33,97},{65,1},{97,33},{2,66}... | collective-permute-start | bytes 786440 | tf_op jit(solution)/shard_map/x_yfar/ppermute | solution.py:382
  31.0 3.2 %collective-permute-start.6 = (f32[8,2,8,512]{3,2,1,0:T(8,128)S(1)}, f32[8,2,8,512]{3,2,1,0:T(8,128)S(1)}, u32[]{:S(2)}, u32[]{:S(2)}) collective-permute-start(f32[8,2,8,512]{3,2,1,0:T(8,128)S(1)} %collective-permute-done.5.across_ref), channel_id=1, source_target_pairs={{0,32},{32,0},{64,96},{96,64},{1,33},{33,1},{65,97},{97,65},{2,34}... | collective-permute-start | bytes 786440 | tf_op jit(solution)/shard_map/x_dnear/ppermute | solution.py:382
  31.6 6.7 %collective-permute-start.9 = (f32[8,2,8,512]{3,2,1,0:T(8,128)S(1)}, f32[8,2,8,512]{3,2,1,0:T(8,128)S(1)}, u32[]{:S(2)}, u32[]{:S(2)}) collective-permute-start(f32[8,2,8,512]{3,2,1,0:T(8,128)S(1)} %slice_add_fusion.1.own_ref.refs_1_), channel_id=1, source_target_pairs={{0,32},{32,0},{64,96},{96,64},{1,33},{33,1},{65,97},{97,65},{2,34}... | collective-permute-start | bytes 786440 | tf_op jit(solution)/shard_map/x_cfar/ppermute | solution.py:382
  37.6 1.9 %collective-permute-start.10 = (f32[8,2,8,512]{3,2,1,0:T(8,128)S(1)}, f32[8,2,8,512]{3,2,1,0:T(8,128)S(1)}, u32[]{:S(2)}, u32[]{:S(2)}) collective-permute-start(f32[8,2,8,512]{3,2,1,0:T(8,128)S(1)} %collective-permute-done.3.across_ref), channel_id=1, source_target_pairs={{0,32},{32,0},{64,96},{96,64},{1,33},{33,1},{65,97},{97,65},{2,34}... | collective-permute-start | bytes 786440 | tf_op jit(solution)/shard_map/x_dfar/ppermute | solution.py:382

commit v6 on v5

--- a/solution.py
+++ b/solution.py
@@ -414,7 +414,9 @@
     across_mid, near_tile = tie((across_mid, near_tile))
     with jax.named_scope("x_dmid"):
         corner_mid = swap(across_mid, 1)
-    beside_mid, corner_mid = tie((beside_mid, corner_mid))
+    with jax.named_scope("k_pmid"):
+        mid_part = pair_gradient(mid, beside_mid, across_mid, observed[:, MARGIN:-MARGIN], ensemble, 1)
+    far_come, mid_part = tie((far_come, mid_part))
     far_come, beside_near = tie((far_come, beside_near))
     far_tile = far_part[:members] + far_come[:members]
     far_seen = far_part[members] + far_come[members]
@@ -422,8 +424,6 @@
         across_far = swap(far_tile, 2)
     with jax.named_scope("x_cfar"):
         beside_far = swap(far_tile, 1)
-    with jax.named_scope("k_pmid"):
-        mid_part = pair_gradient(mid, beside_mid, across_mid, observed[:, MARGIN:-MARGIN], ensemble, 1)
     with jax.named_scope("x_dnear"):
         corner_near = swap(across_near, 1)
     with jax.named_scope("k_pnear"):

time: 42.9 us -> 42.9 us (level)
  starting transfers between devices: 17.2 us -> 15.5 us
  waiting for transfers between devices: 8.73 us -> 10.4 us
    ppermute x9, starting transfers between devices: 11.1 us -> 9.33 us  [swap(): return lax.ppermute(value, 'member', [(i, i ^ bit) for i in range(devices)])]
    ppermute x9, waiting for transfers between devices: 5.51 us -> 7.04 us  [swap(): return lax.ppermute(value, 'member', [(i, i ^ bit) for i in range(devices)])]
    ppermute x1, waiting for transfers between devices: 1.99 us -> 3.35 us  [shards(): far_come = lax.ppermute(far_part, 'band', pairs_of(bands, 1))]
    ppermute x1, waiting for transfers between devices: 1.23 us -> 0.01 us  [shards(): near_come = lax.ppermute(near_part, 'band', pairs_of(bands, 0))]
  transfers between devices with their start and end apart: 11 -> 11, of which waited for: 3 -> 2; matrix products, arithmetic and copies ran while one was open for 1% -> 1% of each run, Pallas kernels for 17% -> 17%
where the time goes in v6:
time: 42.9 us; the launch traced here: 42.7 us
  Pallas kernels  15.5 us (36%)
  starting transfers between devices  15.5 us (36%)
  waiting for transfers between devices  10.4 us (24%)
  local copies, waits for them, and re-layouts  0.92 us (2%)
    ppermute x9, starting transfers between devices, swap(): return lax.ppermute(value, 'member', [(i, i ^ bit) for i in range(devices)])  9.33 us
    ppermute x9, waiting for transfers between devices, swap(): return lax.ppermute(value, 'member', [(i, i ^ bit) for i in range(devices)])  7.04 us
    pallas_call x2, Pallas kernels, spread(): pl.pallas_call(functools.partial(spread_kernel, bands, ensemble, first),...  6.55 us
    pallas_call x1, Pallas kernels, thin(): pl.pallas_call(functools.partial(thin_kernel, bands), in_specs=[pl.BlockS...  5.26 us
    ppermute x1, starting transfers between devices, shards(): far_come = lax.ppermute(far_part, 'band', pairs_of(bands, 1))  4.4 us
    pallas_call x3, Pallas kernels, pair_gradient(): pl.pallas_call(functools.partial(pair_kernel, ensemble), in_specs=[full]...  3.74 us
    ppermute x1, waiting for transfers between devices, shards(): far_come = lax.ppermute(far_part, 'band', pairs_of(bands, 1))  3.35 us
    ppermute x1, starting transfers between devices, shards(): near_come = lax.ppermute(near_part, 'band', pairs_of(bands, 0))  1.72 us
  transfers between devices with their start and end apart: 11, of which 2 were waited for; matrix products, arithmetic and copies ran while one was open for 1% of the time, Pallas kernels for 17%

profile of v6, /device:TPU:31, one launch (start us, length us, event | category | flops | bytes accessed | tf_op | source)
XLA Modules:
  0.0 42.7 jit_solution(10088963352588868803)
XLA Ops:
  0.0 0.9 %copy-done.1 = f32[2,16,512]{2,1,0:T(8,128)S(1)} copy-done((f32[2,16,512]{2,1,0:T(8,128)S(1)}, f32[2,16,512]{2,1,0:T(8,128)}, u32[]{:S(2)}) %copy-start.1) | copy-done | bytes 65560
  0.9 5.3 %k_thin.1 = (f32[9,2,8,512]{3,2,1,0:T(8,128)S(1)}, f32[9,2,8,512]{3,2,1,0:T(8,128)S(1)}, f32[8,2,8,512]{3,2,1,0:T(8,128)S(1)}) custom-call(s32[1]{0:T(128)} %bitcast.where_ref, f32[8,2,64,2048]{3,2,1,0:T(8,128)} %x_ref.1, f32[2,16,512]{2,1,0:T(8,128)S(1)} %copy-done.1), custom_call_target="tpu_custom_call" | custom-call | flops 1 | bytes 1 | tf_op jit(solution)/shard_map/k_thin/pallas_call | solution.py:205
  6.2 1.7 %collective-permute-start.3 = (f32[9,2,8,512]{3,2,1,0:T(8,128)S(1)}, f32[9,2,8,512]{3,2,1,0:T(8,128)S(1)}, u32[]{:S(2)}, u32[]{:S(2)}) collective-permute-start(f32[9,2,8,512]{3,2,1,0:T(8,128)S(1)} %get-tuple-element.20), channel_id=1, source_target_pairs={{0,1},{2,3},{4,5},{6,7},{8,9},{10,11},{12,13},{14,15},{16,17},{18,... | collective-permute-start | bytes 884744 | tf_op jit(solution)/shard_map/x_near/ppermute | solution.py:401
  7.9 1.0 %collective-permute-start.2 = (f32[8,2,8,512]{3,2,1,0:T(8,128)S(1)}, f32[8,2,8,512]{3,2,1,0:T(8,128)S(1)}, u32[]{:S(2)}, u32[]{:S(2)}) collective-permute-start(f32[8,2,8,512]{3,2,1,0:T(8,128)S(1)} %get-tuple-element.19.own_ref.refs_3_), channel_id=1, source_target_pairs={{0,64},{32,96},{64,0},{96,32},{1,65},{33,97},{65,1},{97,33},{2,66}... | collective-permute-start | bytes 786440 | tf_op jit(solution)/shard_map/x_ymid/ppermute | solution.py:382
  8.9 1.2 %collective-permute-start.1 = (f32[8,2,8,512]{3,2,1,0:T(8,128)S(1)}, f32[8,2,8,512]{3,2,1,0:T(8,128)S(1)}, u32[]{:S(2)}, u32[]{:S(2)}) collective-permute-start(f32[8,2,8,512]{3,2,1,0:T(8,128)S(1)} %get-tuple-element.19.own_ref.refs_3_), channel_id=1, source_target_pairs={{0,32},{32,0},{64,96},{96,64},{1,33},{33,1},{65,97},{97,65},{2,34}... | collective-permute-start | bytes 786440 | tf_op jit(solution)/shard_map/x_cmid/ppermute | solution.py:382
  10.1 4.4 %collective-permute-start = (f32[9,2,8,512]{3,2,1,0:T(8,128)S(1)}, f32[9,2,8,512]{3,2,1,0:T(8,128)S(1)}, u32[]{:S(2)}, u32[]{:S(2)}) collective-permute-start(f32[9,2,8,512]{3,2,1,0:T(8,128)S(1)} %get-tuple-element.18), channel_id=1, source_target_pairs={{1,2},{3,4},{5,6},{7,8},{9,10},{11,12},{13,14},{15,16},{17,18},{19... | collective-permute-start | bytes 884744 | tf_op jit(solution)/shard_map/x_far/ppermute | solution.py:407
  14.5 0.0 collective-permute-done.3
  14.6 1.4 %collective-permute-start.4 = (f32[8,2,8,512]{3,2,1,0:T(8,128)S(1)}, f32[8,2,8,512]{3,2,1,0:T(8,128)S(1)}, u32[]{:S(2)}, u32[]{:S(2)}) collective-permute-start(f32[8,2,8,512]{3,2,1,0:T(8,128)S(1)} %slice_add_fusion.own_ref.refs_0_), channel_id=1, source_target_pairs={{0,32},{32,0},{64,96},{96,64},{1,33},{33,1},{65,97},{97,65},{2,34}... | collective-permute-start | bytes 786440 | tf_op jit(solution)/shard_map/x_cnear/ppermute | solution.py:382
  16.0 1.0 %collective-permute-start.6 = (f32[8,2,8,512]{3,2,1,0:T(8,128)S(1)}, f32[8,2,8,512]{3,2,1,0:T(8,128)S(1)}, u32[]{:S(2)}, u32[]{:S(2)}) collective-permute-start(f32[8,2,8,512]{3,2,1,0:T(8,128)S(1)} %slice_add_fusion.own_ref.refs_0_), channel_id=1, source_target_pairs={{0,64},{32,96},{64,0},{96,32},{1,65},{33,97},{65,1},{97,33},{2,66}... | collective-permute-start | bytes 786440 | tf_op jit(solution)/shard_map/x_ynear/ppermute | solution.py:382
  16.9 0.0 copy-done.2
  17.0 0.0 collective-permute-done.2.across_ref
  17.0 1.1 %collective-permute-start.8 = (f32[8,2,8,512]{3,2,1,0:T(8,128)S(1)}, f32[8,2,8,512]{3,2,1,0:T(8,128)S(1)}, u32[]{:S(2)}, u32[]{:S(2)}) collective-permute-start(f32[8,2,8,512]{3,2,1,0:T(8,128)S(1)} %collective-permute-done.2.across_ref), channel_id=1, source_target_pairs={{0,32},{32,0},{64,96},{96,64},{1,33},{33,1},{65,97},{97,65},{2,34}... | collective-permute-start | bytes 786440 | tf_op jit(solution)/shard_map/x_dmid/ppermute | solution.py:382
  18.1 0.0 collective-permute-done.1.beside_ref
  18.1 1.2 %k_pmid.1.refs_4_ = f32[8,2,8,512]{3,2,1,0:T(8,128)S(1)} custom-call(f32[8,2,8,512]{3,2,1,0:T(8,128)S(1)} %get-tuple-element.19.own_ref.refs_3_, f32[8,2,8,512]{3,2,1,0:T(8,128)S(1)} %collective-permute-done.1.beside_ref, f32[8,2,8,512]{3,2,1,0:T(8,128)S(1)} %collective-permute-done.2.across_ref, f32[2,8,512]{2,1,0:T(8,128)S(1)} %slice.30.seen_ref), custom_call_target="tpu_custom_call" | custom-call | flops 1 | bytes 1 | tf_op jit(solution)/shard_map/k_pmid/pallas_call | solution.py:258
  19.4 3.4 %collective-permute-done = f32[9,2,8,512]{3,2,1,0:T(8,128)S(1)} collective-permute-done((f32[9,2,8,512]{3,2,1,0:T(8,128)S(1)}, f32[9,2,8,512]{3,2,1,0:T(8,128)S(1)}, u32[]{:S(2)}, u32[]{:S(2)}) %collective-permute-start) | collective-permute-done | bytes 294944 | tf_op jit(solution)/shard_map/x_far/ppermute | solution.py:407
  22.7 0.0 collective-permute-done.4.beside_ref
  22.8 2.1 %collective-permute-start.5 = (f32[8,2,8,512]{3,2,1,0:T(8,128)S(1)}, f32[8,2,8,512]{3,2,1,0:T(8,128)S(1)}, u32[]{:S(2)}, u32[]{:S(2)}) collective-permute-start(f32[8,2,8,512]{3,2,1,0:T(8,128)S(1)} %slice_add_fusion.1.own_ref.refs_1_), channel_id=1, source_target_pairs={{0,64},{32,96},{64,0},{96,32},{1,65},{33,97},{65,1},{97,33},{2,66}... | collective-permute-start | bytes 786440 | tf_op jit(solution)/shard_map/x_yfar/ppermute | solution.py:382
  24.9 7.0 %collective-permute-done.6.across_ref = f32[8,2,8,512]{3,2,1,0:T(8,128)S(1)} collective-permute-done((f32[8,2,8,512]{3,2,1,0:T(8,128)S(1)}, f32[8,2,8,512]{3,2,1,0:T(8,128)S(1)}, u32[]{:S(2)}, u32[]{:S(2)}) %collective-permute-start.6) | collective-permute-done | bytes 262176 | tf_op jit(solution)/shard_map/x_ynear/ppermute | solution.py:382
  31.9 0.9 %collective-permute-start.7 = (f32[8,2,8,512]{3,2,1,0:T(8,128)S(1)}, f32[8,2,8,512]{3,2,1,0:T(8,128)S(1)}, u32[]{:S(2)}, u32[]{:S(2)}) collective-permute-start(f32[8,2,8,512]{3,2,1,0:T(8,128)S(1)} %collective-permute-done.6.across_ref), channel_id=1, source_target_pairs={{0,32},{32,0},{64,96},{96,64},{1,33},{33,1},{65,97},{97,65},{2,34}... | collective-permute-start | bytes 786440 | tf_op jit(solution)/shard_map/x_dnear/ppermute | solution.py:382
  32.8 0.1 pad_add_fusion.1.where_ref
  32.9 0.0 collective-permute-start.9
  32.9 1.3 %k_pnear.1.refs_1_ = f32[8,2,8,512]{3,2,1,0:T(8,128)S(1)} custom-call(f32[8,2,8,512]{3,2,1,0:T(8,128)S(1)} %slice_add_fusion.own_ref.refs_0_, f32[8,2,8,512]{3,2,1,0:T(8,128)S(1)} %collective-permute-done.4.beside_ref, f32[8,2,8,512]{3,2,1,0:T(8,128)S(1)} %collective-permute-done.6.across_ref, f32[2,8,512]{2,1,0:T(8,128)S(1)} %fusion.seen_ref), custom_call_target="tpu_custom_call" | custom-call | flops 1 | bytes 1 | tf_op jit(solution)/shard_map/k_pnear/pallas_call | solution.py:258
  34.2 0.0 collective-permute-done.8.refs_5_
  34.2 0.0 collective-permute-done.7.refs_2_
  34.2 3.4 %k_near.1 = (f32[8,2,64,2048]{3,2,1,0:T(8,128)}, f32[8,2,8,512]{3,2,1,0:T(8,128)S(1)}) custom-call(s32[2]{0:T(128)S(1)} %pad_add_fusion.1.where_ref, f32[8,2,8,512]{3,2,1,0:T(8,128)S(1)} %slice_add_fusion.own_ref.refs_0_, f32[8,2,8,512]{3,2,1,0:T(8,128)S(1)} %k_pnear.1.refs_1_, f32[8,2,8,512]{3,2,1,0:T(8,128)S(1)} %collective-permute-done.7.refs_2_, ...), custom_call_target="tpu_custom_call" | custom-call | flops 1 | bytes 8000000 | tf_op jit(solution)/shard_map/k_near/pallas_call | solution.py:363
  37.6 0.0 collective-permute-done.5.across_ref
  37.6 0.6 %collective-permute-start.10 = (f32[8,2,8,512]{3,2,1,0:T(8,128)S(1)}, f32[8,2,8,512]{3,2,1,0:T(8,128)S(1)}, u32[]{:S(2)}, u32[]{:S(2)}) collective-permute-start(f32[8,2,8,512]{3,2,1,0:T(8,128)S(1)} %collective-permute-done.5.across_ref), channel_id=1, source_target_pairs={{0,32},{32,0},{64,96},{96,64},{1,33},{33,1},{65,97},{97,65},{2,34}... | collective-permute-start | bytes 786440 | tf_op jit(solution)/shard_map/x_dfar/ppermute | solution.py:382
  38.2 0.1 pad_add_fusion.where_ref
  38.2 0.0 collective-permute-done.9.beside_ref
  38.2 1.3 %k_pfar.1.refs_2_ = f32[8,2,8,512]{3,2,1,0:T(8,128)S(1)} custom-call(f32[8,2,8,512]{3,2,1,0:T(8,128)S(1)} %slice_add_fusion.1.own_ref.refs_1_, f32[8,2,8,512]{3,2,1,0:T(8,128)S(1)} %collective-permute-done.9.beside_ref, f32[8,2,8,512]{3,2,1,0:T(8,128)S(1)} %collective-permute-done.5.across_ref, f32[2,8,512]{2,1,0:T(8,128)S(1)} %add_bitcast_fusion.seen_ref), custom_call_target="tpu_custom_call" | custom-call | flops 1 | bytes 1 | tf_op jit(solution)/shard_map/k_pfar/pallas_call | solution.py:258
  39.5 0.0 collective-permute-done.10.refs_3_
  39.5 3.2 %k_far.1 = f32[8,2,64,2048]{3,2,1,0:T(8,128)} custom-call(s32[2]{0:T(128)S(1)} %pad_add_fusion.where_ref, f32[8,2,64,2048]{3,2,1,0:T(8,128)} %get-tuple-element.28.refs_0_, f32[8,2,8,512]{3,2,1,0:T(8,128)S(1)} %slice_add_fusion.1.own_ref.refs_1_, f32[8,2,8,512]{3,2,1,0:T(8,128)S(1)} %k_pfar.1.refs_2_, ...), custom_call_target="tpu_custom_call", output_to_operand_aliasing={{}: (1, {})} | custom-call | flops 1 | bytes 1 | tf_op jit(solution)/shard_map/k_far/pallas_call | solution.py:363
  (11 shorter events, 0.1 us)
Async XLA Ops:
  0.0 34.2 %copy-start = (bf16[4,256,256]{2,1,0:T(8,128)(2,1)S(1)}, bf16[4,256,256]{2,1,0:T(8,128)(2,1)}, u32[]{:S(2)}) copy-start(bf16[4,256,256]{2,1,0:T(8,128)(2,1)} %constant.25.clone.refs_7_.refs_6_) | copy-start | bytes 1572868
  0.0 0.9 %copy-start.1 = (f32[2,16,512]{2,1,0:T(8,128)S(1)}, f32[2,16,512]{2,1,0:T(8,128)}, u32[]{:S(2)}) copy-start(f32[2,16,512]{2,1,0:T(8,128)} %seen_hbm.1) | copy-start | bytes 196612
  0.9 16.0 %copy-start.2 = (f32[2,16,512]{2,1,0:T(8,128)S(1)}, f32[2,16,512]{2,1,0:T(8,128)}, u32[]{:S(2)}) copy-start(f32[2,16,512]{2,1,0:T(8,128)} %seen_hbm.1) | copy-start | bytes 196612
  0.9 33.3 %copy-start.3 = (bf16[64,96]{1,0:T(8,128)(2,1)S(1)}, bf16[64,96]{1,0:T(8,128)(2,1)}, u32[]{:S(2)}) copy-start(bf16[64,96]{1,0:T(8,128)(2,1)} %constant.24.clone.refs_6_.refs_5_) | copy-start | bytes 36868
  6.2 8.3 %collective-permute-start.3 = (f32[9,2,8,512]{3,2,1,0:T(8,128)S(1)}, f32[9,2,8,512]{3,2,1,0:T(8,128)S(1)}, u32[]{:S(2)}, u32[]{:S(2)}) collective-permute-start(f32[9,2,8,512]{3,2,1,0:T(8,128)S(1)} %get-tuple-element.20), channel_id=1, source_target_pairs={{0,1},{2,3},{4,5},{6,7},{8,9},{10,11},{12,13},{14,15},{16,17},{18,... | collective-permute-start | bytes 884744 | tf_op jit(solution)/shard_map/x_near/ppermute | solution.py:401
  7.9 9.1 %collective-permute-start.2 = (f32[8,2,8,512]{3,2,1,0:T(8,128)S(1)}, f32[8,2,8,512]{3,2,1,0:T(8,128)S(1)}, u32[]{:S(2)}, u32[]{:S(2)}) collective-permute-start(f32[8,2,8,512]{3,2,1,0:T(8,128)S(1)} %get-tuple-element.19.own_ref.refs_3_), channel_id=1, source_target_pairs={{0,64},{32,96},{64,0},{96,32},{1,65},{33,97},{65,1},{97,33},{2,66}... | collective-permute-start | bytes 786440 | tf_op jit(solution)/shard_map/x_ymid/ppermute | solution.py:382
  8.9 9.3 %collective-permute-start.1 = (f32[8,2,8,512]{3,2,1,0:T(8,128)S(1)}, f32[8,2,8,512]{3,2,1,0:T(8,128)S(1)}, u32[]{:S(2)}, u32[]{:S(2)}) collective-permute-start(f32[8,2,8,512]{3,2,1,0:T(8,128)S(1)} %get-tuple-element.19.own_ref.refs_3_), channel_id=1, source_target_pairs={{0,32},{32,0},{64,96},{96,64},{1,33},{33,1},{65,97},{97,65},{2,34}... | collective-permute-start | bytes 786440 | tf_op jit(solution)/shard_map/x_cmid/ppermute | solution.py:382
  10.1 12.6 %collective-permute-start = (f32[9,2,8,512]{3,2,1,0:T(8,128)S(1)}, f32[9,2,8,512]{3,2,1,0:T(8,128)S(1)}, u32[]{:S(2)}, u32[]{:S(2)}) collective-permute-start(f32[9,2,8,512]{3,2,1,0:T(8,128)S(1)} %get-tuple-element.18), channel_id=1, source_target_pairs={{1,2},{3,4},{5,6},{7,8},{9,10},{11,12},{13,14},{15,16},{17,18},{19... | collective-permute-start | bytes 884744 | tf_op jit(solution)/shard_map/x_far/ppermute | solution.py:407
  14.6 8.2 %collective-permute-start.4 = (f32[8,2,8,512]{3,2,1,0:T(8,128)S(1)}, f32[8,2,8,512]{3,2,1,0:T(8,128)S(1)}, u32[]{:S(2)}, u32[]{:S(2)}) collective-permute-start(f32[8,2,8,512]{3,2,1,0:T(8,128)S(1)} %slice_add_fusion.own_ref.refs_0_), channel_id=1, source_target_pairs={{0,32},{32,0},{64,96},{96,64},{1,33},{33,1},{65,97},{97,65},{2,34}... | collective-permute-start | bytes 786440 | tf_op jit(solution)/shard_map/x_cnear/ppermute | solution.py:382
  16.0 15.9 %collective-permute-start.6 = (f32[8,2,8,512]{3,2,1,0:T(8,128)S(1)}, f32[8,2,8,512]{3,2,1,0:T(8,128)S(1)}, u32[]{:S(2)}, u32[]{:S(2)}) collective-permute-start(f32[8,2,8,512]{3,2,1,0:T(8,128)S(1)} %slice_add_fusion.own_ref.refs_0_), channel_id=1, source_target_pairs={{0,64},{32,96},{64,0},{96,32},{1,65},{33,97},{65,1},{97,33},{2,66}... | collective-permute-start | bytes 786440 | tf_op jit(solution)/shard_map/x_ynear/ppermute | solution.py:382
  17.0 17.2 %collective-permute-start.8 = (f32[8,2,8,512]{3,2,1,0:T(8,128)S(1)}, f32[8,2,8,512]{3,2,1,0:T(8,128)S(1)}, u32[]{:S(2)}, u32[]{:S(2)}) collective-permute-start(f32[8,2,8,512]{3,2,1,0:T(8,128)S(1)} %collective-permute-done.2.across_ref), channel_id=1, source_target_pairs={{0,32},{32,0},{64,96},{96,64},{1,33},{33,1},{65,97},{97,65},{2,34}... | collective-permute-start | bytes 786440 | tf_op jit(solution)/shard_map/x_dmid/ppermute | solution.py:382
  22.8 14.8 %collective-permute-start.5 = (f32[8,2,8,512]{3,2,1,0:T(8,128)S(1)}, f32[8,2,8,512]{3,2,1,0:T(8,128)S(1)}, u32[]{:S(2)}, u32[]{:S(2)}) collective-permute-start(f32[8,2,8,512]{3,2,1,0:T(8,128)S(1)} %slice_add_fusion.1.own_ref.refs_1_), channel_id=1, source_target_pairs={{0,64},{32,96},{64,0},{96,32},{1,65},{33,97},{65,1},{97,33},{2,66}... | collective-permute-start | bytes 786440 | tf_op jit(solution)/shard_map/x_yfar/ppermute | solution.py:382
  31.9 2.3 %collective-permute-start.7 = (f32[8,2,8,512]{3,2,1,0:T(8,128)S(1)}, f32[8,2,8,512]{3,2,1,0:T(8,128)S(1)}, u32[]{:S(2)}, u32[]{:S(2)}) collective-permute-start(f32[8,2,8,512]{3,2,1,0:T(8,128)S(1)} %collective-permute-done.6.across_ref), channel_id=1, source_target_pairs={{0,32},{32,0},{64,96},{96,64},{1,33},{33,1},{65,97},{97,65},{2,34}... | collective-permute-start | bytes 786440 | tf_op jit(solution)/shard_map/x_dnear/ppermute | solution.py:382
  32.9 5.4 %collective-permute-start.9 = (f32[8,2,8,512]{3,2,1,0:T(8,128)S(1)}, f32[8,2,8,512]{3,2,1,0:T(8,128)S(1)}, u32[]{:S(2)}, u32[]{:S(2)}) collective-permute-start(f32[8,2,8,512]{3,2,1,0:T(8,128)S(1)} %slice_add_fusion.1.own_ref.refs_1_), channel_id=1, source_target_pairs={{0,32},{32,0},{64,96},{96,64},{1,33},{33,1},{65,97},{97,65},{2,34}... | collective-permute-start | bytes 786440 | tf_op jit(solution)/shard_map/x_cfar/ppermute | solution.py:382
  37.6 1.9 %collective-permute-start.10 = (f32[8,2,8,512]{3,2,1,0:T(8,128)S(1)}, f32[8,2,8,512]{3,2,1,0:T(8,128)S(1)}, u32[]{:S(2)}, u32[]{:S(2)}) collective-permute-start(f32[8,2,8,512]{3,2,1,0:T(8,128)S(1)} %collective-permute-done.5.across_ref), channel_id=1, source_target_pairs={{0,32},{32,0},{64,96},{96,64},{1,33},{33,1},{65,97},{97,65},{2,34}... | collective-permute-start | bytes 786440 | tf_op jit(solution)/shard_map/x_dfar/ppermute | solution.py:382

commit v7 on v6

--- a/solution.py
+++ b/solution.py
@@ -265,6 +265,83 @@
     )(own, beside, across, seen)
 
 
+def early_tile(ensemble, own_ref, beside_ref, out_ref):
+    members, variables, _, columns = own_ref.shape
+    tiles = columns // LANES
+
+    def step(i, carry):
+        v = i // tiles
+        place = pl.ds(pl.multiple_of((i % tiles) * LANES, LANES), LANES)
+        own = [own_ref[m, v, :, place] for m in range(members)]
+        total = [None] * members
+        for m in range(members):
+            for n in range(m + 1, members):
+                term = soft_sign(own[m] - own[n])
+                total[m] = term if total[m] is None else total[m] + term
+                total[n] = -term if total[n] is None else total[n] - term
+        for n in range(members):
+            value = beside_ref[n, v, :, place]
+            for m in range(members):
+                total[m] = total[m] + soft_sign(own[m] - value)
+        for m in range(members):
+            out_ref[m, v, :, place] = total[m]
+        return carry
+
+    lax.fori_loop(0, variables * tiles, step, 0)
+
+
+def mixed_kernel(ensemble, *refs):
+    pair_kernel(ensemble, *refs[:4], refs[6])
+    early_tile(ensemble, *refs[4:6], refs[7])
+
+
+def mixed_gradient(mid, near, ensemble):
+    full = pl.BlockSpec(memory_space=pltpu.VMEM)
+    return pl.pallas_call(
+        functools.partial(mixed_kernel, ensemble),
+        in_specs=[full] * 6,
+        out_specs=[full] * 2,
+        out_shape=[jax.ShapeDtypeStruct(tile[0].shape, jnp.float32) for tile in (mid, near)],
+        compiler_params=pltpu.CompilerParams(vmem_limit_bytes=VMEM),
+        cost_estimate=pl.CostEstimate(flops=1, bytes_accessed=1, transcendentals=0),
+    )(*mid, *near)
+
+
+def later_kernel(ensemble, own_ref, across_ref, part_ref, seen_ref, out_ref):
+    members, variables, _, columns = own_ref.shape
+    tiles = columns // LANES
+
+    def step(i, carry):
+        v = i // tiles
+        place = pl.ds(pl.multiple_of((i % tiles) * LANES, LANES), LANES)
+        own = [own_ref[m, v, :, place] for m in range(members)]
+        total = [part_ref[m, v, :, place] for m in range(members)]
+        for n in range(members):
+            value = across_ref[n, v, :, place]
+            for m in range(members):
+                total[m] = total[m] + soft_sign(own[m] - value)
+        seen = seen_ref[v, :, place]
+        for m in range(members):
+            out_ref[m, v, :, place] = soft_sign(own[m] - seen) * (1.0 / ensemble) - total[m] * (
+                1.0 / (ensemble * (ensemble - 1))
+            )
+        return carry
+
+    lax.fori_loop(0, variables * tiles, step, 0)
+
+
+def later_gradient(own, across, part, seen, ensemble):
+    full = pl.BlockSpec(memory_space=pltpu.VMEM)
+    return pl.pallas_call(
+        functools.partial(later_kernel, ensemble),
+        in_specs=[full] * 4,
+        out_specs=full,
+        out_shape=jax.ShapeDtypeStruct(own.shape, jnp.float32),
+        compiler_params=pltpu.CompilerParams(vmem_limit_bytes=VMEM),
+        cost_estimate=pl.CostEstimate(flops=1, bytes_accessed=1, transcendentals=0),
+    )(own, across, part, seen)
+
+
 def finish(ensemble, group, own_ref, part_ref, corner_ref):
     own = own_ref[group]
     total = jnp.zeros_like(own)
@@ -415,7 +492,9 @@
     with jax.named_scope("x_dmid"):
         corner_mid = swap(across_mid, 1)
     with jax.named_scope("k_pmid"):
-        mid_part = pair_gradient(mid, beside_mid, across_mid, observed[:, MARGIN:-MARGIN], ensemble, 1)
+        mid_set = (mid, beside_mid, across_mid, observed[:, MARGIN:-MARGIN])
+        near_set = (near_tile, beside_near)
+        mid_part, near_early = mixed_gradient(mid_set, near_set, ensemble)
     far_come, mid_part = tie((far_come, mid_part))
     far_come, beside_near = tie((far_come, beside_near))
     far_tile = far_part[:members] + far_come[:members]
@@ -427,7 +506,7 @@
     with jax.named_scope("x_dnear"):
         corner_near = swap(across_near, 1)
     with jax.named_scope("k_pnear"):
-        near_grad = pair_gradient(near_tile, beside_near, across_near, near_seen, ensemble, 1)
+        near_grad = later_gradient(near_tile, across_near, near_early, near_seen, ensemble)
     trio = (near_tile, near_grad, corner_near)
     with jax.named_scope("k_near"):
         out, mid_grad = spread(trio, (mid, mid_part, corner_mid), near, bands, fields.shape, ensemble, 8000000)

time: 42.9 us -> 42.9 us (level)
    pallas_call x0 -> x2, Pallas kernels: none -> 2.62 us  [the longest x1 1.99 us: mixed_gradient(): pl.pallas_call(functools.partial(mixed_kernel, ensemble), in_specs=[full]...]
    pallas_call x3 -> x1, Pallas kernels: 3.74 us -> 1.25 us  [pair_gradient(): pl.pallas_call(functools.partial(pair_kernel, ensemble), in_specs=[full]...]
    ppermute x1, waiting for transfers between devices: 3.35 us -> 2.6 us  [shards(): far_come = lax.ppermute(far_part, 'band', pairs_of(bands, 1))]
    ppermute x9, waiting for transfers between devices: 7.04 us -> 7.6 us  [swap(): return lax.ppermute(value, 'member', [(i, i ^ bit) for i in range(devices)])]
  transfers between devices with their start and end apart: 11 -> 11, of which waited for: 2 -> 4; matrix products, arithmetic and copies ran while one was open for 1% -> 1% of each run, Pallas kernels for 17% -> 17%
where the time goes in v7:
time: 42.9 us; the launch traced here: 42.7 us
  Pallas kernels  15.7 us (37%)
  starting transfers between devices  15.5 us (36%)
  waiting for transfers between devices  10.2 us (24%)
  local copies, waits for them, and re-layouts  0.92 us (2%)
    ppermute x9, starting transfers between devices, swap(): return lax.ppermute(value, 'member', [(i, i ^ bit) for i in range(devices)])  9.41 us
    ppermute x9, waiting for transfers between devices, swap(): return lax.ppermute(value, 'member', [(i, i ^ bit) for i in range(devices)])  7.6 us
    pallas_call x2, Pallas kernels, spread(): pl.pallas_call(functools.partial(spread_kernel, bands, ensemble, first),...  6.59 us
    pallas_call x1, Pallas kernels, thin(): pl.pallas_call(functools.partial(thin_kernel, bands), in_specs=[pl.BlockS...  5.26 us
    ppermute x1, starting transfers between devices, shards(): far_come = lax.ppermute(far_part, 'band', pairs_of(bands, 1))  4.4 us
    ppermute x1, waiting for transfers between devices, shards(): far_come = lax.ppermute(far_part, 'band', pairs_of(bands, 1))  2.6 us
    pallas_call x1, Pallas kernels, mixed_gradient(): pl.pallas_call(functools.partial(mixed_kernel, ensemble), in_specs=[full]...  1.99 us
    ppermute x1, starting transfers between devices, shards(): near_come = lax.ppermute(near_part, 'band', pairs_of(bands, 0))  1.72 us
  transfers between devices with their start and end apart: 11, of which 4 were waited for; matrix products, arithmetic and copies ran while one was open for 1% of the time, Pallas kernels for 17%

profile of v7, /device:TPU:31, one launch (start us, length us, event | category | flops | bytes accessed | tf_op | source)
XLA Modules:
  0.0 42.7 jit_solution(17072292147702136136)
XLA Ops:
  0.0 0.9 %copy-done.1 = f32[2,16,512]{2,1,0:T(8,128)S(1)} copy-done((f32[2,16,512]{2,1,0:T(8,128)S(1)}, f32[2,16,512]{2,1,0:T(8,128)}, u32[]{:S(2)}) %copy-start.1) | copy-done | bytes 65560
  0.9 5.3 %k_thin.1 = (f32[9,2,8,512]{3,2,1,0:T(8,128)S(1)}, f32[9,2,8,512]{3,2,1,0:T(8,128)S(1)}, f32[8,2,8,512]{3,2,1,0:T(8,128)S(1)}) custom-call(s32[1]{0:T(128)} %bitcast.where_ref, f32[8,2,64,2048]{3,2,1,0:T(8,128)} %x_ref.1, f32[2,16,512]{2,1,0:T(8,128)S(1)} %copy-done.1), custom_call_target="tpu_custom_call" | custom-call | flops 1 | bytes 1 | tf_op jit(solution)/shard_map/k_thin/pallas_call | solution.py:205
  6.2 1.7 %collective-permute-start.3 = (f32[9,2,8,512]{3,2,1,0:T(8,128)S(1)}, f32[9,2,8,512]{3,2,1,0:T(8,128)S(1)}, u32[]{:S(2)}, u32[]{:S(2)}) collective-permute-start(f32[9,2,8,512]{3,2,1,0:T(8,128)S(1)} %get-tuple-element.21), channel_id=1, source_target_pairs={{0,1},{2,3},{4,5},{6,7},{8,9},{10,11},{12,13},{14,15},{16,17},{18,... | collective-permute-start | bytes 884744 | tf_op jit(solution)/shard_map/x_near/ppermute | solution.py:478
  7.9 1.0 %collective-permute-start.2 = (f32[8,2,8,512]{3,2,1,0:T(8,128)S(1)}, f32[8,2,8,512]{3,2,1,0:T(8,128)S(1)}, u32[]{:S(2)}, u32[]{:S(2)}) collective-permute-start(f32[8,2,8,512]{3,2,1,0:T(8,128)S(1)} %get-tuple-element.20.refs_0_.refs_3_), channel_id=1, source_target_pairs={{0,64},{32,96},{64,0},{96,32},{1,65},{33,97},{65,1},{97,33},{2,66}... | collective-permute-start | bytes 786440 | tf_op jit(solution)/shard_map/x_ymid/ppermute | solution.py:459
  8.9 1.2 %collective-permute-start.1 = (f32[8,2,8,512]{3,2,1,0:T(8,128)S(1)}, f32[8,2,8,512]{3,2,1,0:T(8,128)S(1)}, u32[]{:S(2)}, u32[]{:S(2)}) collective-permute-start(f32[8,2,8,512]{3,2,1,0:T(8,128)S(1)} %get-tuple-element.20.refs_0_.refs_3_), channel_id=1, source_target_pairs={{0,32},{32,0},{64,96},{96,64},{1,33},{33,1},{65,97},{97,65},{2,34}... | collective-permute-start | bytes 786440 | tf_op jit(solution)/shard_map/x_cmid/ppermute | solution.py:459
  10.1 4.4 %collective-permute-start = (f32[9,2,8,512]{3,2,1,0:T(8,128)S(1)}, f32[9,2,8,512]{3,2,1,0:T(8,128)S(1)}, u32[]{:S(2)}, u32[]{:S(2)}) collective-permute-start(f32[9,2,8,512]{3,2,1,0:T(8,128)S(1)} %get-tuple-element.19), channel_id=1, source_target_pairs={{1,2},{3,4},{5,6},{7,8},{9,10},{11,12},{13,14},{15,16},{17,18},{19... | collective-permute-start | bytes 884744 | tf_op jit(solution)/shard_map/x_far/ppermute | solution.py:484
  14.5 0.0 collective-permute-done.3
  14.6 1.4 %collective-permute-start.4 = (f32[8,2,8,512]{3,2,1,0:T(8,128)S(1)}, f32[8,2,8,512]{3,2,1,0:T(8,128)S(1)}, u32[]{:S(2)}, u32[]{:S(2)}) collective-permute-start(f32[8,2,8,512]{3,2,1,0:T(8,128)S(1)} %slice_add_fusion.refs_4_.own_ref.refs_0_), channel_id=1, source_target_pairs={{0,32},{32,0},{64,96},{96,64},{1,33},{33,1},{65,97},{97,65},{2,34}... | collective-permute-start | bytes 786440 | tf_op jit(solution)/shard_map/x_cnear/ppermute | solution.py:459
  16.0 1.0 %collective-permute-start.6 = (f32[8,2,8,512]{3,2,1,0:T(8,128)S(1)}, f32[8,2,8,512]{3,2,1,0:T(8,128)S(1)}, u32[]{:S(2)}, u32[]{:S(2)}) collective-permute-start(f32[8,2,8,512]{3,2,1,0:T(8,128)S(1)} %slice_add_fusion.refs_4_.own_ref.refs_0_), channel_id=1, source_target_pairs={{0,64},{32,96},{64,0},{96,32},{1,65},{33,97},{65,1},{97,33},{2,66}... | collective-permute-start | bytes 786440 | tf_op jit(solution)/shard_map/x_ynear/ppermute | solution.py:459
  16.9 0.0 copy-done.2
  17.0 0.0 collective-permute-done.2.refs_2_
  17.0 1.1 %collective-permute-start.8 = (f32[8,2,8,512]{3,2,1,0:T(8,128)S(1)}, f32[8,2,8,512]{3,2,1,0:T(8,128)S(1)}, u32[]{:S(2)}, u32[]{:S(2)}) collective-permute-start(f32[8,2,8,512]{3,2,1,0:T(8,128)S(1)} %collective-permute-done.2.refs_2_), channel_id=1, source_target_pairs={{0,32},{32,0},{64,96},{96,64},{1,33},{33,1},{65,97},{97,65},{2,34}... | collective-permute-start | bytes 786440 | tf_op jit(solution)/shard_map/x_dmid/ppermute | solution.py:459
  18.1 0.0 collective-permute-done.1.refs_1_
  18.1 0.0 collective-permute-done.4.refs_5_
  18.1 2.0 %k_pmid.1 = (f32[8,2,8,512]{3,2,1,0:T(8,128)S(1)}, f32[8,2,8,512]{3,2,1,0:T(8,128)S(1)}) custom-call(f32[8,2,8,512]{3,2,1,0:T(8,128)S(1)} %get-tuple-element.20.refs_0_.refs_3_, f32[8,2,8,512]{3,2,1,0:T(8,128)S(1)} %collective-permute-done.1.refs_1_, f32[8,2,8,512]{3,2,1,0:T(8,128)S(1)} %collective-permute-done.2.refs_2_, f32[2,8,512]{2,1,0:T(8,128)S(1)} %slice.30.refs_3_, ...), custom_call_target="tpu_custom_call" | custom-call | flops 1 | bytes 1 | tf_op jit(solution)/shard_map/k_pmid/pallas_call | solution.py:300
  20.1 2.6 %collective-permute-done = f32[9,2,8,512]{3,2,1,0:T(8,128)S(1)} collective-permute-done((f32[9,2,8,512]{3,2,1,0:T(8,128)S(1)}, f32[9,2,8,512]{3,2,1,0:T(8,128)S(1)}, u32[]{:S(2)}, u32[]{:S(2)}) %collective-permute-start) | collective-permute-done | bytes 294944 | tf_op jit(solution)/shard_map/x_far/ppermute | solution.py:484
  22.8 2.1 %collective-permute-start.5 = (f32[8,2,8,512]{3,2,1,0:T(8,128)S(1)}, f32[8,2,8,512]{3,2,1,0:T(8,128)S(1)}, u32[]{:S(2)}, u32[]{:S(2)}) collective-permute-start(f32[8,2,8,512]{3,2,1,0:T(8,128)S(1)} %slice_add_fusion.1.own_ref.refs_1_), channel_id=1, source_target_pairs={{0,64},{32,96},{64,0},{96,32},{1,65},{33,97},{65,1},{97,33},{2,66}... | collective-permute-start | bytes 786440 | tf_op jit(solution)/shard_map/x_yfar/ppermute | solution.py:459
  24.9 7.0 %collective-permute-done.6.across_ref = f32[8,2,8,512]{3,2,1,0:T(8,128)S(1)} collective-permute-done((f32[8,2,8,512]{3,2,1,0:T(8,128)S(1)}, f32[8,2,8,512]{3,2,1,0:T(8,128)S(1)}, u32[]{:S(2)}, u32[]{:S(2)}) %collective-permute-start.6) | collective-permute-done | bytes 262176 | tf_op jit(solution)/shard_map/x_ynear/ppermute | solution.py:459
  31.9 0.9 %collective-permute-start.7 = (f32[8,2,8,512]{3,2,1,0:T(8,128)S(1)}, f32[8,2,8,512]{3,2,1,0:T(8,128)S(1)}, u32[]{:S(2)}, u32[]{:S(2)}) collective-permute-start(f32[8,2,8,512]{3,2,1,0:T(8,128)S(1)} %collective-permute-done.6.across_ref), channel_id=1, source_target_pairs={{0,32},{32,0},{64,96},{96,64},{1,33},{33,1},{65,97},{97,65},{2,34}... | collective-permute-start | bytes 786440 | tf_op jit(solution)/shard_map/x_dnear/ppermute | solution.py:459
  32.8 0.1 pad_add_fusion.1.where_ref
  32.9 0.0 collective-permute-start.9
  32.9 0.6 %k_pnear.1.refs_1_ = f32[8,2,8,512]{3,2,1,0:T(8,128)S(1)} custom-call(f32[8,2,8,512]{3,2,1,0:T(8,128)S(1)} %slice_add_fusion.refs_4_.own_ref.refs_0_, f32[8,2,8,512]{3,2,1,0:T(8,128)S(1)} %collective-permute-done.6.across_ref, f32[8,2,8,512]{3,2,1,0:T(8,128)S(1)} %get-tuple-element.27.part_ref, f32[2,8,512]{2,1,0:T(8,128)S(1)} %fusion.seen_ref), custom_call_target="tpu_custom_call" | custom-call | flops 1 | bytes 1 | tf_op jit(solution)/shard_map/k_pnear/pallas_call | solution.py:335
  33.5 0.0 collective-permute-done.8.refs_5_
  33.6 0.4 collective-permute-done.7.refs_2_
  34.0 3.4 %k_near.1 = (f32[8,2,64,2048]{3,2,1,0:T(8,128)}, f32[8,2,8,512]{3,2,1,0:T(8,128)S(1)}) custom-call(s32[2]{0:T(128)S(1)} %pad_add_fusion.1.where_ref, f32[8,2,8,512]{3,2,1,0:T(8,128)S(1)} %slice_add_fusion.refs_4_.own_ref.refs_0_, f32[8,2,8,512]{3,2,1,0:T(8,128)S(1)} %k_pnear.1.refs_1_, f32[8,2,8,512]{3,2,1,0:T(8,128)S(1)} %collective-permute-done.7.refs_2_, ...), custom_call_target="tpu_custom_call" | custom-call | flops 1 | bytes 8000000 | tf_op jit(solution)/shard_map/k_near/pallas_call | solution.py:440
  37.3 0.2 collective-permute-done.5.across_ref
  37.5 0.7 %collective-permute-start.10 = (f32[8,2,8,512]{3,2,1,0:T(8,128)S(1)}, f32[8,2,8,512]{3,2,1,0:T(8,128)S(1)}, u32[]{:S(2)}, u32[]{:S(2)}) collective-permute-start(f32[8,2,8,512]{3,2,1,0:T(8,128)S(1)} %collective-permute-done.5.across_ref), channel_id=1, source_target_pairs={{0,32},{32,0},{64,96},{96,64},{1,33},{33,1},{65,97},{97,65},{2,34}... | collective-permute-start | bytes 786440 | tf_op jit(solution)/shard_map/x_dfar/ppermute | solution.py:459
  38.2 0.1 pad_add_fusion.where_ref
  38.2 0.0 collective-permute-done.9.beside_ref
  38.2 1.3 %k_pfar.1.refs_2_ = f32[8,2,8,512]{3,2,1,0:T(8,128)S(1)} custom-call(f32[8,2,8,512]{3,2,1,0:T(8,128)S(1)} %slice_add_fusion.1.own_ref.refs_1_, f32[8,2,8,512]{3,2,1,0:T(8,128)S(1)} %collective-permute-done.9.beside_ref, f32[8,2,8,512]{3,2,1,0:T(8,128)S(1)} %collective-permute-done.5.across_ref, f32[2,8,512]{2,1,0:T(8,128)S(1)} %add_bitcast_fusion.seen_ref), custom_call_target="tpu_custom_call" | custom-call | flops 1 | bytes 1 | tf_op jit(solution)/shard_map/k_pfar/pallas_call | solution.py:258
  39.5 0.0 collective-permute-done.10.refs_3_
  39.5 3.2 %k_far.1 = f32[8,2,64,2048]{3,2,1,0:T(8,128)} custom-call(s32[2]{0:T(128)S(1)} %pad_add_fusion.where_ref, f32[8,2,64,2048]{3,2,1,0:T(8,128)} %get-tuple-element.30.refs_0_, f32[8,2,8,512]{3,2,1,0:T(8,128)S(1)} %slice_add_fusion.1.own_ref.refs_1_, f32[8,2,8,512]{3,2,1,0:T(8,128)S(1)} %k_pfar.1.refs_2_, ...), custom_call_target="tpu_custom_call", output_to_operand_aliasing={{}: (1, {})} | custom-call | flops 1 | bytes 1 | tf_op jit(solution)/shard_map/k_far/pallas_call | solution.py:440
  (11 shorter events, 0.1 us)
Async XLA Ops:
  0.0 34.0 %copy-start = (bf16[4,256,256]{2,1,0:T(8,128)(2,1)S(1)}, bf16[4,256,256]{2,1,0:T(8,128)(2,1)}, u32[]{:S(2)}) copy-start(bf16[4,256,256]{2,1,0:T(8,128)(2,1)} %constant.25.clone.refs_7_.refs_6_) | copy-start | bytes 1572868
  0.0 0.9 %copy-start.1 = (f32[2,16,512]{2,1,0:T(8,128)S(1)}, f32[2,16,512]{2,1,0:T(8,128)}, u32[]{:S(2)}) copy-start(f32[2,16,512]{2,1,0:T(8,128)} %seen_hbm.1) | copy-start | bytes 196612
  0.9 16.0 %copy-start.2 = (f32[2,16,512]{2,1,0:T(8,128)S(1)}, f32[2,16,512]{2,1,0:T(8,128)}, u32[]{:S(2)}) copy-start(f32[2,16,512]{2,1,0:T(8,128)} %seen_hbm.1) | copy-start | bytes 196612
  0.9 33.1 %copy-start.3 = (bf16[64,96]{1,0:T(8,128)(2,1)S(1)}, bf16[64,96]{1,0:T(8,128)(2,1)}, u32[]{:S(2)}) copy-start(bf16[64,96]{1,0:T(8,128)(2,1)} %constant.24.clone.refs_6_.refs_5_) | copy-start | bytes 36868
  6.2 8.3 %collective-permute-start.3 = (f32[9,2,8,512]{3,2,1,0:T(8,128)S(1)}, f32[9,2,8,512]{3,2,1,0:T(8,128)S(1)}, u32[]{:S(2)}, u32[]{:S(2)}) collective-permute-start(f32[9,2,8,512]{3,2,1,0:T(8,128)S(1)} %get-tuple-element.21), channel_id=1, source_target_pairs={{0,1},{2,3},{4,5},{6,7},{8,9},{10,11},{12,13},{14,15},{16,17},{18,... | collective-permute-start | bytes 884744 | tf_op jit(solution)/shard_map/x_near/ppermute | solution.py:478
  7.9 9.1 %collective-permute-start.2 = (f32[8,2,8,512]{3,2,1,0:T(8,128)S(1)}, f32[8,2,8,512]{3,2,1,0:T(8,128)S(1)}, u32[]{:S(2)}, u32[]{:S(2)}) collective-permute-start(f32[8,2,8,512]{3,2,1,0:T(8,128)S(1)} %get-tuple-element.20.refs_0_.refs_3_), channel_id=1, source_target_pairs={{0,64},{32,96},{64,0},{96,32},{1,65},{33,97},{65,1},{97,33},{2,66}... | collective-permute-start | bytes 786440 | tf_op jit(solution)/shard_map/x_ymid/ppermute | solution.py:459
  8.9 9.3 %collective-permute-start.1 = (f32[8,2,8,512]{3,2,1,0:T(8,128)S(1)}, f32[8,2,8,512]{3,2,1,0:T(8,128)S(1)}, u32[]{:S(2)}, u32[]{:S(2)}) collective-permute-start(f32[8,2,8,512]{3,2,1,0:T(8,128)S(1)} %get-tuple-element.20.refs_0_.refs_3_), channel_id=1, source_target_pairs={{0,32},{32,0},{64,96},{96,64},{1,33},{33,1},{65,97},{97,65},{2,34}... | collective-permute-start | bytes 786440 | tf_op jit(solution)/shard_map/x_cmid/ppermute | solution.py:459
  10.1 12.6 %collective-permute-start = (f32[9,2,8,512]{3,2,1,0:T(8,128)S(1)}, f32[9,2,8,512]{3,2,1,0:T(8,128)S(1)}, u32[]{:S(2)}, u32[]{:S(2)}) collective-permute-start(f32[9,2,8,512]{3,2,1,0:T(8,128)S(1)} %get-tuple-element.19), channel_id=1, source_target_pairs={{1,2},{3,4},{5,6},{7,8},{9,10},{11,12},{13,14},{15,16},{17,18},{19... | collective-permute-start | bytes 884744 | tf_op jit(solution)/shard_map/x_far/ppermute | solution.py:484
  14.6 3.6 %collective-permute-start.4 = (f32[8,2,8,512]{3,2,1,0:T(8,128)S(1)}, f32[8,2,8,512]{3,2,1,0:T(8,128)S(1)}, u32[]{:S(2)}, u32[]{:S(2)}) collective-permute-start(f32[8,2,8,512]{3,2,1,0:T(8,128)S(1)} %slice_add_fusion.refs_4_.own_ref.refs_0_), channel_id=1, source_target_pairs={{0,32},{32,0},{64,96},{96,64},{1,33},{33,1},{65,97},{97,65},{2,34}... | collective-permute-start | bytes 786440 | tf_op jit(solution)/shard_map/x_cnear/ppermute | solution.py:459
  16.0 15.9 %collective-permute-start.6 = (f32[8,2,8,512]{3,2,1,0:T(8,128)S(1)}, f32[8,2,8,512]{3,2,1,0:T(8,128)S(1)}, u32[]{:S(2)}, u32[]{:S(2)}) collective-permute-start(f32[8,2,8,512]{3,2,1,0:T(8,128)S(1)} %slice_add_fusion.refs_4_.own_ref.refs_0_), channel_id=1, source_target_pairs={{0,64},{32,96},{64,0},{96,32},{1,65},{33,97},{65,1},{97,33},{2,66}... | collective-permute-start | bytes 786440 | tf_op jit(solution)/shard_map/x_ynear/ppermute | solution.py:459
  17.0 16.6 %collective-permute-start.8 = (f32[8,2,8,512]{3,2,1,0:T(8,128)S(1)}, f32[8,2,8,512]{3,2,1,0:T(8,128)S(1)}, u32[]{:S(2)}, u32[]{:S(2)}) collective-permute-start(f32[8,2,8,512]{3,2,1,0:T(8,128)S(1)} %collective-permute-done.2.refs_2_), channel_id=1, source_target_pairs={{0,32},{32,0},{64,96},{96,64},{1,33},{33,1},{65,97},{97,65},{2,34}... | collective-permute-start | bytes 786440 | tf_op jit(solution)/shard_map/x_dmid/ppermute | solution.py:459
  22.8 14.7 %collective-permute-start.5 = (f32[8,2,8,512]{3,2,1,0:T(8,128)S(1)}, f32[8,2,8,512]{3,2,1,0:T(8,128)S(1)}, u32[]{:S(2)}, u32[]{:S(2)}) collective-permute-start(f32[8,2,8,512]{3,2,1,0:T(8,128)S(1)} %slice_add_fusion.1.own_ref.refs_1_), channel_id=1, source_target_pairs={{0,64},{32,96},{64,0},{96,32},{1,65},{33,97},{65,1},{97,33},{2,66}... | collective-permute-start | bytes 786440 | tf_op jit(solution)/shard_map/x_yfar/ppermute | solution.py:459
  31.9 2.1 %collective-permute-start.7 = (f32[8,2,8,512]{3,2,1,0:T(8,128)S(1)}, f32[8,2,8,512]{3,2,1,0:T(8,128)S(1)}, u32[]{:S(2)}, u32[]{:S(2)}) collective-permute-start(f32[8,2,8,512]{3,2,1,0:T(8,128)S(1)} %collective-permute-done.6.across_ref), channel_id=1, source_target_pairs={{0,32},{32,0},{64,96},{96,64},{1,33},{33,1},{65,97},{97,65},{2,34}... | collective-permute-start | bytes 786440 | tf_op jit(solution)/shard_map/x_dnear/ppermute | solution.py:459
  32.9 5.4 %collective-permute-start.9 = (f32[8,2,8,512]{3,2,1,0:T(8,128)S(1)}, f32[8,2,8,512]{3,2,1,0:T(8,128)S(1)}, u32[]{:S(2)}, u32[]{:S(2)}) collective-permute-start(f32[8,2,8,512]{3,2,1,0:T(8,128)S(1)} %slice_add_fusion.1.own_ref.refs_1_), channel_id=1, source_target_pairs={{0,32},{32,0},{64,96},{96,64},{1,33},{33,1},{65,97},{97,65},{2,34}... | collective-permute-start | bytes 786440 | tf_op jit(solution)/shard_map/x_cfar/ppermute | solution.py:459
  37.5 2.0 %collective-permute-start.10 = (f32[8,2,8,512]{3,2,1,0:T(8,128)S(1)}, f32[8,2,8,512]{3,2,1,0:T(8,128)S(1)}, u32[]{:S(2)}, u32[]{:S(2)}) collective-permute-start(f32[8,2,8,512]{3,2,1,0:T(8,128)S(1)} %collective-permute-done.5.across_ref), channel_id=1, source_target_pairs={{0,32},{32,0},{64,96},{96,64},{1,33},{33,1},{65,97},{97,65},{2,34}... | collective-permute-start | bytes 786440 | tf_op jit(solution)/shard_map/x_dfar/ppermute | solution.py:459
